TPU v7x, 32 devices: a whole 2x2x4 slice. The times are simulated.
32 devices in a mesh: seq: 16 (over z, y, core), stream: 2 (over x).
Axes of the slice: x: 2, y: 2, z: 4, core: 2. Of those that a mesh axis runs over, the one named last changes fastest.
Arguments:
- tokens: bfloat16 [2, 8192, 768], P('stream', 'seq'), may hold values from -6 to 6
- lengths: int32 [16, 4], P('seq'), may hold values from 0 to 512, as said below
- cotangent: bfloat16 [2, 8192, 768], P('stream', 'seq'), may hold values from -6 to 6
- attn_gain: bfloat16 [768], P(('seq', 'stream')), may hold values from 0.099609375 to 1.8984375
- qkv_weight: bfloat16 [768, 2304], P(('seq', 'stream')), may hold values from -0.21875 to 0.21875
- out_weight: bfloat16 [768, 768], P(('seq', 'stream')), may hold values from -0.875 to 0.875
- mlp_gain: bfloat16 [768], P(('seq', 'stream')), may hold values from 0.099609375 to 1.8984375
- up_weight: bfloat16 [768, 3072], P(('seq', 'stream')), may hold values from -0.21875 to 0.21875
- up_bias: bfloat16 [3072], P(('seq', 'stream')), may hold values from -3 to 3
- down_weight: bfloat16 [3072, 768], P(('seq', 'stream')), may hold values from -0.109375 to 0.109375
- down_bias: bfloat16 [768], P(('seq', 'stream')), may hold values from -2 to 2
Outputs:
- layer_out: bfloat16 [2, 8192, 768], P('stream', 'seq')
- grad_tokens: float32 [2, 8192, 768], P('stream', 'seq')
- grad_attn_gain: float32 [768], P(('seq', 'stream'))
- grad_qkv_weight: float32 [768, 2304], P(('seq', 'stream'))
- grad_out_weight: float32 [768, 768], P(('seq', 'stream'))
- grad_mlp_gain: float32 [768], P(('seq', 'stream'))
- grad_up_weight: float32 [768, 3072], P(('seq', 'stream'))
- grad_up_bias: float32 [3072], P(('seq', 'stream'))
- grad_down_weight: float32 [3072, 768], P(('seq', 'stream'))
- grad_down_bias: float32 [768], P(('seq', 'stream'))
Inputs may be any that keep to these rules, and one draw needn't show every extreme that they name: `lengths`: each row sums to 512; a 0 is an empty slot; some row holds a single sequence of 512 tokens.
All inputs are finite; a program needn't handle non-finite values.
Results may differ from a plain program's by a relative error of at most 0.014.
Values may be sent and summed in bfloat16 or wider, within the bound.
No kernel may reach another device: no remote copies, remote signals or barrier semaphores. Data moves between devices by JAX's collectives and lax.ppermute only.
A program may use at most 192 MiB of HBM per device.

v0:
```python
from functools import partial
import math

import jax
import jax.numpy as jnp
import numpy as np
from jax import lax
from jax.experimental import pallas as pl
from jax.experimental.pallas import tpu as pltpu
from jax.sharding import PartitionSpec as P

HEADS = 12
HEAD_DIM = 64
BLOCK = 16


EPSILON = 1e-05
NEG_FILL = -1e30


ALL = ("seq", "stream")
STREAM_BIT, CORE_BIT, NEAR_BIT = 1, 2, 4


def device_count():
    return lax.axis_size("seq") * lax.axis_size("stream")


def far_groups():
    bits = []
    bit = 2 * NEAR_BIT
    while bit < device_count():
        bits.append(bit)
        bit *= 2
    groups = []
    while bits:
        taken, bits = bits[:2], bits[2:]
        groups.append(taken if len(taken) == 1 else [taken[0], taken[1], taken[0] + taken[1]])
    return groups


def flip(block, mask):
    return lax.ppermute(block, ALL, [(i, i ^ mask) for i in range(device_count())])


def place(pieces, keys, me):
    total = sum(len(key) for key in keys[0])
    rows = pieces[0][0].shape[1]
    widths = [strip[0].shape[2] for strip in pieces]
    shape = (total, rows, sum(widths))
    flat = [p for strip in pieces for p in strip]

    def body(me_ref, *refs):
        out, sem = refs[-2], refs[-1]
        taken, column = 0, 0
        for key_set, width in zip(keys, widths):
            for key in key_set:
                piece = refs[taken]
                taken += 1
                for j, rel in enumerate(key):
                    to = out.at[me_ref[0] ^ rel]
                    if len(widths) > 1:
                        to = to.at[:, pl.ds(column, width)]
                    pltpu.make_async_copy(piece.at[j], to, sem).start()
            column += width
        pltpu.make_async_copy(out, out, sem).wait()

    return pl.pallas_call(
        body,
        out_shape=like(shape, flat[0].dtype),
        in_specs=[SMEM_SPEC] + [pl.BlockSpec(memory_space=pl.ANY)] * len(flat),
        out_specs=VMEM_SPEC,
        scratch_shapes=[pltpu.SemaphoreType.DMA],
        compiler_params=pltpu.CompilerParams(
            vmem_limit_bytes=2 * math.prod(shape) * (16 // min(16, rows)) * 2 + 2**20
        ),
        cost_estimate=SHORT,
    )(me, *flat)


def after(block, *others):
    return lax.optimization_barrier((block,) + others)[0]


def far_gather(shard, key):
    piece = shard[None]
    for group in far_groups():
        got = [piece] + [flip(piece, mask) for mask in group]
        key = [k ^ mask for mask in [0] + group for k in key]
        piece = jnp.concatenate(got, axis=0)
    return piece, key


def near_gather(piece, key, bit):
    return jnp.concatenate([piece, flip(piece, bit)], axis=0), key + [k ^ bit for k in key]


def last_gather(piece, key, bit, *others):
    got = flip(piece, bit)
    if others:
        got = after(got, *others)
    pieces, keys = [piece, got], [key, [k ^ bit for k in key]]
    pieces = pieces + [flip(after(p, got), CORE_BIT) for p in pieces]
    return pieces, keys + [[k ^ CORE_BIT for k in key] for key in keys]


def relative(whole, me):
    pairs = device_count() // 2
    rows = whole.reshape((pairs, 2, -1) + whole.shape[1:]) if whole.ndim < 3 else whole
    rows = rows.reshape((pairs, -1) + whole.shape[-1:])
    bits = pairs.bit_length() - 1
    rows = rows.reshape((2,) * bits + rows.shape[1:])
    for axis in range(bits):
        mine = (me[0] >> (bits - axis)) % 2
        rows = jnp.where(mine == 1, jnp.flip(rows, axis), rows)
    order = (bits - 1, bits - 2) + tuple(range(bits - 2)) + (bits, bits + 1)
    rows = rows.transpose(order).reshape((2, 2, pairs // 4) + rows.shape[-2:])
    return rows[0], rows[1]


def combine_body(bits, counts, stream_ref, *refs):
    total = sum(sum(groups) for groups in counts)
    ins, outs = refs[:total], refs[total:]
    stream = stream_ref[0]
    for bit, groups in zip(bits, counts):
        (send, keep), outs = outs[:2], outs[2:]
        column = 0
        for count in groups:
            terms, ins = ins[:count], ins[count:]
            columns = slice(column, column + terms[0].shape[-1])
            column = columns.stop

            def part(own):
                if bit == STREAM_BIT:
                    where = (slice(None), slice(None), pl.ds(stream if own else 1 - stream, 1))
                else:
                    where = (slice(0, 1) if own else slice(1, 2),)
                out = terms[0][where].astype(F32)
                for t in terms[1:]:
                    out = out + t[where].astype(F32)
                return out

            send[..., columns] = part(False).astype(send.dtype)
            keep[..., columns] = part(True)


def combine(stream, jobs):
    far_count = jobs[0][0][0][0].shape[1]
    operands, in_specs, out_shape, out_specs = [], [], [], []

    def spec(shape):
        return pl.BlockSpec((shape[0], 1) + shape[2:], lambda j: (0, j, 0, 0, 0))

    for groups, bit in jobs:
        out = list(groups[0][0].shape)
        out[4] = sum(terms[0].shape[4] for terms in groups)
        out[2 if bit == STREAM_BIT else 0] = 1
        out = tuple(out)
        for terms in groups:
            operands += terms
            in_specs += [spec(terms[0].shape)] * len(terms)
        out_shape += [like(out, BF16), like(out, F32)]
        out_specs += [spec(out)] * 2
    outs = pl.pallas_call(
        partial(
            combine_body,
            [bit for _, bit in jobs],
            [[len(terms) for terms in groups] for groups, _ in jobs],
        ),
        grid=(far_count,),
        out_shape=out_shape,
        in_specs=[SMEM_SPEC] + in_specs,
        out_specs=out_specs,
        compiler_params=pltpu.CompilerParams(vmem_limit_bytes=20 * 2**20),
        cost_estimate=SHORT,
    )(stream, *operands)
    return [(outs[2 * i], outs[2 * i + 1]) for i in range(len(jobs))]


class Sum:
    def __init__(self, me, *strips):
        self.me, self.stream = me, me % 2
        self.groups, self.got = [], []
        for parts in strips:
            self.add(parts)

    def add(self, parts):
        if len(parts) == 1:
            parts = relative(parts[0], self.me)
        keep, send = parts
        _, self.far_count, pair_rows, columns = keep.shape
        shape = (2, self.far_count, 2, pair_rows // 2, columns)
        self.got = flip(send, CORE_BIT)
        self.groups.append([keep.reshape(shape), self.got.reshape(shape)])

    def flip(self, bit):
        self.got = flip(self.send, bit)
        self.groups[0].append(self.got)
        return self

    def hold(self, *others):
        self.groups[0][-1] = after(self.groups[0][-1], *others)

    def total(self):
        out = self.groups[0][0].astype(F32)
        for t in self.groups[0][1:]:
            out = out + t.astype(F32)
        return out


def pack_body(far_count, counts, *refs):
    ins, (keep, *sends) = refs[: sum(counts)], refs[sum(counts) :]
    _, rows, _ = keep.shape
    part = far_count // (1 + len(sends))
    column = 0
    for count in counts:
        terms, ins = ins[:count], ins[count:]
        wide, columns = terms[0].shape[-2:]
        for z in range(far_count):
            total = terms[0][0, z, 0].astype(F32)
            for t in terms[1:]:
                total = total + t[0, z, 0].astype(F32)
            out = keep if z < part else sends[z // part - 1]
            for fold in range(wide // rows):
                at = slice(column + fold * columns, column + (fold + 1) * columns)
                value = total[fold * rows : (fold + 1) * rows]
                out[z % part, :, at] = value.astype(out.dtype)
        column += wide // rows * columns


class Far:
    def __init__(self, sums, cost=None):
        groups = [s.groups[0] for s in sums]
        far_count, _, rows, _ = groups[0][0].shape[1:]
        shards = [g[0].shape[3:] for g in groups]
        columns = sum(r // rows * c for r, c in shards)
        self.order = list(reversed(far_groups()))
        part = far_count // (1 + len(self.order[0]))
        shape = (part, rows, columns)
        outs = pl.pallas_call(
            partial(pack_body, far_count, [len(g) for g in groups]),
            out_shape=[like(shape, F32)] + [like(shape, BF16)] * len(self.order[0]),
            in_specs=[VMEM_SPEC] * sum(len(g) for g in groups),
            out_specs=[VMEM_SPEC] * (1 + len(self.order[0])),
            compiler_params=pltpu.CompilerParams(vmem_limit_bytes=16 * 2**20),
            cost_estimate=cost or SHORT,
        )(*[t for g in groups for t in g])
        self.keep, self.sends = outs[0], outs[1:]

    def flip(self):
        self.got = [flip(s, mask) for s, mask in zip(self.sends, self.order[0])]
        return self

    def result(self):
        total = self.keep
        for block in self.got:
            total = total + block.astype(F32)
        for group in self.order[1:]:
            part = total.shape[0] // (len(group) + 1)
            got = [
                flip(total[(i + 1) * part : (i + 2) * part].astype(BF16), mask)
                for i, mask in enumerate(group)
            ]
            total = total[:part]
            for block in got:
                total = total + block.astype(F32)
        return total[0]


def split(*jobs):
    outs = combine(jobs[0][0].stream, [(s.groups, bit) for s, bit in jobs])
    for (s, _), (send, keep) in zip(jobs, outs):
        s.send, s.groups = send, [[keep]]


F32, BF16 = jnp.float32, jnp.bfloat16
SHORT = pl.CostEstimate(flops=1, bytes_accessed=1, transcendentals=0)
LONG = pl.CostEstimate(flops=10**10, bytes_accessed=3 * 10**7, transcendentals=0)
SMEM_SPEC = pl.BlockSpec(memory_space=pltpu.SMEM)
VMEM_SPEC = pl.BlockSpec(memory_space=pltpu.VMEM)


def like(shape, kind):
    return jax.ShapeDtypeStruct(shape, kind)


def in_hbm(*arrays):
    return [pltpu.with_memory_space_constraint(a, pltpu.HBM) for a in arrays]


def doc_layout(pack_lengths, row_count):
    ends = [pack_lengths[0]]
    for i in range(1, pack_lengths.shape[0]):
        ends.append(ends[-1] + pack_lengths[i])
    seq_ends = jnp.stack(ends)
    row_index = jnp.arange(row_count, dtype=jnp.int32)
    passed = seq_ends[None, :] <= row_index[:, None]
    doc_ids = jnp.sum(passed.astype(jnp.int32), axis=1)
    starts = jnp.max(jnp.where(passed, seq_ends[None, :], 0), axis=1)
    return (doc_ids, row_index - starts)


def rotary_tables(positions, head_size):
    half_size = head_size // 2
    frequency = jnp.exp(
        jnp.arange(half_size, dtype=jnp.float32) * (-2.0 * math.log(10000.0) / head_size)
    )
    angles = positions.astype(jnp.float32)[:, None] * frequency[None, :]
    return (jnp.cos(angles), jnp.sin(angles))


PAIR = 2 * HEAD_DIM
TILE = 128
SMALL = 128
REACH = 16
LOG2_E = math.log2(math.e)
SCORE_SCALE = HEAD_DIM ** (-0.5)
GELU_A = math.sqrt(2.0 / math.pi)
GELU_B = 0.044715


def dot(a, b):
    return lax.dot_general(a, b, (((1,), (0,)), ((), ())), preferred_element_type=F32)


def dot_nt(a, b):
    return lax.dot_general(a, b, (((1,), (1,)), ((), ())), preferred_element_type=F32)


def dot_tn(a, b):
    return lax.dot_general(a, b, (((0,), (0,)), ((), ())), preferred_element_type=F32)


def whole_spec(shape):
    return pl.BlockSpec(shape, lambda *_: (0,) * len(shape))


def normed(values):
    center = values - jnp.mean(values, axis=-1, keepdims=True)
    inverse = lax.rsqrt(jnp.mean(center * center, axis=-1, keepdims=True) + EPSILON)
    return center * inverse, inverse


def norm_term(grad_out, norm, inverse, gain):
    grad_norm = grad_out * gain
    return inverse * (
        grad_norm
        - jnp.mean(grad_norm, axis=-1, keepdims=True)
        - norm * jnp.mean(grad_norm * norm, axis=-1, keepdims=True)
    )


def half_swap(block):
    lane = lax.broadcasted_iota(jnp.int32, block.shape, 1)
    quarter = HEAD_DIM // 2
    return jnp.where(
        (lane & quarter) == 0,
        pltpu.roll(block, PAIR - quarter, 1),
        pltpu.roll(block, quarter, 1),
    )


def small_row(extra, column):
    lane = lax.broadcasted_iota(jnp.int32, (8, extra.shape[1]), 1)
    return dot_nt((lane == column).astype(BF16), extra[...])[0:1, :]


def front_body(
    noisy_ref, tok, far_tok, extra, weight, cos, sin,
    first_t, far_first_t, q, k, v, kf, vf, first, far_first,
):
    width = tok.shape[1]
    g = small_row(extra, 0)
    norm, _ = normed(tok[...].astype(F32))
    first[...] = (norm * g).astype(BF16)
    is_noisy = noisy_ref[0] == 1

    @pl.when(is_noisy)
    def _():
        far_norm, _ = normed(far_tok[...].astype(F32))
        far_first[...] = (far_norm * g).astype(BF16)

    @pl.when(jnp.logical_not(is_noisy))
    def _():
        far_first[...] = first[...]

    first_t[...] = first[...].T
    far_first_t[...] = far_first[...].T
    step = 2 * PAIR
    for rows, outs in ((first, (q, k, v)), (far_first, (None, kf, vf))):
        for part, out in enumerate(outs):
            if out is None:
                continue
            for start in range(0, width, step):
                prod = dot(rows[...], weight[:, part * width + start : part * width + start + step])
                for sub in range(0, step, PAIR):
                    x = prod[:, sub : sub + PAIR]
                    if part < 2:
                        x = x * cos[...] + half_swap(x) * sin[...]
                    out[:, start + sub : start + sub + PAIR] = x.astype(BF16)


def joint_specs(width):
    return (
        pl.BlockSpec((width, SMALL), lambda *_: (0, 4 * width // SMALL)),
        pl.BlockSpec((width, 3 * width), lambda *_: (0, 0)),
        pl.BlockSpec((width, width), lambda *_: (0, 3)),
    )


def front(noisy, tok, far_tok, joint, cos, sin):
    rows, width = tok.shape
    act, table = whole_spec((rows, width)), whole_spec((rows, PAIR))
    extra, qkv, _ = joint_specs(width)
    return pl.pallas_call(
        front_body,
        grid=(1,),
        out_shape=[like((width, rows), BF16)] * 2 + [like((rows, width), BF16)] * 5,
        in_specs=[SMEM_SPEC, act, act, extra, qkv, table, table],
        out_specs=[whole_spec((width, rows))] * 2 + [act] * 5,
        scratch_shapes=[pltpu.VMEM((rows, width), BF16)] * 2,
        compiler_params=pltpu.CompilerParams(vmem_limit_bytes=20 * 2**20),
        cost_estimate=SHORT,
    )(noisy, tok, far_tok, joint, joint, cos, sin)


def window(i, rows):
    size = TILE + 2 * REACH
    return min(max(i * TILE - REACH, 0), rows - size), size


def far_width(i, rows, noisy):
    return min(rows, (i + 1) * TILE + (0 if noisy else TILE))


def build_masks(lo, hi, code, code_row, far_bias, near_bias):
    rows = far_bias.shape[0]
    for i in range(rows // TILE):
        r = slice(i * TILE, (i + 1) * TILE)
        keys = code_row[...]
        far_bias[r, :] = jnp.where((keys >= lo[r, :]) & (keys <= hi[r, :]), 0.0, NEG_FILL)
        start, size = window(i, rows)
        near_bias[i] = jnp.where(code_row[:, start : start + size] == code[r, :], 0.0, NEG_FILL)


def build_turned_masks(code, lo_row, hi_row, code_row, far_bias, near_bias):
    rows = far_bias.shape[0]
    for i in range(rows // TILE):
        r = slice(i * TILE, (i + 1) * TILE)
        keys = code[r, :]
        far_bias[r, :] = jnp.where((keys >= lo_row[...]) & (keys <= hi_row[...]), 0.0, NEG_FILL)
        start, size = window(i, rows)
        near = code[start : start + size, :] == code_row[:, r]
        near_bias[i] = jnp.where(near, 0.0, NEG_FILL)


def beside(block):
    return jnp.concatenate([block, block], axis=1)


def stack_heads(block):
    lane = lax.broadcasted_iota(jnp.int32, block.shape, 1)
    zero = jnp.zeros_like(block)
    return jnp.concatenate(
        [jnp.where(lane < HEAD_DIM, block, zero), jnp.where(lane < HEAD_DIM, zero, block)], axis=0
    )


def unstack_heads(block):
    half = block.shape[0] // 2
    lane = lax.broadcasted_iota(jnp.int32, (half, block.shape[1]), 1)
    return jnp.where(lane < HEAD_DIM, block[:half], block[half:])


def twice(block):
    return jnp.concatenate([block, block], axis=0)


def attend_body(noisy_ref, lo, hi, code, code_row, q, k, v, kf, vf, o, lse, far_bias, near_bias):
    rows = q.shape[0]

    @pl.when(pl.program_id(0) == 0)
    def _():
        build_masks(lo, hi, code, code_row, far_bias, near_bias)

    def run(noisy):
        for i in range(rows // TILE):
            r = slice(i * TILE, (i + 1) * TILE)
            q2 = stack_heads(q[r, :])
            w = far_width(i, rows, noisy)
            s = dot_nt(q2, kf[:w, :]) * (SCORE_SCALE * LOG2_E) + twice(far_bias[r, :w])
            top = jnp.max(s, axis=-1, keepdims=True)
            if noisy:
                start, size = window(i, rows)
                n = slice(start, start + size)
                sn = dot_nt(q2, k[n, :]) * (SCORE_SCALE * LOG2_E) + twice(near_bias[i])
                top = jnp.maximum(top, jnp.max(sn, axis=-1, keepdims=True))
            e = jnp.exp2(s - top)
            total = jnp.sum(e, axis=-1, keepdims=True)
            mixed = dot(e.astype(BF16), vf[:w, :])
            if noisy:
                en = jnp.exp2(sn - top)
                total = total + jnp.sum(en, axis=-1, keepdims=True)
                mixed = mixed + dot(en.astype(BF16), v[n, :])
            o[r, :] = unstack_heads(mixed * (1.0 / total)).astype(BF16)
            log_sum = jnp.broadcast_to(top + jnp.log2(total), (2 * TILE, PAIR))
            lse[:, 2 * TILE * i : 2 * TILE * (i + 1)] = log_sum.T[:8]

    @pl.when(noisy_ref[0] == 1)
    def _():
        run(True)

    @pl.when(noisy_ref[0] == 0)
    def _():
        run(False)


def mask_scratch(rows):
    return [
        pltpu.VMEM((rows, rows), F32),
        pltpu.VMEM((rows // TILE, TILE, TILE + 2 * REACH), F32),
    ]


def attend(noisy, lo, hi, code, code_row, q, k, v, kf, vf):
    rows, width = q.shape
    pair = pl.BlockSpec((rows, PAIR), lambda j: (0, j))
    return pl.pallas_call(
        attend_body,
        grid=(width // PAIR,),
        out_shape=[like((rows, width), BF16), like((8 * (width // PAIR), 2 * rows), F32)],
        in_specs=[SMEM_SPEC] + [whole_spec((rows, 1))] * 3 + [whole_spec((1, rows))] + [pair] * 5,
        out_specs=[pair, pl.BlockSpec((8, 2 * rows), lambda j: (j, 0))],
        scratch_shapes=mask_scratch(rows),
        compiler_params=pltpu.CompilerParams(vmem_limit_bytes=12 * 2**20),
        cost_estimate=SHORT,
    )(noisy, lo, hi, code, code_row, q, k, v, kf, vf)


def attend_back_body(
    early, noisy_ref, place_ref, code, lo_row, hi_row, code_row, q, k, v, kf, vf, o, lse, ga, out_w, wq, wk, wv,
    first_t, far_first_t, cos, sin, own, far, *refs,
):
    outs, (far_bias, near_bias, acc_k, acc_v, acc_kf, acc_vf, dw_own, dw_rest) = refs[:-8], refs[-8:]
    rows = q.shape[0]

    @pl.when(pl.program_id(0) == 0)
    def _():
        build_turned_masks(code, lo_row, hi_row, code_row, far_bias, near_bias)
        own[...] = jnp.zeros_like(own)
        far[...] = jnp.zeros_like(far)

    go = dot_nt(ga[...], out_w[...]).astype(BF16)

    def turn_back(x):
        return (x * cos[...] - half_swap(x) * sin[...]).astype(BF16)

    def run(noisy):
        acc_kf[...] = jnp.zeros_like(acc_kf)
        acc_vf[...] = jnp.zeros_like(acc_vf)
        if noisy:
            acc_k[...] = jnp.zeros_like(acc_k)
            acc_v[...] = jnp.zeros_like(acc_v)
        parts = []
        for i in range(rows // TILE):
            r = slice(i * TILE, (i + 1) * TILE)
            q2 = stack_heads(q[r, :])
            go2 = stack_heads(go[r, :])
            delta = jnp.sum(
                (go2.astype(F32) * twice(o[r, :]).astype(F32)).T, axis=0, keepdims=True
            )
            log_sum = lse[0:1, 2 * TILE * i : 2 * TILE * (i + 1)]

            def one(keys, values, bias, acc_keys, acc_values, where):
                s = dot_nt(keys, q2) * (SCORE_SCALE * LOG2_E) + beside(bias)
                p = jnp.exp2(s - log_sum)
                gp = dot_nt(values, go2)
                ds = (p * (gp - delta)).astype(BF16)
                acc_keys[where, :] += dot(ds, q2)
                acc_values[where, :] += dot(p.astype(BF16), go2)
                return dot_tn(keys, ds)

            w = far_width(i, rows, noisy)
            gq = one(kf[:w, :], vf[:w, :], far_bias[:w, r], acc_kf, acc_vf, slice(0, w))
            if noisy:
                start, size = window(i, rows)
                n = slice(start, start + size)
                gq = gq + one(k[n, :], v[n, :], near_bias[i], acc_k, acc_v, n)
            parts.append(unstack_heads(gq.T))
        dq = turn_back(jnp.concatenate(parts, axis=0) * SCORE_SCALE)
        dkf = turn_back(acc_kf[...] * SCORE_SCALE)
        dvf = acc_vf[...].astype(BF16)
        g_far = jnp.concatenate([dkf, dvf], axis=1)
        w_far = jnp.concatenate([wk[...], wv[...]], axis=1)
        far[...] += dot_nt(g_far, w_far)
        dw_far = dot(far_first_t[...], g_far)
        if noisy:
            dk = turn_back(acc_k[...] * SCORE_SCALE)
            dv = acc_v[...].astype(BF16)
            g_own = jnp.concatenate([dq, dk, dv], axis=1)
            own[...] += dot_nt(g_own, jnp.concatenate([wq[...], w_far], axis=1))
            dw = dot(first_t[...], g_own)
            dw_far = dw[:, PAIR:] + dw_far
        else:
            own[...] += dot_nt(dq, wq[...])
            dw = dot(first_t[...], dq)
        dw_own[...] = dw[:, :PAIR].astype(BF16)
        dw_rest[...] = dw_far.astype(BF16)

    @pl.when(noisy_ref[0] == 1)
    def _():
        run(True)

    @pl.when(noisy_ref[0] == 0)
    def _():
        run(False)

    def store(some):
        store_rows(dw_own[...], place_ref, some, slice(0, PAIR))
        store_rows(dw_rest[...], place_ref, some, slice(PAIR, 3 * PAIR))

    half = len(outs) // 2

    @pl.when(pl.program_id(0) < early)
    def _():
        store(outs[:half])

    @pl.when(pl.program_id(0) >= early)
    def _():
        store(outs[half:])


def attend_back(noisy, place_in, masks, heads, ga, joint, first_t, far_first_t, cos, sin, early):
    rows, width = ga.shape
    pairs = width // PAIR
    pair = pl.BlockSpec((rows, PAIR), lambda j: (0, j))

    def strip(part):
        return pl.BlockSpec((width, PAIR), lambda j: (0, part * pairs + j))

    shapes, out_specs = [], []
    for first, last in ((0, early), (early, pairs)):
        for shape in row_grad_shapes(width, 3 * PAIR * (last - first)):
            shapes.append(shape)
            out_specs.append(
                pl.BlockSpec(
                    shape[:-1] + (3 * PAIR,),
                    lambda j, first=first, last=last, n=len(shape): (0,) * (n - 1)
                    + (jnp.clip(j, first, last - 1) - first,),
                )
            )
    act = whole_spec((rows, width))
    turned = whole_spec((width, rows))
    outs = pl.pallas_call(
        partial(attend_back_body, early),
        grid=(pairs,),
        out_shape=[like((rows, width), F32)] * 2 + [like(shape, BF16) for shape in shapes],
        in_specs=[SMEM_SPEC] * 2
        + [whole_spec((rows, 1))]
        + [whole_spec((1, rows))] * 3
        + [pair] * 6
        + [pl.BlockSpec((8, 2 * rows), lambda j: (j, 0))]
        + [act, pl.BlockSpec((PAIR, width), lambda j: (j, 3))]
        + [strip(0), strip(1), strip(2), turned, turned]
        + [whole_spec((rows, PAIR))] * 2,
        out_specs=[act] * 2 + out_specs,
        scratch_shapes=[
            pltpu.VMEM((rows, rows), F32),
            pltpu.VMEM((rows // TILE, TILE + 2 * REACH, TILE), F32),
        ]
        + [pltpu.VMEM((rows, PAIR), F32)] * 4
        + [pltpu.VMEM((width, PAIR), BF16), pltpu.VMEM((width, 2 * PAIR), BF16)],
        compiler_params=pltpu.CompilerParams(vmem_limit_bytes=32 * 2**20),
        cost_estimate=SHORT,
    )(
        noisy,
        place_in,
        *in_hbm(*masks, *heads, ga, joint, joint, joint, joint, first_t, far_first_t, cos, sin),
    )
    half = len(shapes) // 2
    return outs[0], outs[1], outs[2 : 2 + half], outs[2 + half :]


def store_rows(value, place_ref, outs, columns):
    if len(outs) == 1:
        outs[0][:, columns] = value.astype(BF16)
        return
    keep, send = outs
    _, far_count, pair_rows, _ = keep.shape
    core, near, far = place_ref[0], place_ref[1], place_ref[2]
    for z in range(far_count):
        for y in range(2):
            start = (z * 2 + y) * 2 * pair_rows
            first = value[start : start + pair_rows].astype(BF16)
            second = value[start + pair_rows : start + 2 * pair_rows].astype(BF16)
            keep[y ^ near, z ^ far, :, columns] = jnp.where(core == 0, first, second)
            send[y ^ near, z ^ far, :, columns] = jnp.where(core == 0, second, first)


def mlp_body(n_up, *refs):
    (
        place_ref, tok, o, cot, out_w, extra, up_w, down_w, within, which,
        layer_out, gy, ga, *dups, lines, up_lines,
        y1, second, out_acc, gsec_acc, up_line, grad_line,
    ) = refs
    dups, ddowns = dups[:n_up], dups[n_up:]
    step = pl.program_id(0)

    @pl.when(step == 0)
    def _():
        rows = tok[...].astype(F32) + dot(o[...], out_w[...])
        y1[...] = rows
        norm, _ = normed(rows)
        second[...] = (norm * small_row(extra, 1)).astype(BF16)
        out_acc[...] = jnp.zeros_like(out_acc)
        gsec_acc[...] = jnp.zeros_like(gsec_acc)
        lines[...] = jnp.zeros_like(lines)
        lines[2:3, :] = jnp.sum(cot[...].astype(F32), axis=0, keepdims=True)
        chunk = up_w.shape[1]
        quarter = chunk // 4
        row = lax.broadcasted_iota(jnp.int32, (8, SMALL), 0)
        lane = lax.broadcasted_iota(jnp.int32, (8, SMALL), 1)
        pick = (lane == row + 3).astype(BF16)
        line = lax.broadcasted_iota(jnp.int32, (8, chunk), 0)
        for j in range(up_line.shape[0]):
            four = dot_nt(pick, extra[j * quarter : (j + 1) * quarter, :]).astype(BF16)
            values = jnp.where(line == which[...], dot_nt(four, within[...]), 0.0)
            up_line[j : j + 1, :] = jnp.sum(values, axis=0, keepdims=True)

    up_b = up_line[pl.ds(step, 1), :]
    x = dot(second[...], up_w[...]) + up_b
    square = x * x
    t = jnp.tanh(x * (GELU_A + (GELU_A * GELU_B) * square))
    half_t = 0.5 + 0.5 * t
    act = (x * half_t).astype(BF16)
    slope = half_t + (0.5 * x) * (1.0 - t * t) * (GELU_A + (3.0 * GELU_A * GELU_B) * square)
    g_pre = (dot_nt(cot[...], down_w[...]) * slope).astype(BF16)
    dup_b = jnp.sum(g_pre.astype(F32), axis=0, keepdims=True)
    grad_line[pl.ds(step, 1), :] = dup_b
    out_acc[...] += dot(act, down_w[...])
    gsec_acc[...] += dot_nt(g_pre, up_w[...])
    down_grad = dot_tn(act, cot[...])
    if len(ddowns) == 1:
        ddowns[0][...] = down_grad.astype(BF16)
    else:
        pair_rows = down_grad.shape[0] // 4
        core, near = place_ref[0], place_ref[1]
        for y in range(2):
            start = 2 * y * pair_rows
            first = down_grad[start : start + pair_rows].astype(BF16)
            other = down_grad[start + pair_rows : start + 2 * pair_rows].astype(BF16)
            ddowns[0][y ^ near, 0] = jnp.where(core == 0, first, other)
            ddowns[1][y ^ near, 0] = jnp.where(core == 0, other, first)
    store_rows(dot_tn(second[...], g_pre), place_ref, dups, slice(None))

    @pl.when(step == pl.num_programs(0) - 1)
    def _():
        up_lines[...] = jnp.zeros_like(up_lines)
        for j in range(4):
            up_lines[j] = dot(jnp.where(which[...] == j, grad_line[...], 0.0).astype(BF16), within[...])
        rows = y1[...]
        layer_out[...] = (rows + out_acc[...] + small_row(extra, 2)).astype(BF16)
        norm, inverse = normed(rows)
        gs = gsec_acc[...]
        lines[1:2, :] = jnp.sum(gs * norm, axis=0, keepdims=True)
        g = cot[...].astype(F32) + norm_term(gs, norm, inverse, small_row(extra, 1))
        gy[...] = g
        ga[...] = g.astype(BF16)


def row_grad_shapes(width, columns):
    pair_rows = 2 * (width // device_count())
    if pair_rows % 16:
        return [(width, columns)]
    return [(2, device_count() // 8, pair_rows, columns)] * 2


def mlp(place_in, tok, o, cot, joint, up_w, down_w):
    rows, width = tok.shape
    hidden = up_w.shape[1]
    ups = row_grad_shapes(width, hidden)
    pair_rows = 2 * (hidden // device_count())
    if len(ups) == 1:
        chunk = hidden // 4
        up_specs = [pl.BlockSpec((width, chunk), lambda j, _: (0, j))]
        downs = [(hidden, width)]
        down_specs = [pl.BlockSpec((chunk, width), lambda j, _: (j, 0))]
    else:
        chunk = 4 * pair_rows
        far_count = device_count() // 8
        up_specs = [pl.BlockSpec(ups[0][:3] + (chunk,), lambda j, _: (0, 0, 0, j))] * 2
        downs = [(2, far_count, pair_rows, width)] * 2
        down_specs = [
            pl.BlockSpec((2, 1, pair_rows, width), lambda j, p: (0, j ^ p[2], 0, 0))
        ] * 2
    act = whole_spec((rows, width))
    extra, _, out_w = joint_specs(width)
    up_in = pl.BlockSpec((width, chunk), lambda j, _: (0, j))
    shard = hidden // device_count()
    unit = np.arange(chunk)
    within = (unit // shard) * (shard // 4) + unit % (shard // 4)
    which = (unit % shard) // (shard // 4)
    within = jnp.asarray(within[:, None] == np.arange(chunk // 4)[None, :], BF16)
    which = jnp.asarray(which[None], jnp.int32)
    down_in = pl.BlockSpec((chunk, width), lambda j, _: (j, 0))
    outs = pl.pallas_call(
        partial(mlp_body, len(ups)),
        grid_spec=pltpu.PrefetchScalarGridSpec(
            num_scalar_prefetch=1,
            grid=(hidden // chunk,),
            in_specs=[act, act, act, out_w, extra, up_in, down_in]
            + [whole_spec((chunk, chunk // 4)), whole_spec((1, chunk))],
            out_specs=[act, act, act]
            + up_specs
            + down_specs
            + [whole_spec((8, width)), whole_spec((8, hidden // chunk, chunk // 4))],
            scratch_shapes=[
                pltpu.VMEM((rows, width), F32),
                pltpu.VMEM((rows, width), BF16),
                pltpu.VMEM((rows, width), F32),
                pltpu.VMEM((rows, width), F32),
                pltpu.VMEM((hidden // chunk, chunk), F32),
                pltpu.VMEM((hidden // chunk, chunk), F32),
            ],
        ),
        out_shape=[like((rows, width), BF16), like((rows, width), F32), like((rows, width), BF16)]
        + [like(shape, BF16) for shape in ups + downs]
        + [like((8, width), F32), like((8, hidden // chunk, chunk // 4), F32)],
        compiler_params=pltpu.CompilerParams(vmem_limit_bytes=32 * 2**20),
        cost_estimate=SHORT,
    )(place_in, tok, o, cot, joint, joint, up_w, down_w, within, which)
    n = len(ups)
    return (*outs[:3], outs[3 : 3 + n], outs[3 + n : 3 + 2 * n], outs[-2], outs[-1])


def finish_body(
    noisy_ref, place_ref, tok, far_tok, extra, own, far, gy, o, ga, lines, up_lines,
    part, send, *outs
):
    width = tok.shape[1]
    g = small_row(extra, 0)
    norm, inverse = normed(tok[...].astype(F32))
    own, far = own[...], far[...]

    def put_lines(gains):
        row = lax.broadcasted_iota(jnp.int32, (8, width), 0)
        values = jnp.where(row == 0, gains, lines[...]).astype(BF16)
        row = lax.broadcasted_iota(jnp.int32, (8, SMALL), 0)
        lane = lax.broadcasted_iota(jnp.int32, (8, SMALL), 1)
        small = dot_tn(values, (row == lane).astype(BF16))
        later = (row + 3 == lane).astype(BF16)
        biases = [dot_tn(up_lines[:, j, :].astype(BF16), later) for j in range(up_lines.shape[1])]
        small = small + jnp.concatenate(biases, axis=0)
        store_rows(small, place_ref, outs, slice(width, width + SMALL))

    half = width // 2
    for start in (0, half):
        c = slice(start, start + half)
        store_rows(dot_tn(o[...], ga[:, c]), place_ref, outs, c)

    @pl.when(noisy_ref[0] == 1)
    def _():
        part[...] = gy[...] + norm_term(own, norm, inverse, g)
        far_norm, far_inverse = normed(far_tok[...].astype(F32))
        send[...] = norm_term(far, far_norm, far_inverse, g).astype(BF16)
        put_lines(jnp.sum(own * norm + far * far_norm, axis=0, keepdims=True))

    @pl.when(noisy_ref[0] == 0)
    def _():
        both = own + far
        part[...] = gy[...] + norm_term(both, norm, inverse, g)
        send[...] = jnp.zeros_like(send)
        put_lines(jnp.sum(both * norm, axis=0, keepdims=True))


def finish(noisy, place_in, tok, far_tok, joint, own, far, gy, o, ga, lines, up_lines):
    rows, width = tok.shape
    act = whole_spec((rows, width))
    extra, _, _ = joint_specs(width)
    shapes = row_grad_shapes(width, width + SMALL)
    outs = pl.pallas_call(
        finish_body,
        grid=(1,),
        out_shape=[like((rows, width), F32), like((rows, width), BF16)]
        + [like(shape, BF16) for shape in shapes],
        in_specs=[SMEM_SPEC] * 2 + [act, act, extra] + [act] * 5
        + [whole_spec((8, width)), whole_spec(up_lines.shape)],
        out_specs=[act, act] + [whole_spec(shape) for shape in shapes],
        compiler_params=pltpu.CompilerParams(vmem_limit_bytes=32 * 2**20),
        cost_estimate=SHORT,
    )(noisy, place_in, tok, far_tok, joint, own, far, gy, o, ga, lines, up_lines)
    return outs[0], outs[1], outs[2:]


def local(
    tokens,
    lengths,
    cotangent,
    attn_gain,
    qkv_weight,
    out_weight,
    mlp_gain,
    up_weight,
    up_bias,
    down_weight,
    down_bias,
):
    rows, width = tokens.shape[1:]
    stream = lax.axis_index("stream").astype(jnp.int32)
    me = (lax.axis_index("seq").astype(jnp.int32) * 2 + stream)[None]
    noisy = stream[None]
    n_dev = device_count()
    tok = tokens[0]
    cot = cotangent[0]

    shard_rows = qkv_weight.shape[0]
    small = [v.reshape(shard_rows, 1) for v in (attn_gain, mlp_gain, down_bias)]
    small.append(up_bias.reshape(4, shard_rows).T)
    spare = SMALL - sum(v.shape[1] for v in small)
    joint = jnp.concatenate([qkv_weight, out_weight] + small + [jnp.zeros((shard_rows, spare), BF16)], axis=1)
    cut = 2 * width
    j1, jkey = far_gather(joint, [0])
    far_tok = lax.ppermute(tok, "stream", [(0, 1)])
    u1, ukey = far_gather(after(up_weight, j1, far_tok), [0])
    a2, akey = near_gather(after(j1, far_tok)[:, :, :cut], jkey, STREAM_BIT)
    b2, bkey = near_gather(after(j1, far_tok)[:, :, cut:], jkey, NEAR_BIT)
    d1, dkey = far_gather(after(down_weight, u1, a2, b2), [0])
    a2, b2 = after(a2, b2, u1), after(b2, a2, u1)
    a3, akey = last_gather(a2, akey, NEAR_BIT, d1)
    b3, bkey = last_gather(b2, bkey, STREAM_BIT, d1)
    u2, ukey = near_gather(after(u1, d1, a3[1], b3[1]), ukey, NEAR_BIT)
    d2, dkey = near_gather(after(d1, u1, a3[1], b3[1]), dkey, STREAM_BIT)
    joint = place([a3, b3], [akey, bkey], me).reshape(width, -1)

    doc_ids, positions = doc_layout(lengths[0], rows)
    cosine, sine = rotary_tables(positions, HEAD_DIM)
    cos = jnp.concatenate([cosine] * 4, axis=1)
    sin = jnp.concatenate([-sine, sine] * 2, axis=1)
    lo = doc_ids * rows
    code = lo + positions // BLOCK
    masks = (lo[:, None], (code - stream)[:, None], code[:, None], code[None, :])

    joint = after(joint, u2, d2)
    place_in = jnp.stack([(me[0] // bit) % 2 for bit in (CORE_BIT, NEAR_BIT)] + [me[0] // (2 * NEAR_BIT)])
    first_t, far_first_t, q, k, v, kf, vf = front(noisy, tok, far_tok, joint, cos, sin)
    o, lse = attend(noisy, *masks, q, k, v, kf, vf)
    u3, ukey = last_gather(u2, ukey, STREAM_BIT, o)
    d3, dkey = last_gather(d2, dkey, NEAR_BIT, o)
    up_full = place([u3], [ukey], me).reshape(width, -1)
    down_full = place([d3], [dkey], me).reshape(-1, width)
    layer_out, gy, ga, dup, ddown, lines, up_lines = mlp(place_in, tok, o, cot, joint, up_full, down_full)

    up_sum, down_sum = Sum(me, dup), Sum(me, ddown)
    split((up_sum, NEAR_BIT), (down_sum, STREAM_BIT))
    up_sum.flip(NEAR_BIT)
    down_sum.flip(STREAM_BIT)
    ga_next = after(ga, up_sum.send, down_sum.send)
    heads = (q, k, v, kf, vf, o, lse)
    turned_masks = (code[:, None], lo[None], (code - stream)[None], code[None])
    pairs = width // PAIR
    early = 2 * pairs // 3
    own, far, front_outs, back_outs = attend_back(
        noisy, place_in, turned_masks, heads, ga_next, joint, first_t, far_first_t, cos, sin, early
    )
    up_sum.hold(*front_outs)
    down_sum.hold(*front_outs)
    split((up_sum, STREAM_BIT), (down_sum, NEAR_BIT))
    up_sum.flip(STREAM_BIT)
    down_sum.flip(NEAR_BIT)
    front_sum = Sum(me, [after(a, up_sum.send, down_sum.send) for a in front_outs])
    back_sum = Sum(me, [after(a, up_sum.send, down_sum.send) for a in back_outs])
    up_sum.hold(front_sum.got, back_sum.got)
    down_sum.hold(front_sum.got, back_sum.got)
    gy = after(gy, up_sum.send, down_sum.send)
    part, send, outs = finish(
        noisy, place_in, tok, far_tok, joint, own, far, gy, o, ga, lines, up_lines
    )
    back_sum.add(outs)
    half = rows // 2
    received = [lax.ppermute(send[:half], "stream", [(1, 0)])]
    mlp_far = Far([up_sum, down_sum], LONG)
    back_sum.hold(*mlp_far.sends)
    split((front_sum, STREAM_BIT), (back_sum, NEAR_BIT))
    front_sum.flip(STREAM_BIT)
    back_sum.flip(NEAR_BIT)
    mlp_far.flip()
    back_sum.hold(received[0])
    split((front_sum, NEAR_BIT), (back_sum, STREAM_BIT))
    front_sum.flip(NEAR_BIT)
    back_sum.flip(STREAM_BIT)
    back_sum.hold(*mlp_far.got)
    attn_far = Far([front_sum, back_sum])
    later = after(send[half:], *attn_far.sends)
    received.append(lax.ppermute(later, "stream", [(1, 0)]))
    owned_mlp = mlp_far.result()
    owned_attn = attn_far.flip().result()
    grad_input = part + jnp.concatenate(received, axis=0).astype(F32)

    hidden = up_weight.shape[1]
    owned_up = owned_mlp[:, :hidden]
    owned_down = owned_mlp[:, hidden:].reshape(shard_rows, -1, width)
    owned_down = owned_down.transpose(1, 0, 2).reshape(-1, width)
    owned_front = owned_attn[:, : 3 * PAIR * early]
    owned_back = owned_attn[:, 3 * PAIR * early :]
    strips = [owned_front[:, i * PAIR : (i + 1) * PAIR] for i in range(3 * early)]
    strips += [owned_back[:, i * PAIR : (i + 1) * PAIR] for i in range(3 * (pairs - early))]
    owned_qkv = jnp.concatenate([s for p in range(3) for s in strips[p::3]], axis=1)
    owned_out = owned_back[:, 3 * PAIR * (pairs - early) :]
    owned_small = owned_out[:, width:]

    def small_owned(i):
        return owned_small[:, i]

    return (
        layer_out[None],
        grad_input[None],
        small_owned(0),
        owned_qkv,
        owned_out[:, :width],
        small_owned(1),
        owned_up,
        owned_small[:, 3:7].T.reshape(-1),
        owned_down,
        small_owned(2),
    )


def solution(mesh):
    placed = (
        P("stream", "seq", None),
        P("seq", None),
        P("stream", "seq", None),
        P(("seq", "stream")),
        P(("seq", "stream"), None),
        P(("seq", "stream"), None),
        P(("seq", "stream")),
        P(("seq", "stream"), None),
        P(("seq", "stream")),
        P(("seq", "stream"), None),
        P(("seq", "stream")),
    )
    return jax.shard_map(
        local,
        mesh=mesh,
        in_specs=placed,
        out_specs=(
            P("stream", "seq", None),
            P("stream", "seq", None),
            P(("seq", "stream")),
            P(("seq", "stream"), None),
            P(("seq", "stream"), None),
            P(("seq", "stream")),
            P(("seq", "stream"), None),
            P(("seq", "stream")),
            P(("seq", "stream"), None),
            P(("seq", "stream")),
        ),
        check_vma=False,
    )
```

profile of v0, /device:TPU:0, one launch (start us, length us, event | category | flops | bytes accessed | tf_op | source)
XLA Modules:
  0.0 252.5 jit_solution(6496300461278555551)
XLA Ops:
  0.7 5.0 %collective-permute-start = (bf16[512,768]{1,0:T(8,128)(2,1)}, bf16[512,768]{1,0:T(8,128)(2,1)S(1)}, u32[]{:S(2)}, u32[]{:S(2)}) collective-permute-start(bf16[512,768]{1,0:T(8,128)(2,1)} %bitcast.59), channel_id=1, source_target_pairs={{0,1},{2,3},{4,5},{6,7},{8,9},{10,11},{12,13},{14,15},{16,17},{18,... | collective-permute-start | bytes 2359304 | tf_op jit(solution)/shard_map/ppermute | solution.py:923
  9.8 3.7 %collective-permute-start.3 = (bf16[1,24,3200]{2,1,0:T(8,128)(2,1)S(1)}, bf16[1,24,3200]{2,1,0:T(8,128)(2,1)S(1)}, u32[]{:S(2)}, u32[]{:S(2)}) collective-permute-start(bf16[1,24,3200]{2,1,0:T(8,128)(2,1)S(1)} %bitcast.75), channel_id=1, source_target_pairs={{0,24},{1,25},{2,26},{3,27},{4,28},{5,29},{6,30},{7,31},{8,16},{9,... | collective-permute-start | bytes 460808 | tf_op jit(solution)/shard_map/ppermute | solution.py:43
  14.2 4.4 %collective-permute-done.3 = bf16[1,24,3200]{2,1,0:T(8,128)(2,1)S(1)} collective-permute-done((bf16[1,24,3200]{2,1,0:T(8,128)(2,1)S(1)}, bf16[1,24,3200]{2,1,0:T(8,128)(2,1)S(1)}, u32[]{:S(2)}, u32[]{:S(2)}) %collective-permute-start.3) | collective-permute-done | bytes 153632 | tf_op jit(solution)/shard_map/ppermute | solution.py:43
  18.6 7.6 %collective-permute-done.2 = bf16[1,24,3200]{2,1,0:T(8,128)(2,1)S(1)} collective-permute-done((bf16[1,24,3200]{2,1,0:T(8,128)(2,1)S(1)}, bf16[1,24,3200]{2,1,0:T(8,128)(2,1)S(1)}, u32[]{:S(2)}, u32[]{:S(2)}) %collective-permute-start.2) | collective-permute-done | bytes 153632 | tf_op jit(solution)/shard_map/ppermute | solution.py:43
  34.9 5.2 %collective-permute-done.7 = bf16[1,24,3072]{2,1,0:T(8,128)(2,1)S(1)} collective-permute-done((bf16[1,24,3072]{2,1,0:T(8,128)(2,1)S(1)}, bf16[1,24,3072]{2,1,0:T(8,128)(2,1)S(1)}, u32[]{:S(2)}, u32[]{:S(2)}) %collective-permute-start.7) | collective-permute-done | bytes 147488 | tf_op jit(solution)/shard_map/ppermute | solution.py:43
  50.9 3.4 %collective-permute-done.12 = bf16[1,96,768]{2,1,0:T(8,128)(2,1)S(1)} collective-permute-done((bf16[1,96,768]{2,1,0:T(8,128)(2,1)S(1)}, bf16[1,96,768]{2,1,0:T(8,128)(2,1)S(1)}, u32[]{:S(2)}, u32[]{:S(2)}) %collective-permute-start.12) | collective-permute-done | bytes 147488 | tf_op jit(solution)/shard_map/ppermute | solution.py:43
  54.3 5.3 %collective-permute-done.11 = bf16[1,96,768]{2,1,0:T(8,128)(2,1)S(1)} collective-permute-done((bf16[1,96,768]{2,1,0:T(8,128)(2,1)S(1)}, bf16[1,96,768]{2,1,0:T(8,128)(2,1)S(1)}, u32[]{:S(2)}, u32[]{:S(2)}) %collective-permute-start.11) | collective-permute-done | bytes 147488 | tf_op jit(solution)/shard_map/ppermute | solution.py:43
  63.3 10.8 %collective-permute-done.19 = bf16[4,96,768]{2,1,0:T(8,128)(2,1)S(1)} collective-permute-done((bf16[4,96,768]{2,1,0:T(8,128)(2,1)S(1)}, bf16[4,96,768]{2,1,0:T(8,128)(2,1)S(1)}, u32[]{:S(2)}, u32[]{:S(2)}) %collective-permute-start.19) | collective-permute-done | bytes 589856 | tf_op jit(solution)/shard_map/ppermute | solution.py:43
  87.7 4.6 %shard_map.205 = (bf16[768,512]{1,0:T(8,128)(2,1)S(1)}, bf16[768,512]{1,0:T(8,128)(2,1)S(1)}, bf16[512,768]{1,0:T(8,128)(2,1)S(1)}, bf16[512,768]{1,0:T(8,128)(2...) custom-call(s32[1]{0:T(128)} %bitcast.4.noisy_ref, ...), custom_call_target="tpu_custom_call" | custom-call | flops 1 | bytes 1 | tf_op jit(solution)/shard_map/pallas_call | solution.py:415
  93.2 11.2 %shard_map.206 = (bf16[512,768]{1,0:T(8,128)(2,1)S(1)}, f32[48,1024]{1,0:T(8,128)S(1)}) custom-call(s32[1]{0:T(128)} %bitcast.4.noisy_ref, s32[512,1]{1,0:T(8,128)S(1)} %copy-done.18, s32[512,1]{1,0:T(8,128)S(1)} %get-tuple-element.189.hi, s32[512,1]{1,0:T(8,128)S(1)} %get-tuple-element.190.code, s32[1,512]{1,0:T(1,128)S(1)} %get-tuple-element.188.code_row, ...), custom_call_target="tpu_custom_call" | custom-call | flops 1 | bytes 1 | tf_op jit(solution)/shard_map/pallas_call | solution.py:528
  108.7 3.4 %collective-permute-done.22.refs_3_ = bf16[8,24,3072]{2,1,0:T(8,128)(2,1)} collective-permute-done((bf16[8,24,3072]{2,1,0:T(8,128)(2,1)}, bf16[8,24,3072]{2,1,0:T(8,128)(2,1)}, u32[]{:S(2)}, u32[]{:S(2)}) %collective-permute-start.22) | collective-permute-done | bytes 1179680 | tf_op jit(solution)/shard_map/ppermute | solution.py:43
  119.7 24.1 %shard_map.209 = (bf16[512,768]{1,0:T(8,128)(2,1)}, f32[512,768]{1,0:T(8,128)S(1)}, bf16[512,768]{1,0:T(8,128)(2,1)S(1)}, bf16[2,4,48,3072]{3,2,1,0:T(8,128)(2,1...) custom-call(s32[3]{0:T(128)S(1)} %pad_add_fusion.refs_0_.place_ref, ...), custom_call_target="tpu_custom_call" | custom-call | flops 1 | bytes 1 | tf_op jit(solution)/shard_map/pallas_call | solution.py:806
  144.3 4.0 %collective-permute-done.26 = bf16[2,4,48,3072]{3,2,1,0:T(8,128)(2,1)S(1)} collective-permute-done((bf16[2,4,48,3072]{3,2,1,0:T(8,128)(2,1)S(1)}, bf16[2,4,48,3072]{3,2,1,0:T(8,128)(2,1)S(1)}, u32[]{:S(2)}, u32[]{:S(2)}) %collective-permute-start.26) | collective-permute-done | bytes 2359328 | tf_op jit(solution)/shard_map/ppermute | solution.py:43
  148.3 3.4 %collective-permute-done.27 = bf16[2,4,192,768]{3,2,1,0:T(8,128)(2,1)S(1)} collective-permute-done((bf16[2,4,192,768]{3,2,1,0:T(8,128)(2,1)S(1)}, bf16[2,4,192,768]{3,2,1,0:T(8,128)(2,1)S(1)}, u32[]{:S(2)}, u32[]{:S(2)}) %collective-permute-start.27) | collective-permute-done | bytes 2359328 | tf_op jit(solution)/shard_map/ppermute | solution.py:43
  157.6 21.2 %shard_map.211 = (f32[512,768]{1,0:T(8,128)S(1)}, f32[512,768]{1,0:T(8,128)S(1)}, bf16[2,4,48,1536]{3,2,1,0:T(8,128)(2,1)S(1)}, bf16[2,4,48,1536]{3,2,1,0:T(8,12...) custom-call(s32[1]{0:T(128)} %bitcast.4.noisy_ref, ...), custom_call_target="tpu_custom_call" | custom-call | flops 1 | bytes 1 | tf_op jit(solution)/shard_map/pallas_call | solution.py:654
  189.4 3.1 %shard_map.213 = (f32[512,768]{1,0:T(8,128)S(1)}, bf16[512,768]{1,0:T(8,128)(2,1)S(1)}, bf16[2,4,48,896]{3,2,1,0:T(8,128)(2,1)S(1)}, bf16[2,4,48,896]{3,2,1,0:T(8,128)(2,1)S(1)}) custom-call(s32[1]{0:T(128)} %bitcast.4.noisy_ref, s32[3]{0:T(128)S(1)} %pad_add_fusion.refs_0_.place_ref, bf16[512,768]{1,0:T(8,128)(2,1)S(1)} %bitcast.62, ...), custom_call_target="tpu_custom_call" | custom-call | flops 1 | bytes 1 | tf_op jit(solution)/shard_map/pallas_call | solution.py:881
  194.2 6.2 %collective-permute-done.34.refs_3_ = bf16[1,4,1,96,768]{4,3,2,1,0:T(8,128)(2,1)S(1)} collective-permute-done((bf16[1,4,1,96,768]{4,3,2,1,0:T(8,128)(2,1)S(1)}, bf16[1,4,1,96,768]{4,3,2,1,0:T(8,128)(2,1)S(1)}, u32[]{:S(2)}, u32[]{:S(2)}) %collective-permute-start.34) | collective-permute-done | bytes 589856 | tf_op jit(solution)/shard_map/ppermute | solution.py:43
  200.4 3.1 %collective-permute-done.33.refs_1_ = bf16[1,4,1,24,3072]{4,3,2,1,0:T(8,128)(2,1)S(1)} collective-permute-done((bf16[1,4,1,24,3072]{4,3,2,1,0:T(8,128)(2,1)S(1)}, bf16[1,4,1,24,3072]{4,3,2,1,0:T(8,128)(2,1)S(1)}, u32[]{:S(2)}, u32[]{:S(2)}) %collective-permute-start.33) | collective-permute-done | bytes 589856 | tf_op jit(solution)/shard_map/ppermute | solution.py:43
  208.7 3.3 %collective-permute-done.30 = bf16[256,768]{1,0:T(8,128)(2,1)S(1)} collective-permute-done((bf16[256,768]{1,0:T(8,128)(2,1)S(1)}, bf16[256,768]{1,0:T(8,128)(2,1)S(1)}, u32[]{:S(2)}, u32[]{:S(2)}) %collective-permute-start.30) | collective-permute-done | bytes 393248 | tf_op jit(solution)/shard_map/ppermute | solution.py:980
  213.7 5.8 %collective-permute-done.37.refs_3_ = bf16[1,4,2,24,1664]{4,3,2,1,0:T(8,128)(2,1)S(1)} collective-permute-done((bf16[1,4,2,24,1664]{4,3,2,1,0:T(8,128)(2,1)S(1)}, bf16[1,4,2,24,1664]{4,3,2,1,0:T(8,128)(2,1)S(1)}, u32[]{:S(2)}, u32[]{:S(2)}) %collective-permute-start.37) | collective-permute-done | bytes 639008 | tf_op jit(solution)/shard_map/ppermute | solution.py:43
  219.6 4.1 %collective-permute-done.36.refs_1_ = bf16[2,4,1,24,1536]{4,3,2,1,0:T(8,128)(2,1)S(1)} collective-permute-done((bf16[2,4,1,24,1536]{4,3,2,1,0:T(8,128)(2,1)S(1)}, bf16[2,4,1,24,1536]{4,3,2,1,0:T(8,128)(2,1)S(1)}, u32[]{:S(2)}, u32[]{:S(2)}) %collective-permute-start.36) | collective-permute-done | bytes 589856 | tf_op jit(solution)/shard_map/ppermute | solution.py:43
  224.7 5.1 %collective-permute-done.41 = bf16[1,24,6144]{2,1,0:T(8,128)(2,1)S(1)} collective-permute-done((bf16[1,24,6144]{2,1,0:T(8,128)(2,1)S(1)}, bf16[1,24,6144]{2,1,0:T(8,128)(2,1)S(1)}, u32[]{:S(2)}, u32[]{:S(2)}) %collective-permute-start.41) | collective-permute-done | bytes 294944 | tf_op jit(solution)/shard_map/ppermute | solution.py:43
  229.9 3.2 %collective-permute-done.39.refs_3_ = bf16[1,4,1,24,1664]{4,3,2,1,0:T(8,128)(2,1)S(1)} collective-permute-done((bf16[1,4,1,24,1664]{4,3,2,1,0:T(8,128)(2,1)S(1)}, bf16[1,4,1,24,1664]{4,3,2,1,0:T(8,128)(2,1)S(1)}, u32[]{:S(2)}, u32[]{:S(2)}) %collective-permute-start.39) | collective-permute-done | bytes 319520 | tf_op jit(solution)/shard_map/ppermute | solution.py:43
  241.5 5.2 %collective-permute-done.45 = bf16[1,24,3200]{2,1,0:T(8,128)(2,1)} collective-permute-done((bf16[1,24,3200]{2,1,0:T(8,128)(2,1)S(1)}, bf16[1,24,3200]{2,1,0:T(8,128)(2,1)}, u32[]{:S(2)}, u32[]{:S(2)}) %collective-permute-start.45) | collective-permute-done | bytes 153632 | tf_op jit(solution)/shard_map/ppermute | solution.py:43
  (226 shorter events, 92.1 us)
Async XLA Ops:
  0.7 25.6 %collective-permute-start = (bf16[512,768]{1,0:T(8,128)(2,1)}, bf16[512,768]{1,0:T(8,128)(2,1)S(1)}, u32[]{:S(2)}, u32[]{:S(2)}) collective-permute-start(bf16[512,768]{1,0:T(8,128)(2,1)} %bitcast.59), channel_id=1, source_target_pairs={{0,1},{2,3},{4,5},{6,7},{8,9},{10,11},{12,13},{14,15},{16,17},{18,... | collective-permute-start | bytes 2359304 | tf_op jit(solution)/shard_map/ppermute | solution.py:923
  13.4 12.7 %collective-permute-start.2 = (bf16[1,24,3200]{2,1,0:T(8,128)(2,1)S(1)}, bf16[1,24,3200]{2,1,0:T(8,128)(2,1)S(1)}, u32[]{:S(2)}, u32[]{:S(2)}) collective-permute-start(bf16[1,24,3200]{2,1,0:T(8,128)(2,1)S(1)} %bitcast.76), channel_id=1, source_target_pairs={{0,16},{1,17},{2,18},{3,19},{4,20},{5,21},{6,22},{7,23},{8,24},{9,... | collective-permute-start | bytes 460808 | tf_op jit(solution)/shard_map/ppermute | solution.py:43
  13.4 12.7 %collective-permute-start.1 = (bf16[1,24,3200]{2,1,0:T(8,128)(2,1)S(1)}, bf16[1,24,3200]{2,1,0:T(8,128)(2,1)S(1)}, u32[]{:S(2)}, u32[]{:S(2)}) collective-permute-start(bf16[1,24,3200]{2,1,0:T(8,128)(2,1)S(1)} %bitcast.77), channel_id=1, source_target_pairs={{0,8},{1,9},{2,10},{3,11},{4,12},{5,13},{6,14},{7,15},{8,0},{9,1},... | collective-permute-start | bytes 460808 | tf_op jit(solution)/shard_map/ppermute | solution.py:43
  40.4 19.3 %collective-permute-start.15 = (bf16[8,24,1664]{2,1,0:T(8,128)(2,1)S(1)}, bf16[8,24,1664]{2,1,0:T(8,128)(2,1)S(1)}, u32[]{:S(2)}, u32[]{:S(2)}) collective-permute-start(bf16[8,24,1664]{2,1,0:T(8,128)(2,1)S(1)} %pad_maximum_fusion.refs_4_), channel_id=1, source_target_pairs={{0,1},{1,0},{2,3},{3,2},{4,5},{5,4},{6,7},{7,6},{8,9},{9,8},{10,11... | collective-permute-start | bytes 1916936 | tf_op jit(solution)/shard_map/ppermute | solution.py:43
  40.9 18.8 %collective-permute-start.9 = (bf16[8,24,1536]{2,1,0:T(8,128)(2,1)S(1)}, bf16[8,24,1536]{2,1,0:T(8,128)(2,1)S(1)}, u32[]{:S(2)}, u32[]{:S(2)}) collective-permute-start(bf16[8,24,1536]{2,1,0:T(8,128)(2,1)S(1)} %pad_maximum_fusion.2.refs_0_), channel_id=1, source_target_pairs={{0,4},{1,5},{2,6},{3,7},{4,0},{5,1},{6,2},{7,3},{8,12},{9,13},{10,... | collective-permute-start | bytes 1769480 | tf_op jit(solution)/shard_map/ppermute | solution.py:43
  48.3 11.3 %collective-permute-start.11 = (bf16[1,96,768]{2,1,0:T(8,128)(2,1)S(1)}, bf16[1,96,768]{2,1,0:T(8,128)(2,1)S(1)}, u32[]{:S(2)}, u32[]{:S(2)}) collective-permute-start(bf16[1,96,768]{2,1,0:T(8,128)(2,1)S(1)} %bitcast.85), channel_id=1, source_target_pairs={{0,16},{1,17},{2,18},{3,19},{4,20},{5,21},{6,22},{7,23},{8,24},{9,... | collective-permute-start | bytes 442376 | tf_op jit(solution)/shard_map/ppermute | solution.py:43
  48.3 11.3 %collective-permute-start.10 = (bf16[1,96,768]{2,1,0:T(8,128)(2,1)S(1)}, bf16[1,96,768]{2,1,0:T(8,128)(2,1)S(1)}, u32[]{:S(2)}, u32[]{:S(2)}) collective-permute-start(bf16[1,96,768]{2,1,0:T(8,128)(2,1)S(1)} %bitcast.86), channel_id=1, source_target_pairs={{0,8},{1,9},{2,10},{3,11},{4,12},{5,13},{6,14},{7,15},{8,0},{9,1},... | collective-permute-start | bytes 442376 | tf_op jit(solution)/shard_map/ppermute | solution.py:43
  59.7 14.4 %collective-permute-start.19 = (bf16[4,96,768]{2,1,0:T(8,128)(2,1)S(1)}, bf16[4,96,768]{2,1,0:T(8,128)(2,1)S(1)}, u32[]{:S(2)}, u32[]{:S(2)}) collective-permute-start(bf16[4,96,768]{2,1,0:T(8,128)(2,1)S(1)} %pad_maximum_fusion.4), channel_id=1, source_target_pairs={{0,1},{1,0},{2,3},{3,2},{4,5},{5,4},{6,7},{7,6},{8,9},{9,8},{10,11... | collective-permute-start | bytes 1769480 | tf_op jit(solution)/shard_map/ppermute | solution.py:43
  61.0 20.8 %collective-permute-start.13 = (bf16[8,24,1536]{2,1,0:T(8,128)(2,1)S(1)}, bf16[8,24,1536]{2,1,0:T(8,128)(2,1)}, u32[]{:S(2)}, u32[]{:S(2)}) collective-permute-start(bf16[8,24,1536]{2,1,0:T(8,128)(2,1)S(1)} %pad_maximum_fusion.2.refs_0_), channel_id=1, source_target_pairs={{0,2},{1,3},{2,0},{3,1},{4,6},{5,7},{6,4},{7,5},{8,10},{9,11},{10,... | collective-permute-start | bytes 1769480 | tf_op jit(solution)/shard_map/ppermute | solution.py:43
  61.0 16.1 %collective-permute-start.18 = (bf16[4,24,3072]{2,1,0:T(8,128)(2,1)S(1)}, bf16[4,24,3072]{2,1,0:T(8,128)(2,1)S(1)}, u32[]{:S(2)}, u32[]{:S(2)}) collective-permute-start(bf16[4,24,3072]{2,1,0:T(8,128)(2,1)S(1)} %pad_maximum_fusion.3), channel_id=1, source_target_pairs={{0,4},{1,5},{2,6},{3,7},{4,0},{5,1},{6,2},{7,3},{8,12},{9,13},{10,... | collective-permute-start | bytes 1769480 | tf_op jit(solution)/shard_map/ppermute | solution.py:43
  75.0 30.2 %collective-permute-start.23 = (bf16[8,96,768]{2,1,0:T(8,128)(2,1)}, bf16[8,96,768]{2,1,0:T(8,128)(2,1)}, u32[]{:S(2)}, u32[]{:S(2)}) collective-permute-start(bf16[8,96,768]{2,1,0:T(8,128)(2,1)} %constant_dynamic-update-slice_fusion.2.refs_0_), channel_id=1, source_target_pairs={{0,4},{1,5},{2,6},{3,7},{4,0},{5,1},{6,2},{7,3},{8,12},{9,13},{10,... | collective-permute-start | bytes 3538952 | tf_op jit(solution)/shard_map/ppermute | solution.py:43
  78.0 27.5 %collective-permute-start.20 = (bf16[8,24,3072]{2,1,0:T(8,128)(2,1)}, bf16[8,24,3072]{2,1,0:T(8,128)(2,1)}, u32[]{:S(2)}, u32[]{:S(2)}) collective-permute-start(bf16[8,24,3072]{2,1,0:T(8,128)(2,1)} %constant_dynamic-update-slice_fusion.refs_0_), channel_id=1, source_target_pairs={{0,1},{1,0},{2,3},{3,2},{4,5},{5,4},{6,7},{7,6},{8,9},{9,8},{10,11... | collective-permute-start | bytes 3538952 | tf_op jit(solution)/shard_map/ppermute | solution.py:43
  153.7 28.1 %collective-permute-start.28 = (bf16[1,4,2,24,3072]{4,3,2,1,0:T(8,128)(2,1)S(1)}, bf16[1,4,2,24,3072]{4,3,2,1,0:T(8,128)(2,1)S(1)}, u32[]{:S(2)}, u32[]{:S(2)}) collective-permute-start(bf16[1,4,2,24,3072]{4,3,2,1,0:T(8,128)(2,1)S(1)} %get-tuple-element.129), channel_id=1, source_target_pairs={{0,4},{1,5},{2,6},{3,7},{4,0},{5,1},{6,2},{7,3},{8,12},{9,13},{10,... | collective-permute-start | bytes 3538952 | tf_op jit(solution)/shard_map/ppermute | solution.py:43
  154.8 29.0 %collective-permute-start.29 = (bf16[2,4,1,96,768]{4,3,2,1,0:T(8,128)(2,1)S(1)}, bf16[2,4,1,96,768]{4,3,2,1,0:T(8,128)(2,1)S(1)}, u32[]{:S(2)}, u32[]{:S(2)}) collective-permute-start(bf16[2,4,1,96,768]{4,3,2,1,0:T(8,128)(2,1)S(1)} %get-tuple-element.130), channel_id=1, source_target_pairs={{0,1},{1,0},{2,3},{3,2},{4,5},{5,4},{6,7},{7,6},{8,9},{9,8},{10,11... | collective-permute-start | bytes 3538952 | tf_op jit(solution)/shard_map/ppermute | solution.py:43
  184.5 15.9 %collective-permute-start.31 = (bf16[2,4,48,1536]{3,2,1,0:T(8,128)(2,1)S(1)}, bf16[2,4,48,1536]{3,2,1,0:T(8,128)(2,1)S(1)}, u32[]{:S(2)}, u32[]{:S(2)}) collective-permute-start(bf16[2,4,48,1536]{3,2,1,0:T(8,128)(2,1)S(1)} %get-tuple-element.151), channel_id=1, source_target_pairs={{0,2},{1,3},{2,0},{3,1},{4,6},{5,7},{6,4},{7,5},{8,10},{9,11},{10,... | collective-permute-start | bytes 3538952 | tf_op jit(solution)/shard_map/ppermute | solution.py:43
  185.1 15.3 %collective-permute-start.34 = (bf16[1,4,1,96,768]{4,3,2,1,0:T(8,128)(2,1)S(1)}, bf16[1,4,1,96,768]{4,3,2,1,0:T(8,128)(2,1)S(1)}, u32[]{:S(2)}, u32[]{:S(2)}) collective-permute-start(bf16[1,4,1,96,768]{4,3,2,1,0:T(8,128)(2,1)S(1)} %get-tuple-element.144), channel_id=1, source_target_pairs={{0,4},{1,5},{2,6},{3,7},{4,0},{5,1},{6,2},{7,3},{8,12},{9,13},{10,... | collective-permute-start | bytes 1769480 | tf_op jit(solution)/shard_map/ppermute | solution.py:43
  186.6 16.9 %collective-permute-start.33 = (bf16[1,4,1,24,3072]{4,3,2,1,0:T(8,128)(2,1)S(1)}, bf16[1,4,1,24,3072]{4,3,2,1,0:T(8,128)(2,1)S(1)}, u32[]{:S(2)}, u32[]{:S(2)}) collective-permute-start(bf16[1,4,1,24,3072]{4,3,2,1,0:T(8,128)(2,1)S(1)} %get-tuple-element.143), channel_id=1, source_target_pairs={{0,1},{1,0},{2,3},{3,2},{4,5},{5,4},{6,7},{7,6},{8,9},{9,8},{10,11... | collective-permute-start | bytes 1769480 | tf_op jit(solution)/shard_map/ppermute | solution.py:43
  192.6 19.3 %collective-permute-start.30 = (bf16[256,768]{1,0:T(8,128)(2,1)S(1)}, bf16[256,768]{1,0:T(8,128)(2,1)S(1)}, u32[]{:S(2)}, u32[]{:S(2)}) collective-permute-start(bf16[256,768]{1,0:T(8,128)(2,1)S(1)} %get-tuple-element.191), channel_id=1, source_target_pairs={{1,0},{3,2},{5,4},{7,6},{9,8},{11,10},{13,12},{15,14},{17,16},{19,... | collective-permute-start | bytes 1179656 | tf_op jit(solution)/shard_map/ppermute | solution.py:980
  204.8 14.7 %collective-permute-start.37 = (bf16[1,4,2,24,1664]{4,3,2,1,0:T(8,128)(2,1)S(1)}, bf16[1,4,2,24,1664]{4,3,2,1,0:T(8,128)(2,1)S(1)}, u32[]{:S(2)}, u32[]{:S(2)}) collective-permute-start(bf16[1,4,2,24,1664]{4,3,2,1,0:T(8,128)(2,1)S(1)} %get-tuple-element.169), channel_id=1, source_target_pairs={{0,4},{1,5},{2,6},{3,7},{4,0},{5,1},{6,2},{7,3},{8,12},{9,13},{10,... | collective-permute-start | bytes 1916936 | tf_op jit(solution)/shard_map/ppermute | solution.py:43
  205.4 18.3 %collective-permute-start.36 = (bf16[2,4,1,24,1536]{4,3,2,1,0:T(8,128)(2,1)S(1)}, bf16[2,4,1,24,1536]{4,3,2,1,0:T(8,128)(2,1)S(1)}, u32[]{:S(2)}, u32[]{:S(2)}) collective-permute-start(bf16[2,4,1,24,1536]{4,3,2,1,0:T(8,128)(2,1)S(1)} %get-tuple-element.167), channel_id=1, source_target_pairs={{0,1},{1,0},{2,3},{3,2},{4,5},{5,4},{6,7},{7,6},{8,9},{9,8},{10,11... | collective-permute-start | bytes 1769480 | tf_op jit(solution)/shard_map/ppermute | solution.py:43
  206.3 18.4 %collective-permute-start.40 = (bf16[1,24,6144]{2,1,0:T(8,128)(2,1)S(1)}, bf16[1,24,6144]{2,1,0:T(8,128)(2,1)S(1)}, u32[]{:S(2)}, u32[]{:S(2)}) collective-permute-start(bf16[1,24,6144]{2,1,0:T(8,128)(2,1)S(1)} %get-tuple-element.160), channel_id=1, source_target_pairs={{0,8},{1,9},{2,10},{3,11},{4,12},{5,13},{6,14},{7,15},{8,0},{9,1},... | collective-permute-start | bytes 884744 | tf_op jit(solution)/shard_map/ppermute | solution.py:43
  206.3 23.5 %collective-permute-start.41 = (bf16[1,24,6144]{2,1,0:T(8,128)(2,1)S(1)}, bf16[1,24,6144]{2,1,0:T(8,128)(2,1)S(1)}, u32[]{:S(2)}, u32[]{:S(2)}) collective-permute-start(bf16[1,24,6144]{2,1,0:T(8,128)(2,1)S(1)} %get-tuple-element.161), channel_id=1, source_target_pairs={{0,16},{1,17},{2,18},{3,19},{4,20},{5,21},{6,22},{7,23},{8,24},{9,... | collective-permute-start | bytes 884744 | tf_op jit(solution)/shard_map/ppermute | solution.py:43
  211.9 17.9 %collective-permute-start.42 = (bf16[1,24,6144]{2,1,0:T(8,128)(2,1)S(1)}, bf16[1,24,6144]{2,1,0:T(8,128)(2,1)S(1)}, u32[]{:S(2)}, u32[]{:S(2)}) collective-permute-start(bf16[1,24,6144]{2,1,0:T(8,128)(2,1)S(1)} %get-tuple-element.162), channel_id=1, source_target_pairs={{0,24},{1,25},{2,26},{3,27},{4,28},{5,29},{6,30},{7,31},{8,16},{9,... | collective-permute-start | bytes 884744 | tf_op jit(solution)/shard_map/ppermute | solution.py:43
  234.5 12.2 %collective-permute-start.45 = (bf16[1,24,3200]{2,1,0:T(8,128)(2,1)S(1)}, bf16[1,24,3200]{2,1,0:T(8,128)(2,1)}, u32[]{:S(2)}, u32[]{:S(2)}) collective-permute-start(bf16[1,24,3200]{2,1,0:T(8,128)(2,1)S(1)} %get-tuple-element.177), channel_id=1, source_target_pairs={{0,16},{1,17},{2,18},{3,19},{4,20},{5,21},{6,22},{7,23},{8,24},{9,... | collective-permute-start | bytes 460808 | tf_op jit(solution)/shard_map/ppermute | solution.py:43
  (63 other events, 574.6 us)
where the time goes:
time: 253 us
  waiting for transfers between devices  95.5 us (38%)
  Pallas kernels  76.8 us (30%)
  starting transfers between devices  49.4 us (20%)
  local copies, waits for them, and re-layouts  17.1 us (7%)
  other arithmetic  9.61 us (4%)
  between operations  4.11 us (2%)
    ppermute x44, waiting for transfers between devices, flip(): lax.ppermute(block, ALL, [(i, i ^ mask) for i in range(device_count())])  92.3 us
    ppermute x44, starting transfers between devices, flip(): lax.ppermute(block, ALL, [(i, i ^ mask) for i in range(device_count())])  41.4 us
    pallas_call x1, Pallas kernels, mlp(): pl.pallas_call(partial(mlp_body, len(ups)), grid_spec=pltpu.PrefetchScala...  24.1 us
    pallas_call x1, Pallas kernels, attend_back(): pl.pallas_call(partial(attend_back_body, early), grid=(pairs,), out_shape...  21.2 us
    pallas_call x1, Pallas kernels, attend(): pl.pallas_call(attend_body, grid=(width // PAIR,), out_shape=[like((rows,...  11.2 us
    pallas_call x3, Pallas kernels, place(): pl.pallas_call(body, out_shape=like(shape, flat[0].dtype), in_specs=[SMEM...  8.06 us
    unnamed x99, local copies, waits for them, and re-layouts  5.75 us
  transfers between devices with their start and end apart: 47, of which 24 were waited for; matrix products, arithmetic and copies ran while one was open for 8% of the time, Pallas kernels for 19%

commit v1 on v0

--- a/solution.py
+++ b/solution.py
@@ -78,17 +78,75 @@
     )(me, *flat)
 
 
+def place_pair(up, up_keys, down, down_keys, me):
+    total, (rows, hidden) = sum(len(key) for key in up_keys), up[0].shape[1:]
+    width = total * rows
+    folds = down[0].shape[2] // width
+
+    def body(me_ref, *refs):
+        up_out, down_out, up_sem, down_sem = refs[-4:]
+        for piece, key in zip(refs, up_keys):
+            for j, rel in enumerate(key):
+                pltpu.make_async_copy(piece.at[j], up_out.at[me_ref[0] ^ rel], up_sem).start()
+        for piece, key in zip(refs[len(up) :], down_keys):
+            for j, rel in enumerate(key):
+                for f in range(folds):
+                    part = piece.at[j, :, pl.ds(f * width, width)]
+                    pltpu.make_async_copy(part, down_out.at[me_ref[0] ^ rel, f], down_sem).start()
+        pltpu.make_async_copy(up_out, up_out, up_sem).wait()
+        pltpu.make_async_copy(down_out, down_out, down_sem).wait()
+
+    return pl.pallas_call(
+        body,
+        out_shape=[like((total, rows, hidden), BF16), like((total, folds, rows, width), BF16)],
+        in_specs=[SMEM_SPEC] + [pl.BlockSpec(memory_space=pl.ANY)] * len(up + down),
+        out_specs=[VMEM_SPEC] * 2,
+        scratch_shapes=[pltpu.SemaphoreType.DMA] * 2,
+        compiler_params=pltpu.CompilerParams(
+            vmem_limit_bytes=4 * total * rows * hidden * (16 // min(16, rows)) + 2**20
+        ),
+        cost_estimate=SHORT,
+    )(me, *up, *down)
+
+
 def after(block, *others):
     return lax.optimization_barrier((block,) + others)[0]
 
 
-def far_gather(shard, key):
-    piece = shard[None]
-    for group in far_groups():
+def stack_body(count, widths, *refs):
+    ins, outs = refs[:count], refs[count:]
+    column = 0
+    for out, width in zip(outs, widths):
+        at = 0
+        for piece in ins:
+            out[at : at + piece.shape[0]] = piece[:, :, column : column + width]
+            at += piece.shape[0]
+        column += width
+
+
+def stack(pieces, widths, cost):
+    total, rows = sum(p.shape[0] for p in pieces), pieces[0].shape[1]
+    return pl.pallas_call(
+        partial(stack_body, len(pieces), widths),
+        out_shape=[like((total, rows, width), BF16) for width in widths],
+        in_specs=[VMEM_SPEC] * len(pieces),
+        out_specs=[VMEM_SPEC] * len(widths),
+        compiler_params=pltpu.CompilerParams(vmem_limit_bytes=16 * 2**20),
+        cost_estimate=cost,
+    )(*pieces)
+
+
+def far_gather(shard, widths, cost, *others):
+    piece, key = shard[None], [0]
+    groups = far_groups()
+    for group in groups:
         got = [piece] + [flip(piece, mask) for mask in group]
         key = [k ^ mask for mask in [0] + group for k in key]
-        piece = jnp.concatenate(got, axis=0)
-    return piece, key
+        if group != groups[-1]:
+            piece = jnp.concatenate(got, axis=0)
+    if others:
+        got[-1] = after(got[-1], *others)
+    return stack(got, widths, cost), key
 
 
 def near_gather(piece, key, bit):
@@ -100,7 +158,7 @@
     if others:
         got = after(got, *others)
     pieces, keys = [piece, got], [key, [k ^ bit for k in key]]
-    pieces = pieces + [flip(after(p, got), CORE_BIT) for p in pieces]
+    pieces = pieces + [flip(p, CORE_BIT) for p in pieces]
     return pieces, keys + [[k ^ CORE_BIT for k in key] for key in keys]
 
 
@@ -249,22 +307,20 @@
 
     def flip(self):
         self.got = [flip(s, mask) for s, mask in zip(self.sends, self.order[0])]
-        return self
-
-    def result(self):
-        total = self.keep
-        for block in self.got:
-            total = total + block.astype(F32)
+        return self.advance()
+
+    def advance(self):
         for group in self.order[1:]:
+            total = self.keep
+            for block in self.got:
+                total = total + block.astype(F32)
             part = total.shape[0] // (len(group) + 1)
             got = [
                 flip(total[(i + 1) * part : (i + 2) * part].astype(BF16), mask)
                 for i, mask in enumerate(group)
             ]
-            total = total[:part]
-            for block in got:
-                total = total + block.astype(F32)
-        return total[0]
+            self.keep, self.got = total[:part], got
+        return self
 
 
 def split(*jobs):
@@ -360,13 +416,54 @@
     )
 
 
+def prepare_body(qkv, out, up, down, attn_gain, mlp_gain, down_bias, up_bias, joint, pair_weights):
+    rows, hidden = up.shape
+    width = out.shape[1]
+    joint[:, : 3 * width] = qkv[...]
+    joint[:, 3 * width : 4 * width] = out[...]
+    lane = lax.broadcasted_iota(jnp.int32, (rows, SMALL), 1)
+    small = jnp.zeros((rows, SMALL), F32)
+    column = 0
+    for line in (attn_gain, mlp_gain, down_bias, up_bias):
+        values = line[...].astype(F32)
+        for start in range(0, line.shape[1], rows):
+            row = lax.broadcasted_iota(jnp.int32, (rows, line.shape[1]), 0)
+            item = lax.broadcasted_iota(jnp.int32, (rows, line.shape[1]), 1)
+            picked = jnp.sum(jnp.where(item == row + start, values, 0.0), axis=1, keepdims=True)
+            small = jnp.where(lane == column, picked, small)
+            column += 1
+    joint[:, 4 * width :] = small.astype(BF16)
+    pair_weights[:, :hidden] = up[...]
+    tall = down[...].astype(F32)
+    for fold in range(down.shape[0] // rows):
+        at = hidden + fold * width
+        pair_weights[:, at : at + width] = tall[fold * rows : (fold + 1) * rows].astype(BF16)
+
+
+def prepare(qkv, out, up, down, *lines):
+    rows, width = out.shape
+    shapes = ((rows, 4 * width + SMALL), (rows, up.shape[1] + down.size // rows))
+    return pl.pallas_call(
+        prepare_body,
+        out_shape=[like(shape, BF16) for shape in shapes],
+        in_specs=[VMEM_SPEC] * 8,
+        out_specs=[VMEM_SPEC] * 2,
+        compiler_params=pltpu.CompilerParams(vmem_limit_bytes=8 * 2**20),
+        cost_estimate=SHORT,
+    )(*in_hbm(qkv, out, up, down, *(v[None] for v in lines)))
+
+
 def small_row(extra, column):
     lane = lax.broadcasted_iota(jnp.int32, (8, extra.shape[1]), 1)
     return dot_nt((lane == column).astype(BF16), extra[...])[0:1, :]
 
 
+def both(begin, end):
+    return jnp.concatenate([begin[...], end[...]], axis=0).astype(F32)
+
+
 def front_body(
-    noisy_ref, tok, far_tok, extra, weight, cos, sin,
+    noisy_ref, tok, far_tok, far_tok_end, extra, weight, cos, sin,
     first_t, far_first_t, q, k, v, kf, vf, first, far_first,
 ):
     width = tok.shape[1]
@@ -377,7 +474,7 @@
 
     @pl.when(is_noisy)
     def _():
-        far_norm, _ = normed(far_tok[...].astype(F32))
+        far_norm, _ = normed(both(far_tok, far_tok_end))
         far_first[...] = (far_norm * g).astype(BF16)
 
     @pl.when(jnp.logical_not(is_noisy))
@@ -408,20 +505,20 @@
     )
 
 
-def front(noisy, tok, far_tok, joint, cos, sin):
+def front(noisy, tok, far_tok, far_tok_end, joint, cos, sin):
     rows, width = tok.shape
     act, table = whole_spec((rows, width)), whole_spec((rows, PAIR))
     extra, qkv, _ = joint_specs(width)
     return pl.pallas_call(
         front_body,
         grid=(1,),
-        out_shape=[like((width, rows), BF16)] * 2 + [like((rows, width), BF16)] * 5,
-        in_specs=[SMEM_SPEC, act, act, extra, qkv, table, table],
+        out_shape=[pltpu.HBM((width, rows), BF16)] * 2 + [pltpu.HBM((rows, width), BF16)] * 5,
+        in_specs=[SMEM_SPEC, act] + [whole_spec((rows // 2, width))] * 2 + [extra, qkv, table, table],
         out_specs=[whole_spec((width, rows))] * 2 + [act] * 5,
         scratch_shapes=[pltpu.VMEM((rows, width), BF16)] * 2,
         compiler_params=pltpu.CompilerParams(vmem_limit_bytes=20 * 2**20),
         cost_estimate=SHORT,
-    )(noisy, tok, far_tok, joint, joint, cos, sin)
+    )(noisy, tok, far_tok, far_tok_end, joint, joint, cos, sin)
 
 
 def window(i, rows):
@@ -534,7 +631,7 @@
         scratch_shapes=mask_scratch(rows),
         compiler_params=pltpu.CompilerParams(vmem_limit_bytes=12 * 2**20),
         cost_estimate=SHORT,
-    )(noisy, lo, hi, code, code_row, q, k, v, kf, vf)
+    )(noisy, *in_hbm(lo, hi, code, code_row, q, k, v, kf, vf))
 
 
 def attend_back_body(
@@ -828,13 +925,13 @@
         + [like((8, width), F32), like((8, hidden // chunk, chunk // 4), F32)],
         compiler_params=pltpu.CompilerParams(vmem_limit_bytes=32 * 2**20),
         cost_estimate=SHORT,
-    )(place_in, tok, o, cot, joint, joint, up_w, down_w, within, which)
+    )(place_in, *in_hbm(tok), o, *in_hbm(cot), joint, joint, up_w, down_w, *in_hbm(within, which))
     n = len(ups)
     return (*outs[:3], outs[3 : 3 + n], outs[3 + n : 3 + 2 * n], outs[-2], outs[-1])
 
 
 def finish_body(
-    noisy_ref, place_ref, tok, far_tok, extra, own, far, gy, o, ga, lines, up_lines,
+    noisy_ref, place_ref, tok, far_tok, far_tok_end, extra, own, far, gy, o, ga, lines, up_lines,
     part, send, *outs
 ):
     width = tok.shape[1]
@@ -861,7 +958,7 @@
     @pl.when(noisy_ref[0] == 1)
     def _():
         part[...] = gy[...] + norm_term(own, norm, inverse, g)
-        far_norm, far_inverse = normed(far_tok[...].astype(F32))
+        far_norm, far_inverse = normed(both(far_tok, far_tok_end))
         send[...] = norm_term(far, far_norm, far_inverse, g).astype(BF16)
         put_lines(jnp.sum(own * norm + far * far_norm, axis=0, keepdims=True))
 
@@ -873,7 +970,7 @@
         put_lines(jnp.sum(both * norm, axis=0, keepdims=True))
 
 
-def finish(noisy, place_in, tok, far_tok, joint, own, far, gy, o, ga, lines, up_lines):
+def finish(noisy, place_in, tok, far_tok, far_tok_end, joint, own, far, gy, o, ga, lines, up_lines):
     rows, width = tok.shape
     act = whole_spec((rows, width))
     extra, _, _ = joint_specs(width)
@@ -881,15 +978,92 @@
     outs = pl.pallas_call(
         finish_body,
         grid=(1,),
-        out_shape=[like((rows, width), F32), like((rows, width), BF16)]
+        out_shape=[like((rows, width), F32)]
+        + [like((rows, width), BF16)]
         + [like(shape, BF16) for shape in shapes],
-        in_specs=[SMEM_SPEC] * 2 + [act, act, extra] + [act] * 5
+        in_specs=[SMEM_SPEC] * 2
+        + [act]
+        + [whole_spec((rows // 2, width))] * 2
+        + [extra]
+        + [act] * 5
         + [whole_spec((8, width)), whole_spec(up_lines.shape)],
         out_specs=[act, act] + [whole_spec(shape) for shape in shapes],
         compiler_params=pltpu.CompilerParams(vmem_limit_bytes=32 * 2**20),
         cost_estimate=SHORT,
-    )(noisy, place_in, tok, far_tok, joint, own, far, gy, o, ga, lines, up_lines)
+    )(noisy, place_in, tok, far_tok, far_tok_end, joint, own, far, gy, o, ga, lines, up_lines)
     return outs[0], outs[1], outs[2:]
+
+
+def last_sum_body(pairs, keep, *refs):
+    got, (qkv, out, small) = refs[:-3], refs[-3:]
+    total = keep[0]
+    for g in got:
+        total = total + g[0].astype(F32)
+    width = out.shape[1]
+    for i in range(pairs):
+        at = 3 * PAIR * i
+        for p in range(3):
+            qkv[:, p * width + i * PAIR : p * width + (i + 1) * PAIR] = total[
+                :, at + p * PAIR : at + (p + 1) * PAIR
+            ]
+    out[...] = total[:, 3 * width : 4 * width]
+    small[...] = total[:, 4 * width :]
+
+
+def last_sum(keep, got, width):
+    rows = keep.shape[1]
+    shapes = ((rows, 3 * width), (rows, width), (rows, SMALL))
+    return pl.pallas_call(
+        partial(last_sum_body, width // PAIR),
+        out_shape=[like(shape, F32) for shape in shapes],
+        in_specs=[VMEM_SPEC] * (1 + len(got)),
+        out_specs=[VMEM_SPEC] * 3,
+        compiler_params=pltpu.CompilerParams(vmem_limit_bytes=8 * 2**20),
+        cost_estimate=SHORT,
+    )(keep, *got)
+
+
+def mlp_sum_body(keep, *refs):
+    got, (up, down) = refs[:-2], refs[-2:]
+    total = keep[0]
+    for g in got:
+        total = total + g[0].astype(F32)
+    rows, hidden = up.shape
+    width = down.shape[1]
+    up[...] = total[:, :hidden]
+    for f in range(down.shape[0] // rows):
+        at = hidden + f * width
+        down[f * rows : (f + 1) * rows, :] = total[:, at : at + width]
+
+
+def mlp_sum(keep, got, hidden, width):
+    _, rows, columns = keep.shape
+    return pl.pallas_call(
+        mlp_sum_body,
+        out_shape=[like((rows, hidden), F32), like(((columns - hidden) // width * rows, width), F32)],
+        in_specs=[VMEM_SPEC] * (1 + len(got)),
+        out_specs=[VMEM_SPEC] * 2,
+        compiler_params=pltpu.CompilerParams(vmem_limit_bytes=8 * 2**20),
+        cost_estimate=LONG,
+    )(keep, *got)
+
+
+def add_body(part, got, out):
+    out[...] = part[...] + got[...].astype(F32)
+
+
+def add(part, got):
+    rows, width = part.shape
+    block = pl.BlockSpec((rows // 4, width), lambda j: (j, 0))
+    return pl.pallas_call(
+        add_body,
+        grid=(4,),
+        out_shape=like((rows, width), F32),
+        in_specs=[block] * 2,
+        out_specs=block,
+        compiler_params=pltpu.CompilerParams(vmem_limit_bytes=8 * 2**20),
+        cost_estimate=LONG,
+    )(part, got)
 
 
 def local(
@@ -913,23 +1087,23 @@
     tok = tokens[0]
     cot = cotangent[0]
 
-    shard_rows = qkv_weight.shape[0]
-    small = [v.reshape(shard_rows, 1) for v in (attn_gain, mlp_gain, down_bias)]
-    small.append(up_bias.reshape(4, shard_rows).T)
-    spare = SMALL - sum(v.shape[1] for v in small)
-    joint = jnp.concatenate([qkv_weight, out_weight] + small + [jnp.zeros((shard_rows, spare), BF16)], axis=1)
+    shard_rows, hidden = up_weight.shape
+    joint, pair_weights = prepare(
+        qkv_weight, out_weight, up_weight, down_weight, attn_gain, mlp_gain, down_bias, up_bias
+    )
     cut = 2 * width
-    j1, jkey = far_gather(joint, [0])
-    far_tok = lax.ppermute(tok, "stream", [(0, 1)])
-    u1, ukey = far_gather(after(up_weight, j1, far_tok), [0])
-    a2, akey = near_gather(after(j1, far_tok)[:, :, :cut], jkey, STREAM_BIT)
-    b2, bkey = near_gather(after(j1, far_tok)[:, :, cut:], jkey, NEAR_BIT)
-    d1, dkey = far_gather(after(down_weight, u1, a2, b2), [0])
-    a2, b2 = after(a2, b2, u1), after(b2, a2, u1)
-    a3, akey = last_gather(a2, akey, NEAR_BIT, d1)
-    b3, bkey = last_gather(b2, bkey, STREAM_BIT, d1)
-    u2, ukey = near_gather(after(u1, d1, a3[1], b3[1]), ukey, NEAR_BIT)
-    d2, dkey = near_gather(after(d1, u1, a3[1], b3[1]), dkey, STREAM_BIT)
+    half = rows // 2
+    far_tok = [lax.ppermute(tok[:half], "stream", [(0, 1)])]
+    far_tok.append(lax.ppermute(after(tok[half:], far_tok[0]), "stream", [(0, 1)]))
+    (a1, b1), jkey = far_gather(joint, (cut, joint.shape[1] - cut), SHORT, far_tok[0])
+    (u1, d1), ukey = far_gather(after(pair_weights, a1), (hidden, hidden), LONG)
+    a2, akey = near_gather(a1, jkey, STREAM_BIT)
+    b2, bkey = near_gather(b1, jkey, NEAR_BIT)
+    a2, b2 = after(a2, far_tok[1]), after(b2, far_tok[1])
+    a3, akey = last_gather(a2, akey, NEAR_BIT, u1, d1)
+    b3, bkey = last_gather(b2, bkey, STREAM_BIT, u1, d1)
+    u1, d1 = after(u1, a3[1], b3[1]), after(d1, a3[1], b3[1])
+    u_got, d_got = flip(u1, NEAR_BIT), flip(d1, STREAM_BIT)
     joint = place([a3, b3], [akey, bkey], me).reshape(width, -1)
 
     doc_ids, positions = doc_layout(lengths[0], rows)
@@ -940,15 +1114,28 @@
     code = lo + positions // BLOCK
     masks = (lo[:, None], (code - stream)[:, None], code[:, None], code[None, :])
 
-    joint = after(joint, u2, d2)
     place_in = jnp.stack([(me[0] // bit) % 2 for bit in (CORE_BIT, NEAR_BIT)] + [me[0] // (2 * NEAR_BIT)])
-    first_t, far_first_t, q, k, v, kf, vf = front(noisy, tok, far_tok, joint, cos, sin)
-    o, lse = attend(noisy, *masks, q, k, v, kf, vf)
-    u3, ukey = last_gather(u2, ukey, STREAM_BIT, o)
-    d3, dkey = last_gather(d2, dkey, NEAR_BIT, o)
-    up_full = place([u3], [ukey], me).reshape(width, -1)
-    down_full = place([d3], [dkey], me).reshape(-1, width)
-    layer_out, gy, ga, dup, ddown, lines, up_lines = mlp(place_in, tok, o, cot, joint, up_full, down_full)
+    first_t, far_first_t, q, k, v, kf, vf = front(noisy, tok, *far_tok, joint, cos, sin)
+    u_got, d_got = after(u_got, q), after(d_got, q)
+    u2, d2 = jnp.concatenate([u1, u_got], axis=0), jnp.concatenate([d1, d_got], axis=0)
+    u_got, d_got = flip(u2, STREAM_BIT), flip(d2, NEAR_BIT)
+    u_core, d_core = flip(u2, CORE_BIT), flip(d2, CORE_BIT)
+    o, lse = attend(noisy, *masks, after(q, u2, d2), k, v, kf, vf)
+    u_got, d_got = after(u_got, o), after(d_got, o)
+    u3 = [u2, u_got, u_core, flip(u_got, CORE_BIT)]
+    d3 = [d2, d_got, d_core, flip(d_got, CORE_BIT)]
+
+    def keys(*bits):
+        out = [ukey]
+        for bit in bits:
+            out = out + [[key ^ bit for key in line] for line in out]
+        return [out[0] + out[1], out[2] + out[3], out[4] + out[5], out[6] + out[7]]
+
+    ukey, dkey = keys(NEAR_BIT, STREAM_BIT, CORE_BIT), keys(STREAM_BIT, NEAR_BIT, CORE_BIT)
+    up_full, down_full = place_pair(u3, ukey, d3, dkey, me)
+    layer_out, gy, ga, dup, ddown, lines, up_lines = mlp(
+        place_in, tok, o, cot, joint, up_full.reshape(width, -1), down_full.reshape(-1, width)
+    )
 
     up_sum, down_sum = Sum(me, dup), Sum(me, ddown)
     split((up_sum, NEAR_BIT), (down_sum, STREAM_BIT))
@@ -973,40 +1160,26 @@
     down_sum.hold(front_sum.got, back_sum.got)
     gy = after(gy, up_sum.send, down_sum.send)
     part, send, outs = finish(
-        noisy, place_in, tok, far_tok, joint, own, far, gy, o, ga, lines, up_lines
+        noisy, place_in, tok, *far_tok, joint, own, far, gy, o, ga, lines, up_lines
     )
     back_sum.add(outs)
-    half = rows // 2
-    received = [lax.ppermute(send[:half], "stream", [(1, 0)])]
     mlp_far = Far([up_sum, down_sum], LONG)
     back_sum.hold(*mlp_far.sends)
     split((front_sum, STREAM_BIT), (back_sum, NEAR_BIT))
     front_sum.flip(STREAM_BIT)
     back_sum.flip(NEAR_BIT)
     mlp_far.flip()
-    back_sum.hold(received[0])
     split((front_sum, NEAR_BIT), (back_sum, STREAM_BIT))
     front_sum.flip(NEAR_BIT)
     back_sum.flip(STREAM_BIT)
-    back_sum.hold(*mlp_far.got)
+    owned_up, owned_down = mlp_sum(mlp_far.keep, mlp_far.got, hidden, width)
+    back_sum.hold(owned_up, owned_down)
+    received = lax.ppermute(after(send, front_sum.send, back_sum.send), "stream", [(1, 0)])
     attn_far = Far([front_sum, back_sum])
-    later = after(send[half:], *attn_far.sends)
-    received.append(lax.ppermute(later, "stream", [(1, 0)]))
-    owned_mlp = mlp_far.result()
-    owned_attn = attn_far.flip().result()
-    grad_input = part + jnp.concatenate(received, axis=0).astype(F32)
-
-    hidden = up_weight.shape[1]
-    owned_up = owned_mlp[:, :hidden]
-    owned_down = owned_mlp[:, hidden:].reshape(shard_rows, -1, width)
-    owned_down = owned_down.transpose(1, 0, 2).reshape(-1, width)
-    owned_front = owned_attn[:, : 3 * PAIR * early]
-    owned_back = owned_attn[:, 3 * PAIR * early :]
-    strips = [owned_front[:, i * PAIR : (i + 1) * PAIR] for i in range(3 * early)]
-    strips += [owned_back[:, i * PAIR : (i + 1) * PAIR] for i in range(3 * (pairs - early))]
-    owned_qkv = jnp.concatenate([s for p in range(3) for s in strips[p::3]], axis=1)
-    owned_out = owned_back[:, 3 * PAIR * (pairs - early) :]
-    owned_small = owned_out[:, width:]
+    attn_far.flip()
+    grad_input = add(part, received)
+    attn_far.got[0] = after(attn_far.got[0], grad_input)
+    owned_qkv, owned_out, owned_small = last_sum(attn_far.keep, attn_far.got, width)
 
     def small_owned(i):
         return owned_small[:, i]
@@ -1016,7 +1189,7 @@
         grad_input[None],
         small_owned(0),
         owned_qkv,
-        owned_out[:, :width],
+        owned_out,
         small_owned(1),
         owned_up,
         owned_small[:, 3:7].T.reshape(-1),

time: 253 us -> 245 us (0.968)
  local copies, waits for them, and re-layouts: 17.1 us -> 4.44 us
  starting transfers between devices: 49.4 us -> 59.8 us
  waiting for transfers between devices: 95.5 us -> 89.1 us
  Pallas kernels: 76.8 us -> 83.1 us
  other arithmetic: 9.61 us -> 4.07 us
    ppermute x44 -> x41, waiting for transfers between devices: 92.3 us -> 78 us  [flip(): lax.ppermute(block, ALL, [(i, i ^ mask) for i in range(device_count())])]
    ppermute x44 -> x41, starting transfers between devices: 41.4 us -> 53 us  [flip(): lax.ppermute(block, ALL, [(i, i ^ mask) for i in range(device_count())])]
    pallas_call x1 -> x8, Pallas kernels: 4.58 us -> 15.8 us  [the longest x1 6.45 us: front(): pl.pallas_call(front_body, grid=(1,), out_shape=[pltpu.HBM((width, rows),...]
    ppermute x3, waiting for transfers between devices: 3.27 us -> 11.1 us  [the longest x1 5.61 us: local(): lax.ppermute(after(tok[half:], far_tok[0]), 'stream', [(0, 1)])]
    pallas_call x3 -> x1, Pallas kernels: 8.06 us -> 2.33 us  [place(): pl.pallas_call(body, out_shape=like(shape, flat[0].dtype), in_specs=[SMEM...]
    unnamed x99 -> x42, local copies, waits for them, and re-layouts: 5.75 us -> 0.83 us
    reshape x6 -> x0, local copies, waits for them, and re-layouts: 3.22 us -> none  [the longest x3 2.24 us: local(): small = [v.reshape(shard_rows, 1) for v in (attn_gain, mlp_gain, down_bias)]]
    concatenate x4 -> x2, local copies, waits for them, and re-layouts: 2.76 us -> 0.08 us  [the longest x1 0.04 us: local(): jnp.concatenate([u1, u_got], axis=0)]
  transfers between devices with their start and end apart: 47 -> 44, of which waited for: 24 -> 22; matrix products, arithmetic and copies ran while one was open for 8% -> 3% of each run, Pallas kernels for 19% -> 20%
where the time goes in v1:
time: 245 us; the launch traced here: 244 us
  waiting for transfers between devices  89.1 us (36%)
  Pallas kernels  83.1 us (34%)
  starting transfers between devices  59.8 us (24%)
  local copies, waits for them, and re-layouts  4.44 us (2%)
  other arithmetic  4.07 us (2%)
  between operations  3.77 us (2%)
    ppermute x41, waiting for transfers between devices, flip(): lax.ppermute(block, ALL, [(i, i ^ mask) for i in range(device_count())])  78 us
    ppermute x41, starting transfers between devices, flip(): lax.ppermute(block, ALL, [(i, i ^ mask) for i in range(device_count())])  53 us
    pallas_call x1, Pallas kernels, mlp(): pl.pallas_call(partial(mlp_body, len(ups)), grid_spec=pltpu.PrefetchScala...  24.1 us
    pallas_call x1, Pallas kernels, attend_back(): pl.pallas_call(partial(attend_back_body, early), grid=(pairs,), out_shape...  21.1 us
    pallas_call x1, Pallas kernels, attend(): pl.pallas_call(attend_body, grid=(width // PAIR,), out_shape=[like((rows,...  12 us
    pallas_call x1, Pallas kernels, front(): pl.pallas_call(front_body, grid=(1,), out_shape=[pltpu.HBM((width, rows),...  6.45 us
    ppermute x1, waiting for transfers between devices, local(): lax.ppermute(after(tok[half:], far_tok[0]), 'stream', [(0, 1)])  5.61 us
  transfers between devices with their start and end apart: 44, of which 22 were waited for; matrix products, arithmetic and copies ran while one was open for 3% of the time, Pallas kernels for 20%

profile of v1, /device:TPU:0, one launch (start us, length us, event | category | flops | bytes accessed | tf_op | source)
XLA Modules:
  0.0 244.2 jit_solution(12232844104011923107)
XLA Ops:
  1.9 5.1 %collective-permute-start.4 = (bf16[1,24,3200]{2,1,0:T(8,128)(2,1)S(1)}, bf16[1,24,3200]{2,1,0:T(8,128)(2,1)S(1)}, u32[]{:S(2)}, u32[]{:S(2)}) collective-permute-start(bf16[1,24,3200]{2,1,0:T(8,128)(2,1)S(1)} %bitcast.68), channel_id=1, source_target_pairs={{0,24},{1,25},{2,26},{3,27},{4,28},{5,29},{6,30},{7,31},{8,16},{9,... | collective-permute-start | bytes 460808 | tf_op jit(solution)/shard_map/ppermute | solution.py:43
  8.8 3.6 %collective-permute-start = (bf16[256,768]{1,0:T(8,128)(2,1)S(1)}, bf16[256,768]{1,0:T(8,128)(2,1)S(1)}, u32[]{:S(2)}, u32[]{:S(2)}) collective-permute-start(bf16[256,768]{1,0:T(8,128)(2,1)S(1)} %get-tuple-element.206), channel_id=1, source_target_pairs={{0,1},{2,3},{4,5},{6,7},{8,9},{10,11},{12,13},{14,15},{16,17},{18,... | collective-permute-start | bytes 1179656 | tf_op jit(solution)/shard_map/ppermute | solution.py:1096
  16.4 3.6 %collective-permute-done.far_tok = bf16[256,768]{1,0:T(8,128)(2,1)S(1)} collective-permute-done((bf16[256,768]{1,0:T(8,128)(2,1)S(1)}, bf16[256,768]{1,0:T(8,128)(2,1)S(1)}, u32[]{:S(2)}, u32[]{:S(2)}) %collective-permute-start) | collective-permute-done | bytes 393248 | tf_op jit(solution)/shard_map/ppermute | solution.py:1096
  25.7 3.5 %collective-permute-start.9 = (bf16[1,24,6144]{2,1,0:T(8,128)(2,1)S(1)}, bf16[1,24,6144]{2,1,0:T(8,128)(2,1)S(1)}, u32[]{:S(2)}, u32[]{:S(2)}) collective-permute-start(bf16[1,24,6144]{2,1,0:T(8,128)(2,1)S(1)} %bitcast.72), channel_id=1, source_target_pairs={{0,24},{1,25},{2,26},{3,27},{4,28},{5,29},{6,30},{7,31},{8,16},{9,... | collective-permute-start | bytes 884744 | tf_op jit(solution)/shard_map/ppermute | solution.py:43
  32.2 5.6 %collective-permute-done.1.far_tok_end = bf16[256,768]{1,0:T(8,128)(2,1)S(1)} collective-permute-done((bf16[256,768]{1,0:T(8,128)(2,1)S(1)}, bf16[256,768]{1,0:T(8,128)(2,1)S(1)}, u32[]{:S(2)}, u32[]{:S(2)}) %collective-permute-start.1) | collective-permute-done | bytes 393248 | tf_op jit(solution)/shard_map/ppermute | solution.py:1097
  41.4 10.8 %collective-permute-done.8.refs_2_ = bf16[1,24,6144]{2,1,0:T(8,128)(2,1)S(1)} collective-permute-done((bf16[1,24,6144]{2,1,0:T(8,128)(2,1)S(1)}, bf16[1,24,6144]{2,1,0:T(8,128)(2,1)S(1)}, u32[]{:S(2)}, u32[]{:S(2)}) %collective-permute-start.8) | collective-permute-done | bytes 294944 | tf_op jit(solution)/shard_map/ppermute | solution.py:43
  61.4 6.5 %shard_map.208 = (bf16[768,512]{1,0:T(8,128)(2,1)}, bf16[768,512]{1,0:T(8,128)(2,1)}, bf16[512,768]{1,0:T(8,128)(2,1)}, bf16[512,768]{1,0:T(8,128)(2,1)}, bf16[5...) custom-call(s32[1]{0:T(128)} %bitcast.4.noisy_ref, bf16[512,768]{1,0:T(8,128)(2,1)S(1)} %bitcast.54, ...), custom_call_target="tpu_custom_call" | custom-call | flops 1 | bytes 1 | tf_op jit(solution)/shard_map/pallas_call | solution.py:512
  67.9 4.7 %collective-permute-done.17 = bf16[4,24,3072]{2,1,0:T(8,128)(2,1)S(1)} collective-permute-done((bf16[4,24,3072]{2,1,0:T(8,128)(2,1)S(1)}, bf16[4,24,3072]{2,1,0:T(8,128)(2,1)S(1)}, u32[]{:S(2)}, u32[]{:S(2)}) %collective-permute-start.17) | collective-permute-done | bytes 589856 | tf_op jit(solution)/shard_map/ppermute | solution.py:43
  78.1 12.0 %shard_map.209 = (bf16[512,768]{1,0:T(8,128)(2,1)S(1)}, f32[48,1024]{1,0:T(8,128)S(1)}) custom-call(s32[1]{0:T(128)} %bitcast.4.noisy_ref, s32[512,1]{1,0:T(8,128)} %copy-done.15, s32[512,1]{1,0:T(8,128)} %get-tuple-element.203.hi, s32[512,1]{1,0:T(8,128)} %get-tuple-element.204.code, s32[1,512]{1,0:T(1,128)} %get-tuple-element.202.code_row, ...), custom_call_target="tpu_custom_call" | custom-call | flops 1 | bytes 1 | tf_op jit(solution)/shard_map/pallas_call | solution.py:625
  90.7 9.4 %collective-permute-done.18.refs_1_ = bf16[8,24,3072]{2,1,0:T(8,128)(2,1)} collective-permute-done((bf16[8,24,3072]{2,1,0:T(8,128)(2,1)S(1)}, bf16[8,24,3072]{2,1,0:T(8,128)(2,1)}, u32[]{:S(2)}, u32[]{:S(2)}) %collective-permute-start.18) | collective-permute-done | bytes 1179680 | tf_op jit(solution)/shard_map/ppermute | solution.py:43
  105.0 4.7 %shard_map.210 = (bf16[32,24,3072]{2,1,0:T(8,128)(2,1)S(1)}, bf16[32,4,24,768]{3,2,1,0:T(8,128)(2,1)S(1)}) custom-call(s32[1]{0:T(128)} %bitcast.15.me_ref, bf16[8,24,3072]{2,1,0:T(8,128)(2,1)S(1)} %constant_dynamic-update-slice_fusion.refs_0_, bf16[8,24,3072]{2,1,0:T(8,128)(2,1)} %collective-permute-done.18.refs_1_, ...), custom_call_target="tpu_custom_call" | custom-call | flops 1 | bytes 1 | tf_op jit(solution)/shard_map/pallas_call | solution.py:99
  109.7 24.1 %shard_map.211 = (bf16[512,768]{1,0:T(8,128)(2,1)}, f32[512,768]{1,0:T(8,128)S(1)}, bf16[512,768]{1,0:T(8,128)(2,1)S(1)}, bf16[2,4,48,3072]{3,2,1,0:T(8,128)(2,1...) custom-call(s32[3]{0:T(128)S(1)} %pad_add_fusion.refs_0_.place_ref, ...), custom_call_target="tpu_custom_call" | custom-call | flops 1 | bytes 1 | tf_op jit(solution)/shard_map/pallas_call | solution.py:903
  134.3 4.0 %collective-permute-done.24 = bf16[2,4,48,3072]{3,2,1,0:T(8,128)(2,1)S(1)} collective-permute-done((bf16[2,4,48,3072]{3,2,1,0:T(8,128)(2,1)S(1)}, bf16[2,4,48,3072]{3,2,1,0:T(8,128)(2,1)S(1)}, u32[]{:S(2)}, u32[]{:S(2)}) %collective-permute-start.24) | collective-permute-done | bytes 2359328 | tf_op jit(solution)/shard_map/ppermute | solution.py:43
  138.4 3.4 %collective-permute-done.25 = bf16[2,4,192,768]{3,2,1,0:T(8,128)(2,1)S(1)} collective-permute-done((bf16[2,4,192,768]{3,2,1,0:T(8,128)(2,1)S(1)}, bf16[2,4,192,768]{3,2,1,0:T(8,128)(2,1)S(1)}, u32[]{:S(2)}, u32[]{:S(2)}) %collective-permute-start.25) | collective-permute-done | bytes 2359328 | tf_op jit(solution)/shard_map/ppermute | solution.py:43
  146.6 21.1 %shard_map.213 = (f32[512,768]{1,0:T(8,128)S(1)}, f32[512,768]{1,0:T(8,128)S(1)}, bf16[2,4,48,1536]{3,2,1,0:T(8,128)(2,1)S(1)}, bf16[2,4,48,1536]{3,2,1,0:T(8,12...) custom-call(s32[1]{0:T(128)} %bitcast.4.noisy_ref, ...), custom_call_target="tpu_custom_call" | custom-call | flops 1 | bytes 1 | tf_op jit(solution)/shard_map/pallas_call | solution.py:751
  167.7 4.1 %collective-permute-done.26.refs_1_ = bf16[1,4,2,24,3072]{4,3,2,1,0:T(8,128)(2,1)S(1)} collective-permute-done((bf16[1,4,2,24,3072]{4,3,2,1,0:T(8,128)(2,1)S(1)}, bf16[1,4,2,24,3072]{4,3,2,1,0:T(8,128)(2,1)S(1)}, u32[]{:S(2)}, u32[]{:S(2)}) %collective-permute-start.26) | collective-permute-done | bytes 1179680 | tf_op jit(solution)/shard_map/ppermute | solution.py:43
  174.9 3.1 %collective-permute-start.30 = (bf16[1,4,1,24,3072]{4,3,2,1,0:T(8,128)(2,1)S(1)}, bf16[1,4,1,24,3072]{4,3,2,1,0:T(8,128)(2,1)S(1)}, u32[]{:S(2)}, u32[]{:S(2)}) collective-permute-start(bf16[1,4,1,24,3072]{4,3,2,1,0:T(8,128)(2,1)S(1)} %get-tuple-element.152), channel_id=1, source_target_pairs={{0,1},{1,0},{2,3},{3,2},{4,5},{5,4},{6,7},{7,6},{8,9},{9,8},{10,11... | collective-permute-start | bytes 1769480 | tf_op jit(solution)/shard_map/ppermute | solution.py:43
  178.1 3.1 %shard_map.215 = (f32[512,768]{1,0:T(8,128)S(1)}, bf16[512,768]{1,0:T(8,128)(2,1)S(1)}, bf16[2,4,48,896]{3,2,1,0:T(8,128)(2,1)S(1)}, bf16[2,4,48,896]{3,2,1,0:T(8,128)(2,1)S(1)}) custom-call(s32[1]{0:T(128)} %bitcast.4.noisy_ref, s32[3]{0:T(128)S(1)} %pad_add_fusion.refs_0_.place_ref, bf16[512,768]{1,0:T(8,128)(2,1)S(1)} %bitcast.55, ...), custom_call_target="tpu_custom_call" | custom-call | flops 1 | bytes 1 | tf_op jit(solution)/shard_map/pallas_call | solution.py:978
  181.3 8.0 %collective-permute-done.31.refs_3_ = bf16[1,4,1,96,768]{4,3,2,1,0:T(8,128)(2,1)S(1)} collective-permute-done((bf16[1,4,1,96,768]{4,3,2,1,0:T(8,128)(2,1)S(1)}, bf16[1,4,1,96,768]{4,3,2,1,0:T(8,128)(2,1)S(1)}, u32[]{:S(2)}, u32[]{:S(2)}) %collective-permute-start.31) | collective-permute-done | bytes 589856 | tf_op jit(solution)/shard_map/ppermute | solution.py:43
  195.6 5.7 %collective-permute-start.38 = (bf16[1,24,6144]{2,1,0:T(8,128)(2,1)S(1)}, bf16[1,24,6144]{2,1,0:T(8,128)(2,1)S(1)}, u32[]{:S(2)}, u32[]{:S(2)}) collective-permute-start(bf16[1,24,6144]{2,1,0:T(8,128)(2,1)S(1)} %get-tuple-element.169), channel_id=1, source_target_pairs={{0,8},{1,9},{2,10},{3,11},{4,12},{5,13},{6,14},{7,15},{8,0},{9,1},... | collective-permute-start | bytes 884744 | tf_op jit(solution)/shard_map/ppermute | solution.py:43
  203.7 4.4 %collective-permute-done.33.refs_1_ = bf16[2,4,1,24,1536]{4,3,2,1,0:T(8,128)(2,1)S(1)} collective-permute-done((bf16[2,4,1,24,1536]{4,3,2,1,0:T(8,128)(2,1)S(1)}, bf16[2,4,1,24,1536]{4,3,2,1,0:T(8,128)(2,1)S(1)}, u32[]{:S(2)}, u32[]{:S(2)}) %collective-permute-start.33) | collective-permute-done | bytes 589856 | tf_op jit(solution)/shard_map/ppermute | solution.py:43
  212.6 11.5 %collective-permute-done.39.refs_1_ = bf16[1,24,6144]{2,1,0:T(8,128)(2,1)S(1)} collective-permute-done((bf16[1,24,6144]{2,1,0:T(8,128)(2,1)S(1)}, bf16[1,24,6144]{2,1,0:T(8,128)(2,1)S(1)}, u32[]{:S(2)}, u32[]{:S(2)}) %collective-permute-start.39) | collective-permute-done | bytes 294944 | tf_op jit(solution)/shard_map/ppermute | solution.py:43
  225.1 4.8 %collective-permute-start.41 = (bf16[1,24,3200]{2,1,0:T(8,128)(2,1)S(1)}, bf16[1,24,3200]{2,1,0:T(8,128)(2,1)S(1)}, u32[]{:S(2)}, u32[]{:S(2)}) collective-permute-start(bf16[1,24,3200]{2,1,0:T(8,128)(2,1)S(1)} %get-tuple-element.189), channel_id=1, source_target_pairs={{0,8},{1,9},{2,10},{3,11},{4,12},{5,13},{6,14},{7,15},{8,0},{9,1},... | collective-permute-start | bytes 460808 | tf_op jit(solution)/shard_map/ppermute | solution.py:43
  236.2 5.8 %collective-permute-done.42.refs_1_ = bf16[1,24,3200]{2,1,0:T(8,128)(2,1)S(1)} collective-permute-done((bf16[1,24,3200]{2,1,0:T(8,128)(2,1)S(1)}, bf16[1,24,3200]{2,1,0:T(8,128)(2,1)S(1)}, u32[]{:S(2)}, u32[]{:S(2)}) %collective-permute-start.42) | collective-permute-done | bytes 153632 | tf_op jit(solution)/shard_map/ppermute | solution.py:43
  (148 shorter events, 68.1 us)
Async XLA Ops:
  1.9 14.6 %collective-permute-start.4 = (bf16[1,24,3200]{2,1,0:T(8,128)(2,1)S(1)}, bf16[1,24,3200]{2,1,0:T(8,128)(2,1)S(1)}, u32[]{:S(2)}, u32[]{:S(2)}) collective-permute-start(bf16[1,24,3200]{2,1,0:T(8,128)(2,1)S(1)} %bitcast.68), channel_id=1, source_target_pairs={{0,24},{1,25},{2,26},{3,27},{4,28},{5,29},{6,30},{7,31},{8,16},{9,... | collective-permute-start | bytes 460808 | tf_op jit(solution)/shard_map/ppermute | solution.py:43
  29.2 23.0 %collective-permute-start.8 = (bf16[1,24,6144]{2,1,0:T(8,128)(2,1)S(1)}, bf16[1,24,6144]{2,1,0:T(8,128)(2,1)S(1)}, u32[]{:S(2)}, u32[]{:S(2)}) collective-permute-start(bf16[1,24,6144]{2,1,0:T(8,128)(2,1)S(1)} %bitcast.73), channel_id=1, source_target_pairs={{0,16},{1,17},{2,18},{3,19},{4,20},{5,21},{6,22},{7,23},{8,24},{9,... | collective-permute-start | bytes 884744 | tf_op jit(solution)/shard_map/ppermute | solution.py:43
  29.2 23.0 %collective-permute-start.7 = (bf16[1,24,6144]{2,1,0:T(8,128)(2,1)S(1)}, bf16[1,24,6144]{2,1,0:T(8,128)(2,1)S(1)}, u32[]{:S(2)}, u32[]{:S(2)}) collective-permute-start(bf16[1,24,6144]{2,1,0:T(8,128)(2,1)S(1)} %bitcast.74), channel_id=1, source_target_pairs={{0,8},{1,9},{2,10},{3,11},{4,12},{5,13},{6,14},{7,15},{8,0},{9,1},... | collective-permute-start | bytes 884744 | tf_op jit(solution)/shard_map/ppermute | solution.py:43
  37.8 19.3 %collective-permute-start.10 = (bf16[8,24,1536]{2,1,0:T(8,128)(2,1)S(1)}, bf16[8,24,1536]{2,1,0:T(8,128)(2,1)S(1)}, u32[]{:S(2)}, u32[]{:S(2)}) collective-permute-start(bf16[8,24,1536]{2,1,0:T(8,128)(2,1)S(1)} %pad_maximum_fusion.1.refs_0_), channel_id=1, source_target_pairs={{0,2},{1,3},{2,0},{3,1},{4,6},{5,7},{6,4},{7,5},{8,10},{9,11},{10,... | collective-permute-start | bytes 1769480 | tf_op jit(solution)/shard_map/ppermute | solution.py:43
  37.9 15.7 %collective-permute-start.6 = (bf16[8,24,1536]{2,1,0:T(8,128)(2,1)S(1)}, bf16[8,24,1536]{2,1,0:T(8,128)(2,1)S(1)}, u32[]{:S(2)}, u32[]{:S(2)}) collective-permute-start(bf16[8,24,1536]{2,1,0:T(8,128)(2,1)S(1)} %pad_maximum_fusion.1.refs_0_), channel_id=1, source_target_pairs={{0,4},{1,5},{2,6},{3,7},{4,0},{5,1},{6,2},{7,3},{8,12},{9,13},{10,... | collective-permute-start | bytes 1769480 | tf_op jit(solution)/shard_map/ppermute | solution.py:43
  39.0 17.3 %collective-permute-start.13 = (bf16[8,24,1664]{2,1,0:T(8,128)(2,1)S(1)}, bf16[8,24,1664]{2,1,0:T(8,128)(2,1)S(1)}, u32[]{:S(2)}, u32[]{:S(2)}) collective-permute-start(bf16[8,24,1664]{2,1,0:T(8,128)(2,1)S(1)} %pad_maximum_fusion.refs_4_), channel_id=1, source_target_pairs={{0,1},{1,0},{2,3},{3,2},{4,5},{5,4},{6,7},{7,6},{8,9},{9,8},{10,11... | collective-permute-start | bytes 1916936 | tf_op jit(solution)/shard_map/ppermute | solution.py:43
  56.2 16.4 %collective-permute-start.16 = (bf16[4,24,3072]{2,1,0:T(8,128)(2,1)S(1)}, bf16[4,24,3072]{2,1,0:T(8,128)(2,1)S(1)}, u32[]{:S(2)}, u32[]{:S(2)}) collective-permute-start(bf16[4,24,3072]{2,1,0:T(8,128)(2,1)S(1)} %get-tuple-element.117), channel_id=1, source_target_pairs={{0,4},{1,5},{2,6},{3,7},{4,0},{5,1},{6,2},{7,3},{8,12},{9,13},{10,... | collective-permute-start | bytes 1769480 | tf_op jit(solution)/shard_map/ppermute | solution.py:43
  57.1 15.5 %collective-permute-start.17 = (bf16[4,24,3072]{2,1,0:T(8,128)(2,1)S(1)}, bf16[4,24,3072]{2,1,0:T(8,128)(2,1)S(1)}, u32[]{:S(2)}, u32[]{:S(2)}) collective-permute-start(bf16[4,24,3072]{2,1,0:T(8,128)(2,1)S(1)} %get-tuple-element.119), channel_id=1, source_target_pairs={{0,1},{1,0},{2,3},{3,2},{4,5},{5,4},{6,7},{7,6},{8,9},{9,8},{10,11... | collective-permute-start | bytes 1769480 | tf_op jit(solution)/shard_map/ppermute | solution.py:43
  72.7 27.5 %collective-permute-start.18 = (bf16[8,24,3072]{2,1,0:T(8,128)(2,1)S(1)}, bf16[8,24,3072]{2,1,0:T(8,128)(2,1)}, u32[]{:S(2)}, u32[]{:S(2)}) collective-permute-start(bf16[8,24,3072]{2,1,0:T(8,128)(2,1)S(1)} %constant_dynamic-update-slice_fusion.refs_0_), channel_id=1, source_target_pairs={{0,1},{1,0},{2,3},{3,2},{4,5},{5,4},{6,7},{7,6},{8,9},{9,8},{10,11... | collective-permute-start | bytes 3538952 | tf_op jit(solution)/shard_map/ppermute | solution.py:43
  74.5 27.2 %collective-permute-start.21 = (bf16[8,24,3072]{2,1,0:T(8,128)(2,1)S(1)}, bf16[8,24,3072]{2,1,0:T(8,128)(2,1)}, u32[]{:S(2)}, u32[]{:S(2)}) collective-permute-start(bf16[8,24,3072]{2,1,0:T(8,128)(2,1)S(1)} %constant_dynamic-update-slice_fusion.2.refs_4_), channel_id=1, source_target_pairs={{0,4},{1,5},{2,6},{3,7},{4,0},{5,1},{6,2},{7,3},{8,12},{9,13},{10,... | collective-permute-start | bytes 3538952 | tf_op jit(solution)/shard_map/ppermute | solution.py:43
  77.6 24.2 %collective-permute-start.19 = (bf16[8,24,3072]{2,1,0:T(8,128)(2,1)S(1)}, bf16[8,24,3072]{2,1,0:T(8,128)(2,1)}, u32[]{:S(2)}, u32[]{:S(2)}) collective-permute-start(bf16[8,24,3072]{2,1,0:T(8,128)(2,1)S(1)} %constant_dynamic-update-slice_fusion.refs_0_), channel_id=1, source_target_pairs={{0,2},{1,3},{2,0},{3,1},{4,6},{5,7},{6,4},{7,5},{8,10},{9,11},{10,... | collective-permute-start | bytes 3538952 | tf_op jit(solution)/shard_map/ppermute | solution.py:43
  77.6 24.2 %collective-permute-start.22 = (bf16[8,24,3072]{2,1,0:T(8,128)(2,1)S(1)}, bf16[8,24,3072]{2,1,0:T(8,128)(2,1)}, u32[]{:S(2)}, u32[]{:S(2)}) collective-permute-start(bf16[8,24,3072]{2,1,0:T(8,128)(2,1)S(1)} %constant_dynamic-update-slice_fusion.2.refs_4_), channel_id=1, source_target_pairs={{0,2},{1,3},{2,0},{3,1},{4,6},{5,7},{6,4},{7,5},{8,10},{9,11},{10,... | collective-permute-start | bytes 3538952 | tf_op jit(solution)/shard_map/ppermute | solution.py:43
  143.7 28.1 %collective-permute-start.26 = (bf16[1,4,2,24,3072]{4,3,2,1,0:T(8,128)(2,1)S(1)}, bf16[1,4,2,24,3072]{4,3,2,1,0:T(8,128)(2,1)S(1)}, u32[]{:S(2)}, u32[]{:S(2)}) collective-permute-start(bf16[1,4,2,24,3072]{4,3,2,1,0:T(8,128)(2,1)S(1)} %get-tuple-element.138), channel_id=1, source_target_pairs={{0,4},{1,5},{2,6},{3,7},{4,0},{5,1},{6,2},{7,3},{8,12},{9,13},{10,... | collective-permute-start | bytes 3538952 | tf_op jit(solution)/shard_map/ppermute | solution.py:43
  144.9 27.7 %collective-permute-start.27 = (bf16[2,4,1,96,768]{4,3,2,1,0:T(8,128)(2,1)S(1)}, bf16[2,4,1,96,768]{4,3,2,1,0:T(8,128)(2,1)S(1)}, u32[]{:S(2)}, u32[]{:S(2)}) collective-permute-start(bf16[2,4,1,96,768]{4,3,2,1,0:T(8,128)(2,1)S(1)} %get-tuple-element.139), channel_id=1, source_target_pairs={{0,1},{1,0},{2,3},{3,2},{4,5},{5,4},{6,7},{7,6},{8,9},{9,8},{10,11... | collective-permute-start | bytes 3538952 | tf_op jit(solution)/shard_map/ppermute | solution.py:43
  173.4 15.9 %collective-permute-start.28 = (bf16[2,4,48,1536]{3,2,1,0:T(8,128)(2,1)S(1)}, bf16[2,4,48,1536]{3,2,1,0:T(8,128)(2,1)S(1)}, u32[]{:S(2)}, u32[]{:S(2)}) collective-permute-start(bf16[2,4,48,1536]{3,2,1,0:T(8,128)(2,1)S(1)} %get-tuple-element.160), channel_id=1, source_target_pairs={{0,2},{1,3},{2,0},{3,1},{4,6},{5,7},{6,4},{7,5},{8,10},{9,11},{10,... | collective-permute-start | bytes 3538952 | tf_op jit(solution)/shard_map/ppermute | solution.py:43
  174.0 15.3 %collective-permute-start.31 = (bf16[1,4,1,96,768]{4,3,2,1,0:T(8,128)(2,1)S(1)}, bf16[1,4,1,96,768]{4,3,2,1,0:T(8,128)(2,1)S(1)}, u32[]{:S(2)}, u32[]{:S(2)}) collective-permute-start(bf16[1,4,1,96,768]{4,3,2,1,0:T(8,128)(2,1)S(1)} %get-tuple-element.153), channel_id=1, source_target_pairs={{0,4},{1,5},{2,6},{3,7},{4,0},{5,1},{6,2},{7,3},{8,12},{9,13},{10,... | collective-permute-start | bytes 1769480 | tf_op jit(solution)/shard_map/ppermute | solution.py:43
  174.9 16.4 %collective-permute-start.30 = (bf16[1,4,1,24,3072]{4,3,2,1,0:T(8,128)(2,1)S(1)}, bf16[1,4,1,24,3072]{4,3,2,1,0:T(8,128)(2,1)S(1)}, u32[]{:S(2)}, u32[]{:S(2)}) collective-permute-start(bf16[1,4,1,24,3072]{4,3,2,1,0:T(8,128)(2,1)S(1)} %get-tuple-element.152), channel_id=1, source_target_pairs={{0,1},{1,0},{2,3},{3,2},{4,5},{5,4},{6,7},{7,6},{8,9},{9,8},{10,11... | collective-permute-start | bytes 1769480 | tf_op jit(solution)/shard_map/ppermute | solution.py:43
  192.7 15.6 %collective-permute-start.34 = (bf16[1,4,2,24,1664]{4,3,2,1,0:T(8,128)(2,1)S(1)}, bf16[1,4,2,24,1664]{4,3,2,1,0:T(8,128)(2,1)S(1)}, u32[]{:S(2)}, u32[]{:S(2)}) collective-permute-start(bf16[1,4,2,24,1664]{4,3,2,1,0:T(8,128)(2,1)S(1)} %get-tuple-element.178), channel_id=1, source_target_pairs={{0,4},{1,5},{2,6},{3,7},{4,0},{5,1},{6,2},{7,3},{8,12},{9,13},{10,... | collective-permute-start | bytes 1916936 | tf_op jit(solution)/shard_map/ppermute | solution.py:43
  195.6 15.7 %collective-permute-start.38 = (bf16[1,24,6144]{2,1,0:T(8,128)(2,1)S(1)}, bf16[1,24,6144]{2,1,0:T(8,128)(2,1)S(1)}, u32[]{:S(2)}, u32[]{:S(2)}) collective-permute-start(bf16[1,24,6144]{2,1,0:T(8,128)(2,1)S(1)} %get-tuple-element.169), channel_id=1, source_target_pairs={{0,8},{1,9},{2,10},{3,11},{4,12},{5,13},{6,14},{7,15},{8,0},{9,1},... | collective-permute-start | bytes 884744 | tf_op jit(solution)/shard_map/ppermute | solution.py:43
  201.3 22.8 %collective-permute-start.39 = (bf16[1,24,6144]{2,1,0:T(8,128)(2,1)S(1)}, bf16[1,24,6144]{2,1,0:T(8,128)(2,1)S(1)}, u32[]{:S(2)}, u32[]{:S(2)}) collective-permute-start(bf16[1,24,6144]{2,1,0:T(8,128)(2,1)S(1)} %get-tuple-element.170), channel_id=1, source_target_pairs={{0,16},{1,17},{2,18},{3,19},{4,20},{5,21},{6,22},{7,23},{8,24},{9,... | collective-permute-start | bytes 884744 | tf_op jit(solution)/shard_map/ppermute | solution.py:43
  201.3 22.8 %collective-permute-start.40 = (bf16[1,24,6144]{2,1,0:T(8,128)(2,1)S(1)}, bf16[1,24,6144]{2,1,0:T(8,128)(2,1)S(1)}, u32[]{:S(2)}, u32[]{:S(2)}) collective-permute-start(bf16[1,24,6144]{2,1,0:T(8,128)(2,1)S(1)} %get-tuple-element.171), channel_id=1, source_target_pairs={{0,24},{1,25},{2,26},{3,27},{4,28},{5,29},{6,30},{7,31},{8,16},{9,... | collective-permute-start | bytes 884744 | tf_op jit(solution)/shard_map/ppermute | solution.py:43
  208.7 16.2 %collective-permute-start.36 = (bf16[1,4,1,24,1536]{4,3,2,1,0:T(8,128)(2,1)S(1)}, bf16[1,4,1,24,1536]{4,3,2,1,0:T(8,128)(2,1)S(1)}, u32[]{:S(2)}, u32[]{:S(2)}) collective-permute-start(bf16[1,4,1,24,1536]{4,3,2,1,0:T(8,128)(2,1)S(1)} %get-tuple-element.179), channel_id=1, source_target_pairs={{0,4},{1,5},{2,6},{3,7},{4,0},{5,1},{6,2},{7,3},{8,12},{9,13},{10,... | collective-permute-start | bytes 884744 | tf_op jit(solution)/shard_map/ppermute | solution.py:43
  209.9 15.1 %collective-permute-start.37 = (bf16[1,4,1,24,1664]{4,3,2,1,0:T(8,128)(2,1)S(1)}, bf16[1,4,1,24,1664]{4,3,2,1,0:T(8,128)(2,1)S(1)}, u32[]{:S(2)}, u32[]{:S(2)}) collective-permute-start(bf16[1,4,1,24,1664]{4,3,2,1,0:T(8,128)(2,1)S(1)} %get-tuple-element.180), channel_id=1, source_target_pairs={{0,1},{1,0},{2,3},{3,2},{4,5},{5,4},{6,7},{7,6},{8,9},{9,8},{10,11... | collective-permute-start | bytes 958472 | tf_op jit(solution)/shard_map/ppermute | solution.py:43
  211.3 22.9 %collective-permute-start.35 = (bf16[512,768]{1,0:T(8,128)(2,1)S(1)}, bf16[512,768]{1,0:T(8,128)(2,1)S(1)}, u32[]{:S(2)}, u32[]{:S(2)}) collective-permute-start(bf16[512,768]{1,0:T(8,128)(2,1)S(1)} %get-tuple-element.181), channel_id=1, source_target_pairs={{1,0},{3,2},{5,4},{7,6},{9,8},{11,10},{13,12},{15,14},{17,16},{19,... | collective-permute-start | bytes 2359304 | tf_op jit(solution)/shard_map/ppermute | solution.py:1177
  (40 other events, 438.2 us)

commit v2 on v1

--- a/solution.py
+++ b/solution.py
@@ -158,7 +158,7 @@
     if others:
         got = after(got, *others)
     pieces, keys = [piece, got], [key, [k ^ bit for k in key]]
-    pieces = pieces + [flip(p, CORE_BIT) for p in pieces]
+    pieces = pieces + [flip(after(piece, *others), CORE_BIT), flip(got, CORE_BIT)]
     return pieces, keys + [[k ^ CORE_BIT for k in key] for key in keys]
 
 
@@ -668,21 +668,25 @@
             )
             log_sum = lse[0:1, 2 * TILE * i : 2 * TILE * (i + 1)]
 
-            def one(keys, values, bias, acc_keys, acc_values, where):
-                s = dot_nt(keys, q2) * (SCORE_SCALE * LOG2_E) + beside(bias)
-                p = jnp.exp2(s - log_sum)
-                gp = dot_nt(values, go2)
-                ds = (p * (gp - delta)).astype(BF16)
-                acc_keys[where, :] += dot(ds, q2)
-                acc_values[where, :] += dot(p.astype(BF16), go2)
-                return dot_tn(keys, ds)
-
             w = far_width(i, rows, noisy)
-            gq = one(kf[:w, :], vf[:w, :], far_bias[:w, r], acc_kf, acc_vf, slice(0, w))
+            keys, values, bias = kf[:w, :], vf[:w, :], far_bias[:w, r]
             if noisy:
                 start, size = window(i, rows)
                 n = slice(start, start + size)
-                gq = gq + one(k[n, :], v[n, :], near_bias[i], acc_k, acc_v, n)
+                keys = jnp.concatenate([keys, k[n, :]], axis=0)
+                values = jnp.concatenate([values, v[n, :]], axis=0)
+                bias = jnp.concatenate([bias, near_bias[i]], axis=0)
+            s = dot_nt(keys, q2) * (SCORE_SCALE * LOG2_E) + beside(bias)
+            p = jnp.exp2(s - log_sum)
+            gp = dot_nt(values, go2)
+            ds = (p * (gp - delta)).astype(BF16)
+            g_keys, g_values = dot(ds, q2), dot(p.astype(BF16), go2)
+            acc_kf[:w, :] += g_keys[:w]
+            acc_vf[:w, :] += g_values[:w]
+            if noisy:
+                acc_k[n, :] += g_keys[w:]
+                acc_v[n, :] += g_values[w:]
+            gq = dot_tn(keys, ds)
             parts.append(unstack_heads(gq.T))
         dq = turn_back(jnp.concatenate(parts, axis=0) * SCORE_SCALE)
         dkf = turn_back(acc_kf[...] * SCORE_SCALE)
@@ -1096,10 +1100,9 @@
     far_tok = [lax.ppermute(tok[:half], "stream", [(0, 1)])]
     far_tok.append(lax.ppermute(after(tok[half:], far_tok[0]), "stream", [(0, 1)]))
     (a1, b1), jkey = far_gather(joint, (cut, joint.shape[1] - cut), SHORT, far_tok[0])
-    (u1, d1), ukey = far_gather(after(pair_weights, a1), (hidden, hidden), LONG)
+    (u1, d1), ukey = far_gather(after(pair_weights, a1), (hidden, hidden), LONG, far_tok[1])
     a2, akey = near_gather(a1, jkey, STREAM_BIT)
     b2, bkey = near_gather(b1, jkey, NEAR_BIT)
-    a2, b2 = after(a2, far_tok[1]), after(b2, far_tok[1])
     a3, akey = last_gather(a2, akey, NEAR_BIT, u1, d1)
     b3, bkey = last_gather(b2, bkey, STREAM_BIT, u1, d1)
     u1, d1 = after(u1, a3[1], b3[1]), after(d1, a3[1], b3[1])

time: 245 us -> 238 us (0.971)
  starting transfers between devices: 59.8 us -> 54.4 us
    ppermute x41, starting transfers between devices: 53 us -> 45.6 us  [flip(): lax.ppermute(block, ALL, [(i, i ^ mask) for i in range(device_count())])]
    ppermute x41, waiting for transfers between devices: 78 us -> 72 us  [flip(): lax.ppermute(block, ALL, [(i, i ^ mask) for i in range(device_count())])]
    ppermute x1, waiting for transfers between devices: 1.91 us -> 4.91 us  [local(): lax.ppermute(after(send, front_sum.send, back_sum.send), 'stream', [(1, 0)])]
  transfers between devices with their start and end apart: 44 -> 44, of which waited for: 22 -> 21; matrix products, arithmetic and copies ran while one was open for 3% -> 3% of each run, Pallas kernels for 20% -> 20%
where the time goes in v2:
time: 238 us
  waiting for transfers between devices  88.2 us (37%)
  Pallas kernels  83.1 us (35%)
  starting transfers between devices  54.4 us (23%)
  local copies, waits for them, and re-layouts  4.54 us (2%)
  other arithmetic  3.96 us (2%)
  between operations  3.78 us (2%)
    ppermute x41, waiting for transfers between devices, flip(): lax.ppermute(block, ALL, [(i, i ^ mask) for i in range(device_count())])  72 us
    ppermute x41, starting transfers between devices, flip(): lax.ppermute(block, ALL, [(i, i ^ mask) for i in range(device_count())])  45.6 us
    pallas_call x1, Pallas kernels, mlp(): pl.pallas_call(partial(mlp_body, len(ups)), grid_spec=pltpu.PrefetchScala...  24.1 us
    pallas_call x1, Pallas kernels, attend_back(): pl.pallas_call(partial(attend_back_body, early), grid=(pairs,), out_shape...  21.1 us
    pallas_call x1, Pallas kernels, attend(): pl.pallas_call(attend_body, grid=(width // PAIR,), out_shape=[like((rows,...  12 us
    ppermute x1, waiting for transfers between devices, local(): lax.ppermute(after(tok[half:], far_tok[0]), 'stream', [(0, 1)])  7.77 us
    pallas_call x1, Pallas kernels, front(): pl.pallas_call(front_body, grid=(1,), out_shape=[pltpu.HBM((width, rows),...  6.46 us
    ppermute x1, waiting for transfers between devices, local(): lax.ppermute(after(send, front_sum.send, back_sum.send), 'stream', [(1, 0)])  4.91 us
  transfers between devices with their start and end apart: 44, of which 21 were waited for; matrix products, arithmetic and copies ran while one was open for 3% of the time, Pallas kernels for 20%

profile of v2, /device:TPU:0, one launch (start us, length us, event | category | flops | bytes accessed | tf_op | source)
XLA Modules:
  0.0 237.9 jit_solution(193830036372329864)
XLA Ops:
  1.9 5.1 %collective-permute-start.4 = (bf16[1,24,3200]{2,1,0:T(8,128)(2,1)S(1)}, bf16[1,24,3200]{2,1,0:T(8,128)(2,1)S(1)}, u32[]{:S(2)}, u32[]{:S(2)}) collective-permute-start(bf16[1,24,3200]{2,1,0:T(8,128)(2,1)S(1)} %bitcast.68), channel_id=1, source_target_pairs={{0,24},{1,25},{2,26},{3,27},{4,28},{5,29},{6,30},{7,31},{8,16},{9,... | collective-permute-start | bytes 460808 | tf_op jit(solution)/shard_map/ppermute | solution.py:43
  8.8 3.6 %collective-permute-start = (bf16[256,768]{1,0:T(8,128)(2,1)S(1)}, bf16[256,768]{1,0:T(8,128)(2,1)S(1)}, u32[]{:S(2)}, u32[]{:S(2)}) collective-permute-start(bf16[256,768]{1,0:T(8,128)(2,1)S(1)} %get-tuple-element.208), channel_id=1, source_target_pairs={{0,1},{2,3},{4,5},{6,7},{8,9},{10,11},{12,13},{14,15},{16,17},{18,... | collective-permute-start | bytes 1179656 | tf_op jit(solution)/shard_map/ppermute | solution.py:1100
  16.4 3.6 %collective-permute-done.far_tok = bf16[256,768]{1,0:T(8,128)(2,1)S(1)} collective-permute-done((bf16[256,768]{1,0:T(8,128)(2,1)S(1)}, bf16[256,768]{1,0:T(8,128)(2,1)S(1)}, u32[]{:S(2)}, u32[]{:S(2)}) %collective-permute-start) | collective-permute-done | bytes 393248 | tf_op jit(solution)/shard_map/ppermute | solution.py:1100
  20.0 3.5 %collective-permute-start.9 = (bf16[1,24,6144]{2,1,0:T(8,128)(2,1)S(1)}, bf16[1,24,6144]{2,1,0:T(8,128)(2,1)S(1)}, u32[]{:S(2)}, u32[]{:S(2)}) collective-permute-start(bf16[1,24,6144]{2,1,0:T(8,128)(2,1)S(1)} %bitcast.72), channel_id=1, source_target_pairs={{0,24},{1,25},{2,26},{3,27},{4,28},{5,29},{6,30},{7,31},{8,16},{9,... | collective-permute-start | bytes 884744 | tf_op jit(solution)/shard_map/ppermute | solution.py:43
  28.6 3.1 %collective-permute-done.5 = bf16[4,24,1536]{2,1,0:T(8,128)(2,1)S(1)} collective-permute-done((bf16[4,24,1536]{2,1,0:T(8,128)(2,1)S(1)}, bf16[4,24,1536]{2,1,0:T(8,128)(2,1)S(1)}, u32[]{:S(2)}, u32[]{:S(2)}) %collective-permute-start.5) | collective-permute-done | bytes 294944 | tf_op jit(solution)/shard_map/ppermute | solution.py:43
  31.7 3.9 %collective-permute-start.1 = (bf16[256,768]{1,0:T(8,128)(2,1)S(1)}, bf16[256,768]{1,0:T(8,128)(2,1)S(1)}, u32[]{:S(2)}, u32[]{:S(2)}) collective-permute-start(bf16[256,768]{1,0:T(8,128)(2,1)S(1)} %get-tuple-element.104), channel_id=1, source_target_pairs={{0,1},{2,3},{4,5},{6,7},{8,9},{10,11},{12,13},{14,15},{16,17},{18,... | collective-permute-start | bytes 1179656 | tf_op jit(solution)/shard_map/ppermute | solution.py:1101
  37.4 7.8 %collective-permute-done.1.far_tok_end = bf16[256,768]{1,0:T(8,128)(2,1)S(1)} collective-permute-done((bf16[256,768]{1,0:T(8,128)(2,1)S(1)}, bf16[256,768]{1,0:T(8,128)(2,1)S(1)}, u32[]{:S(2)}, u32[]{:S(2)}) %collective-permute-start.1) | collective-permute-done | bytes 393248 | tf_op jit(solution)/shard_map/ppermute | solution.py:1101
  49.5 4.9 %collective-permute-done.13.refs_5_ = bf16[8,24,1664]{2,1,0:T(8,128)(2,1)S(1)} collective-permute-done((bf16[8,24,1664]{2,1,0:T(8,128)(2,1)S(1)}, bf16[8,24,1664]{2,1,0:T(8,128)(2,1)S(1)}, u32[]{:S(2)}, u32[]{:S(2)}) %collective-permute-start.13) | collective-permute-done | bytes 639008 | tf_op jit(solution)/shard_map/ppermute | solution.py:43
  60.9 6.5 %shard_map.208 = (bf16[768,512]{1,0:T(8,128)(2,1)}, bf16[768,512]{1,0:T(8,128)(2,1)}, bf16[512,768]{1,0:T(8,128)(2,1)}, bf16[512,768]{1,0:T(8,128)(2,1)}, bf16[5...) custom-call(s32[1]{0:T(128)} %bitcast.4.noisy_ref, bf16[512,768]{1,0:T(8,128)(2,1)S(1)} %bitcast.54, ...), custom_call_target="tpu_custom_call" | custom-call | flops 1 | bytes 1 | tf_op jit(solution)/shard_map/pallas_call | solution.py:512
  67.4 4.7 %collective-permute-done.17 = bf16[4,24,3072]{2,1,0:T(8,128)(2,1)S(1)} collective-permute-done((bf16[4,24,3072]{2,1,0:T(8,128)(2,1)S(1)}, bf16[4,24,3072]{2,1,0:T(8,128)(2,1)S(1)}, u32[]{:S(2)}, u32[]{:S(2)}) %collective-permute-start.17) | collective-permute-done | bytes 589856 | tf_op jit(solution)/shard_map/ppermute | solution.py:43
  77.0 12.0 %shard_map.209 = (bf16[512,768]{1,0:T(8,128)(2,1)S(1)}, f32[48,1024]{1,0:T(8,128)S(1)}) custom-call(s32[1]{0:T(128)} %bitcast.4.noisy_ref, s32[512,1]{1,0:T(8,128)} %copy-done.15, s32[512,1]{1,0:T(8,128)} %get-tuple-element.205.hi, s32[512,1]{1,0:T(8,128)} %get-tuple-element.206.code, s32[1,512]{1,0:T(1,128)} %get-tuple-element.204.code_row, ...), custom_call_target="tpu_custom_call" | custom-call | flops 1 | bytes 1 | tf_op jit(solution)/shard_map/pallas_call | solution.py:625
  89.6 10.3 %collective-permute-done.18.refs_1_ = bf16[8,24,3072]{2,1,0:T(8,128)(2,1)} collective-permute-done((bf16[8,24,3072]{2,1,0:T(8,128)(2,1)S(1)}, bf16[8,24,3072]{2,1,0:T(8,128)(2,1)}, u32[]{:S(2)}, u32[]{:S(2)}) %collective-permute-start.18) | collective-permute-done | bytes 1179680 | tf_op jit(solution)/shard_map/ppermute | solution.py:43
  104.8 4.7 %shard_map.210 = (bf16[32,24,3072]{2,1,0:T(8,128)(2,1)S(1)}, bf16[32,4,24,768]{3,2,1,0:T(8,128)(2,1)S(1)}) custom-call(s32[1]{0:T(128)} %bitcast.15.me_ref, bf16[8,24,3072]{2,1,0:T(8,128)(2,1)S(1)} %constant_dynamic-update-slice_fusion.4.refs_0_, bf16[8,24,3072]{2,1,0:T(8,128)(2,1)} %collective-permute-done.18.refs_1_, ...), custom_call_target="tpu_custom_call" | custom-call | flops 1 | bytes 1 | tf_op jit(solution)/shard_map/pallas_call | solution.py:99
  109.5 24.1 %shard_map.211 = (bf16[512,768]{1,0:T(8,128)(2,1)}, f32[512,768]{1,0:T(8,128)S(1)}, bf16[512,768]{1,0:T(8,128)(2,1)S(1)}, bf16[2,4,48,3072]{3,2,1,0:T(8,128)(2,1...) custom-call(s32[3]{0:T(128)S(1)} %pad_add_fusion.refs_0_.place_ref, ...), custom_call_target="tpu_custom_call" | custom-call | flops 1 | bytes 1 | tf_op jit(solution)/shard_map/pallas_call | solution.py:907
  134.1 4.0 %collective-permute-done.24 = bf16[2,4,48,3072]{3,2,1,0:T(8,128)(2,1)S(1)} collective-permute-done((bf16[2,4,48,3072]{3,2,1,0:T(8,128)(2,1)S(1)}, bf16[2,4,48,3072]{3,2,1,0:T(8,128)(2,1)S(1)}, u32[]{:S(2)}, u32[]{:S(2)}) %collective-permute-start.24) | collective-permute-done | bytes 2359328 | tf_op jit(solution)/shard_map/ppermute | solution.py:43
  138.2 3.4 %collective-permute-done.25 = bf16[2,4,192,768]{3,2,1,0:T(8,128)(2,1)S(1)} collective-permute-done((bf16[2,4,192,768]{3,2,1,0:T(8,128)(2,1)S(1)}, bf16[2,4,192,768]{3,2,1,0:T(8,128)(2,1)S(1)}, u32[]{:S(2)}, u32[]{:S(2)}) %collective-permute-start.25) | collective-permute-done | bytes 2359328 | tf_op jit(solution)/shard_map/ppermute | solution.py:43
  145.6 21.1 %shard_map.213 = (f32[512,768]{1,0:T(8,128)S(1)}, f32[512,768]{1,0:T(8,128)S(1)}, bf16[2,4,48,1536]{3,2,1,0:T(8,128)(2,1)S(1)}, bf16[2,4,48,1536]{3,2,1,0:T(8,12...) custom-call(s32[1]{0:T(128)} %bitcast.4.noisy_ref, ...), custom_call_target="tpu_custom_call" | custom-call | flops 1 | bytes 1 | tf_op jit(solution)/shard_map/pallas_call | solution.py:755
  166.7 4.9 %collective-permute-done.26.refs_1_ = bf16[1,4,2,24,3072]{4,3,2,1,0:T(8,128)(2,1)S(1)} collective-permute-done((bf16[1,4,2,24,3072]{4,3,2,1,0:T(8,128)(2,1)S(1)}, bf16[1,4,2,24,3072]{4,3,2,1,0:T(8,128)(2,1)S(1)}, u32[]{:S(2)}, u32[]{:S(2)}) %collective-permute-start.26) | collective-permute-done | bytes 1179680 | tf_op jit(solution)/shard_map/ppermute | solution.py:43
  176.2 3.1 %shard_map.215 = (f32[512,768]{1,0:T(8,128)S(1)}, bf16[512,768]{1,0:T(8,128)(2,1)S(1)}, bf16[2,4,48,896]{3,2,1,0:T(8,128)(2,1)S(1)}, bf16[2,4,48,896]{3,2,1,0:T(8,128)(2,1)S(1)}) custom-call(s32[1]{0:T(128)} %bitcast.4.noisy_ref, s32[3]{0:T(128)S(1)} %pad_add_fusion.refs_0_.place_ref, bf16[512,768]{1,0:T(8,128)(2,1)S(1)} %bitcast.55, ...), custom_call_target="tpu_custom_call" | custom-call | flops 1 | bytes 1 | tf_op jit(solution)/shard_map/pallas_call | solution.py:982
  179.4 9.1 %collective-permute-done.31.refs_3_ = bf16[1,4,1,96,768]{4,3,2,1,0:T(8,128)(2,1)S(1)} collective-permute-done((bf16[1,4,1,96,768]{4,3,2,1,0:T(8,128)(2,1)S(1)}, bf16[1,4,1,96,768]{4,3,2,1,0:T(8,128)(2,1)S(1)}, u32[]{:S(2)}, u32[]{:S(2)}) %collective-permute-start.31) | collective-permute-done | bytes 589856 | tf_op jit(solution)/shard_map/ppermute | solution.py:43
  198.0 7.6 %collective-permute-done.33.refs_1_ = bf16[2,4,1,24,1536]{4,3,2,1,0:T(8,128)(2,1)S(1)} collective-permute-done((bf16[2,4,1,24,1536]{4,3,2,1,0:T(8,128)(2,1)S(1)}, bf16[2,4,1,24,1536]{4,3,2,1,0:T(8,128)(2,1)S(1)}, u32[]{:S(2)}, u32[]{:S(2)}) %collective-permute-start.33) | collective-permute-done | bytes 589856 | tf_op jit(solution)/shard_map/ppermute | solution.py:43
  210.3 8.6 %collective-permute-done.39.refs_1_ = bf16[1,24,6144]{2,1,0:T(8,128)(2,1)S(1)} collective-permute-done((bf16[1,24,6144]{2,1,0:T(8,128)(2,1)S(1)}, bf16[1,24,6144]{2,1,0:T(8,128)(2,1)S(1)}, u32[]{:S(2)}, u32[]{:S(2)}) %collective-permute-start.39) | collective-permute-done | bytes 294944 | tf_op jit(solution)/shard_map/ppermute | solution.py:43
  219.9 4.4 %collective-permute-start.41 = (bf16[1,24,3200]{2,1,0:T(8,128)(2,1)S(1)}, bf16[1,24,3200]{2,1,0:T(8,128)(2,1)S(1)}, u32[]{:S(2)}, u32[]{:S(2)}) collective-permute-start(bf16[1,24,3200]{2,1,0:T(8,128)(2,1)S(1)} %get-tuple-element.191), channel_id=1, source_target_pairs={{0,8},{1,9},{2,10},{3,11},{4,12},{5,13},{6,14},{7,15},{8,0},{9,1},... | collective-permute-start | bytes 460808 | tf_op jit(solution)/shard_map/ppermute | solution.py:43
  226.7 4.9 %collective-permute-done.35.got = bf16[512,768]{1,0:T(8,128)(2,1)S(1)} collective-permute-done((bf16[512,768]{1,0:T(8,128)(2,1)S(1)}, bf16[512,768]{1,0:T(8,128)(2,1)S(1)}, u32[]{:S(2)}, u32[]{:S(2)}) %collective-permute-start.35) | collective-permute-done | bytes 786464 | tf_op jit(solution)/shard_map/ppermute | solution.py:1180
  (150 shorter events, 65.4 us)
Async XLA Ops:
  1.9 14.5 %collective-permute-start.4 = (bf16[1,24,3200]{2,1,0:T(8,128)(2,1)S(1)}, bf16[1,24,3200]{2,1,0:T(8,128)(2,1)S(1)}, u32[]{:S(2)}, u32[]{:S(2)}) collective-permute-start(bf16[1,24,3200]{2,1,0:T(8,128)(2,1)S(1)} %bitcast.68), channel_id=1, source_target_pairs={{0,24},{1,25},{2,26},{3,27},{4,28},{5,29},{6,30},{7,31},{8,16},{9,... | collective-permute-start | bytes 460808 | tf_op jit(solution)/shard_map/ppermute | solution.py:43
  20.0 17.3 %collective-permute-start.9 = (bf16[1,24,6144]{2,1,0:T(8,128)(2,1)S(1)}, bf16[1,24,6144]{2,1,0:T(8,128)(2,1)S(1)}, u32[]{:S(2)}, u32[]{:S(2)}) collective-permute-start(bf16[1,24,6144]{2,1,0:T(8,128)(2,1)S(1)} %bitcast.72), channel_id=1, source_target_pairs={{0,24},{1,25},{2,26},{3,27},{4,28},{5,29},{6,30},{7,31},{8,16},{9,... | collective-permute-start | bytes 884744 | tf_op jit(solution)/shard_map/ppermute | solution.py:43
  23.6 23.6 %collective-permute-start.8 = (bf16[1,24,6144]{2,1,0:T(8,128)(2,1)S(1)}, bf16[1,24,6144]{2,1,0:T(8,128)(2,1)S(1)}, u32[]{:S(2)}, u32[]{:S(2)}) collective-permute-start(bf16[1,24,6144]{2,1,0:T(8,128)(2,1)S(1)} %bitcast.73), channel_id=1, source_target_pairs={{0,16},{1,17},{2,18},{3,19},{4,20},{5,21},{6,22},{7,23},{8,24},{9,... | collective-permute-start | bytes 884744 | tf_op jit(solution)/shard_map/ppermute | solution.py:43
  23.6 23.6 %collective-permute-start.7 = (bf16[1,24,6144]{2,1,0:T(8,128)(2,1)S(1)}, bf16[1,24,6144]{2,1,0:T(8,128)(2,1)S(1)}, u32[]{:S(2)}, u32[]{:S(2)}) collective-permute-start(bf16[1,24,6144]{2,1,0:T(8,128)(2,1)S(1)} %bitcast.74), channel_id=1, source_target_pairs={{0,8},{1,9},{2,10},{3,11},{4,12},{5,13},{6,14},{7,15},{8,0},{9,1},... | collective-permute-start | bytes 884744 | tf_op jit(solution)/shard_map/ppermute | solution.py:43
  31.7 13.5 %collective-permute-start.1 = (bf16[256,768]{1,0:T(8,128)(2,1)S(1)}, bf16[256,768]{1,0:T(8,128)(2,1)S(1)}, u32[]{:S(2)}, u32[]{:S(2)}) collective-permute-start(bf16[256,768]{1,0:T(8,128)(2,1)S(1)} %get-tuple-element.104), channel_id=1, source_target_pairs={{0,1},{2,3},{4,5},{6,7},{8,9},{10,11},{12,13},{14,15},{16,17},{18,... | collective-permute-start | bytes 1179656 | tf_op jit(solution)/shard_map/ppermute | solution.py:1101
  35.7 13.7 %collective-permute-start.6 = (bf16[8,24,1536]{2,1,0:T(8,128)(2,1)S(1)}, bf16[8,24,1536]{2,1,0:T(8,128)(2,1)S(1)}, u32[]{:S(2)}, u32[]{:S(2)}) collective-permute-start(bf16[8,24,1536]{2,1,0:T(8,128)(2,1)S(1)} %constant_dynamic-update-slice_fusion.refs_0_), channel_id=1, source_target_pairs={{0,4},{1,5},{2,6},{3,7},{4,0},{5,1},{6,2},{7,3},{8,12},{9,13},{10,... | collective-permute-start | bytes 1769480 | tf_op jit(solution)/shard_map/ppermute | solution.py:43
  37.3 17.0 %collective-permute-start.13 = (bf16[8,24,1664]{2,1,0:T(8,128)(2,1)S(1)}, bf16[8,24,1664]{2,1,0:T(8,128)(2,1)S(1)}, u32[]{:S(2)}, u32[]{:S(2)}) collective-permute-start(bf16[8,24,1664]{2,1,0:T(8,128)(2,1)S(1)} %constant_dynamic-update-slice_fusion.2.refs_4_), channel_id=1, source_target_pairs={{0,1},{1,0},{2,3},{3,2},{4,5},{5,4},{6,7},{7,6},{8,9},{9,8},{10,11... | collective-permute-start | bytes 1916936 | tf_op jit(solution)/shard_map/ppermute | solution.py:43
  54.3 17.7 %collective-permute-start.16 = (bf16[4,24,3072]{2,1,0:T(8,128)(2,1)S(1)}, bf16[4,24,3072]{2,1,0:T(8,128)(2,1)S(1)}, u32[]{:S(2)}, u32[]{:S(2)}) collective-permute-start(bf16[4,24,3072]{2,1,0:T(8,128)(2,1)S(1)} %get-tuple-element.119), channel_id=1, source_target_pairs={{0,4},{1,5},{2,6},{3,7},{4,0},{5,1},{6,2},{7,3},{8,12},{9,13},{10,... | collective-permute-start | bytes 1769480 | tf_op jit(solution)/shard_map/ppermute | solution.py:43
  55.9 16.2 %collective-permute-start.17 = (bf16[4,24,3072]{2,1,0:T(8,128)(2,1)S(1)}, bf16[4,24,3072]{2,1,0:T(8,128)(2,1)S(1)}, u32[]{:S(2)}, u32[]{:S(2)}) collective-permute-start(bf16[4,24,3072]{2,1,0:T(8,128)(2,1)S(1)} %get-tuple-element.121), channel_id=1, source_target_pairs={{0,1},{1,0},{2,3},{3,2},{4,5},{5,4},{6,7},{7,6},{8,9},{9,8},{10,11... | collective-permute-start | bytes 1769480 | tf_op jit(solution)/shard_map/ppermute | solution.py:43
  72.1 27.8 %collective-permute-start.18 = (bf16[8,24,3072]{2,1,0:T(8,128)(2,1)S(1)}, bf16[8,24,3072]{2,1,0:T(8,128)(2,1)}, u32[]{:S(2)}, u32[]{:S(2)}) collective-permute-start(bf16[8,24,3072]{2,1,0:T(8,128)(2,1)S(1)} %constant_dynamic-update-slice_fusion.4.refs_0_), channel_id=1, source_target_pairs={{0,1},{1,0},{2,3},{3,2},{4,5},{5,4},{6,7},{7,6},{8,9},{9,8},{10,11... | collective-permute-start | bytes 3538952 | tf_op jit(solution)/shard_map/ppermute | solution.py:43
  74.0 27.2 %collective-permute-start.21 = (bf16[8,24,3072]{2,1,0:T(8,128)(2,1)S(1)}, bf16[8,24,3072]{2,1,0:T(8,128)(2,1)}, u32[]{:S(2)}, u32[]{:S(2)}) collective-permute-start(bf16[8,24,3072]{2,1,0:T(8,128)(2,1)S(1)} %constant_dynamic-update-slice_fusion.6.refs_4_), channel_id=1, source_target_pairs={{0,4},{1,5},{2,6},{3,7},{4,0},{5,1},{6,2},{7,3},{8,12},{9,13},{10,... | collective-permute-start | bytes 3538952 | tf_op jit(solution)/shard_map/ppermute | solution.py:43
  76.4 24.8 %collective-permute-start.19 = (bf16[8,24,3072]{2,1,0:T(8,128)(2,1)S(1)}, bf16[8,24,3072]{2,1,0:T(8,128)(2,1)}, u32[]{:S(2)}, u32[]{:S(2)}) collective-permute-start(bf16[8,24,3072]{2,1,0:T(8,128)(2,1)S(1)} %constant_dynamic-update-slice_fusion.4.refs_0_), channel_id=1, source_target_pairs={{0,2},{1,3},{2,0},{3,1},{4,6},{5,7},{6,4},{7,5},{8,10},{9,11},{10,... | collective-permute-start | bytes 3538952 | tf_op jit(solution)/shard_map/ppermute | solution.py:43
  76.4 24.8 %collective-permute-start.22 = (bf16[8,24,3072]{2,1,0:T(8,128)(2,1)S(1)}, bf16[8,24,3072]{2,1,0:T(8,128)(2,1)}, u32[]{:S(2)}, u32[]{:S(2)}) collective-permute-start(bf16[8,24,3072]{2,1,0:T(8,128)(2,1)S(1)} %constant_dynamic-update-slice_fusion.6.refs_4_), channel_id=1, source_target_pairs={{0,2},{1,3},{2,0},{3,1},{4,6},{5,7},{6,4},{7,5},{8,10},{9,11},{10,... | collective-permute-start | bytes 3538952 | tf_op jit(solution)/shard_map/ppermute | solution.py:43
  143.5 28.1 %collective-permute-start.26 = (bf16[1,4,2,24,3072]{4,3,2,1,0:T(8,128)(2,1)S(1)}, bf16[1,4,2,24,3072]{4,3,2,1,0:T(8,128)(2,1)S(1)}, u32[]{:S(2)}, u32[]{:S(2)}) collective-permute-start(bf16[1,4,2,24,3072]{4,3,2,1,0:T(8,128)(2,1)S(1)} %get-tuple-element.140), channel_id=1, source_target_pairs={{0,4},{1,5},{2,6},{3,7},{4,0},{5,1},{6,2},{7,3},{8,12},{9,13},{10,... | collective-permute-start | bytes 3538952 | tf_op jit(solution)/shard_map/ppermute | solution.py:43
  144.1 27.7 %collective-permute-start.27 = (bf16[2,4,1,96,768]{4,3,2,1,0:T(8,128)(2,1)S(1)}, bf16[2,4,1,96,768]{4,3,2,1,0:T(8,128)(2,1)S(1)}, u32[]{:S(2)}, u32[]{:S(2)}) collective-permute-start(bf16[2,4,1,96,768]{4,3,2,1,0:T(8,128)(2,1)S(1)} %get-tuple-element.141), channel_id=1, source_target_pairs={{0,1},{1,0},{2,3},{3,2},{4,5},{5,4},{6,7},{7,6},{8,9},{9,8},{10,11... | collective-permute-start | bytes 3538952 | tf_op jit(solution)/shard_map/ppermute | solution.py:43
  172.6 15.9 %collective-permute-start.28 = (bf16[2,4,48,1536]{3,2,1,0:T(8,128)(2,1)S(1)}, bf16[2,4,48,1536]{3,2,1,0:T(8,128)(2,1)S(1)}, u32[]{:S(2)}, u32[]{:S(2)}) collective-permute-start(bf16[2,4,48,1536]{3,2,1,0:T(8,128)(2,1)S(1)} %get-tuple-element.162), channel_id=1, source_target_pairs={{0,2},{1,3},{2,0},{3,1},{4,6},{5,7},{6,4},{7,5},{8,10},{9,11},{10,... | collective-permute-start | bytes 3538952 | tf_op jit(solution)/shard_map/ppermute | solution.py:43
  173.2 15.3 %collective-permute-start.31 = (bf16[1,4,1,96,768]{4,3,2,1,0:T(8,128)(2,1)S(1)}, bf16[1,4,1,96,768]{4,3,2,1,0:T(8,128)(2,1)S(1)}, u32[]{:S(2)}, u32[]{:S(2)}) collective-permute-start(bf16[1,4,1,96,768]{4,3,2,1,0:T(8,128)(2,1)S(1)} %get-tuple-element.155), channel_id=1, source_target_pairs={{0,4},{1,5},{2,6},{3,7},{4,0},{5,1},{6,2},{7,3},{8,12},{9,13},{10,... | collective-permute-start | bytes 1769480 | tf_op jit(solution)/shard_map/ppermute | solution.py:43
  174.7 15.0 %collective-permute-start.30 = (bf16[1,4,1,24,3072]{4,3,2,1,0:T(8,128)(2,1)S(1)}, bf16[1,4,1,24,3072]{4,3,2,1,0:T(8,128)(2,1)S(1)}, u32[]{:S(2)}, u32[]{:S(2)}) collective-permute-start(bf16[1,4,1,24,3072]{4,3,2,1,0:T(8,128)(2,1)S(1)} %get-tuple-element.154), channel_id=1, source_target_pairs={{0,1},{1,0},{2,3},{3,2},{4,5},{5,4},{6,7},{7,6},{8,9},{9,8},{10,11... | collective-permute-start | bytes 1769480 | tf_op jit(solution)/shard_map/ppermute | solution.py:43
  191.1 15.3 %collective-permute-start.34 = (bf16[1,4,2,24,1664]{4,3,2,1,0:T(8,128)(2,1)S(1)}, bf16[1,4,2,24,1664]{4,3,2,1,0:T(8,128)(2,1)S(1)}, u32[]{:S(2)}, u32[]{:S(2)}) collective-permute-start(bf16[1,4,2,24,1664]{4,3,2,1,0:T(8,128)(2,1)S(1)} %get-tuple-element.180), channel_id=1, source_target_pairs={{0,4},{1,5},{2,6},{3,7},{4,0},{5,1},{6,2},{7,3},{8,12},{9,13},{10,... | collective-permute-start | bytes 1916936 | tf_op jit(solution)/shard_map/ppermute | solution.py:43
  191.7 14.0 %collective-permute-start.33 = (bf16[2,4,1,24,1536]{4,3,2,1,0:T(8,128)(2,1)S(1)}, bf16[2,4,1,24,1536]{4,3,2,1,0:T(8,128)(2,1)S(1)}, u32[]{:S(2)}, u32[]{:S(2)}) collective-permute-start(bf16[2,4,1,24,1536]{4,3,2,1,0:T(8,128)(2,1)S(1)} %get-tuple-element.178), channel_id=1, source_target_pairs={{0,1},{1,0},{2,3},{3,2},{4,5},{5,4},{6,7},{7,6},{8,9},{9,8},{10,11... | collective-permute-start | bytes 1769480 | tf_op jit(solution)/shard_map/ppermute | solution.py:43
  193.2 15.8 %collective-permute-start.38 = (bf16[1,24,6144]{2,1,0:T(8,128)(2,1)S(1)}, bf16[1,24,6144]{2,1,0:T(8,128)(2,1)S(1)}, u32[]{:S(2)}, u32[]{:S(2)}) collective-permute-start(bf16[1,24,6144]{2,1,0:T(8,128)(2,1)S(1)} %get-tuple-element.171), channel_id=1, source_target_pairs={{0,8},{1,9},{2,10},{3,11},{4,12},{5,13},{6,14},{7,15},{8,0},{9,1},... | collective-permute-start | bytes 884744 | tf_op jit(solution)/shard_map/ppermute | solution.py:43
  195.7 23.2 %collective-permute-start.39 = (bf16[1,24,6144]{2,1,0:T(8,128)(2,1)S(1)}, bf16[1,24,6144]{2,1,0:T(8,128)(2,1)S(1)}, u32[]{:S(2)}, u32[]{:S(2)}) collective-permute-start(bf16[1,24,6144]{2,1,0:T(8,128)(2,1)S(1)} %get-tuple-element.172), channel_id=1, source_target_pairs={{0,16},{1,17},{2,18},{3,19},{4,20},{5,21},{6,22},{7,23},{8,24},{9,... | collective-permute-start | bytes 884744 | tf_op jit(solution)/shard_map/ppermute | solution.py:43
  197.1 21.8 %collective-permute-start.40 = (bf16[1,24,6144]{2,1,0:T(8,128)(2,1)S(1)}, bf16[1,24,6144]{2,1,0:T(8,128)(2,1)S(1)}, u32[]{:S(2)}, u32[]{:S(2)}) collective-permute-start(bf16[1,24,6144]{2,1,0:T(8,128)(2,1)S(1)} %get-tuple-element.173), channel_id=1, source_target_pairs={{0,24},{1,25},{2,26},{3,27},{4,28},{5,29},{6,30},{7,31},{8,16},{9,... | collective-permute-start | bytes 884744 | tf_op jit(solution)/shard_map/ppermute | solution.py:43
  209.0 22.6 %collective-permute-start.35 = (bf16[512,768]{1,0:T(8,128)(2,1)S(1)}, bf16[512,768]{1,0:T(8,128)(2,1)S(1)}, u32[]{:S(2)}, u32[]{:S(2)}) collective-permute-start(bf16[512,768]{1,0:T(8,128)(2,1)S(1)} %get-tuple-element.183), channel_id=1, source_target_pairs={{1,0},{3,2},{5,4},{7,6},{9,8},{11,10},{13,12},{15,14},{17,16},{19,... | collective-permute-start | bytes 2359304 | tf_op jit(solution)/shard_map/ppermute | solution.py:1180
  (40 other events, 390.9 us)

commit v3 on v2

--- a/solution.py
+++ b/solution.py
@@ -78,35 +78,45 @@
     )(me, *flat)
 
 
-def place_pair(up, up_keys, down, down_keys, me):
-    total, (rows, hidden) = sum(len(key) for key in up_keys), up[0].shape[1:]
+def place_pair(up, up_keys, down, down_keys, total, me, begun=()):
+    rows, hidden = up[0].shape[1:]
     width = total * rows
     folds = down[0].shape[2] // width
 
     def body(me_ref, *refs):
         up_out, down_out, up_sem, down_sem = refs[-4:]
-        for piece, key in zip(refs, up_keys):
+        pieces = refs[len(begun) : -4]
+        copies = []
+        for piece, key in zip(pieces, up_keys):
             for j, rel in enumerate(key):
-                pltpu.make_async_copy(piece.at[j], up_out.at[me_ref[0] ^ rel], up_sem).start()
-        for piece, key in zip(refs[len(up) :], down_keys):
+                copies.append((piece.at[j], up_out.at[me_ref[0] ^ rel], up_sem))
+        for piece, key in zip(pieces[len(up) :], down_keys):
             for j, rel in enumerate(key):
                 for f in range(folds):
                     part = piece.at[j, :, pl.ds(f * width, width)]
-                    pltpu.make_async_copy(part, down_out.at[me_ref[0] ^ rel, f], down_sem).start()
-        pltpu.make_async_copy(up_out, up_out, up_sem).wait()
-        pltpu.make_async_copy(down_out, down_out, down_sem).wait()
-
+                    copies.append((part, down_out.at[me_ref[0] ^ rel, f], down_sem))
+        for source, target, sem in copies:
+            pltpu.make_async_copy(source, target, sem).start()
+        count = sum(len(key) for key in up_keys)
+        for out, sem in ((up_out, up_sem), (down_out, down_sem)):
+            some = out.at[pl.ds(0, count)]
+            pltpu.make_async_copy(some, some, sem).wait()
+
+    shapes = ((total, rows, hidden), (total, folds, rows, width))
     return pl.pallas_call(
         body,
-        out_shape=[like((total, rows, hidden), BF16), like((total, folds, rows, width), BF16)],
-        in_specs=[SMEM_SPEC] + [pl.BlockSpec(memory_space=pl.ANY)] * len(up + down),
+        out_shape=[pltpu.VMEM(shape, BF16) for shape in shapes],
+        in_specs=[SMEM_SPEC]
+        + [VMEM_SPEC] * len(begun)
+        + [pl.BlockSpec(memory_space=pl.ANY)] * len(up + down),
         out_specs=[VMEM_SPEC] * 2,
         scratch_shapes=[pltpu.SemaphoreType.DMA] * 2,
+        input_output_aliases={1: 0, 2: 1} if begun else {},
         compiler_params=pltpu.CompilerParams(
             vmem_limit_bytes=4 * total * rows * hidden * (16 // min(16, rows)) + 2**20
         ),
         cost_estimate=SHORT,
-    )(me, *up, *down)
+    )(me, *(pltpu.with_memory_space_constraint(b, pltpu.VMEM) for b in begun), *up, *down)
 
 
 def after(block, *others):
@@ -131,7 +141,7 @@
         out_shape=[like((total, rows, width), BF16) for width in widths],
         in_specs=[VMEM_SPEC] * len(pieces),
         out_specs=[VMEM_SPEC] * len(widths),
-        compiler_params=pltpu.CompilerParams(vmem_limit_bytes=16 * 2**20),
+        compiler_params=pltpu.CompilerParams(vmem_limit_bytes=6 * 2**20),
         cost_estimate=cost,
     )(*pieces)
 
@@ -300,7 +310,7 @@
             out_shape=[like(shape, F32)] + [like(shape, BF16)] * len(self.order[0]),
             in_specs=[VMEM_SPEC] * sum(len(g) for g in groups),
             out_specs=[VMEM_SPEC] * (1 + len(self.order[0])),
-            compiler_params=pltpu.CompilerParams(vmem_limit_bytes=16 * 2**20),
+            compiler_params=pltpu.CompilerParams(vmem_limit_bytes=10 * 2**20),
             cost_estimate=cost or SHORT,
         )(*[t for g in groups for t in g])
         self.keep, self.sends = outs[0], outs[1:]
@@ -516,7 +526,7 @@
         in_specs=[SMEM_SPEC, act] + [whole_spec((rows // 2, width))] * 2 + [extra, qkv, table, table],
         out_specs=[whole_spec((width, rows))] * 2 + [act] * 5,
         scratch_shapes=[pltpu.VMEM((rows, width), BF16)] * 2,
-        compiler_params=pltpu.CompilerParams(vmem_limit_bytes=20 * 2**20),
+        compiler_params=pltpu.CompilerParams(vmem_limit_bytes=15 * 2**20),
         cost_estimate=SHORT,
     )(noisy, tok, far_tok, far_tok_end, joint, joint, cos, sin)
 
@@ -629,7 +639,7 @@
         in_specs=[SMEM_SPEC] + [whole_spec((rows, 1))] * 3 + [whole_spec((1, rows))] + [pair] * 5,
         out_specs=[pair, pl.BlockSpec((8, 2 * rows), lambda j: (j, 0))],
         scratch_shapes=mask_scratch(rows),
-        compiler_params=pltpu.CompilerParams(vmem_limit_bytes=12 * 2**20),
+        compiler_params=pltpu.CompilerParams(vmem_limit_bytes=8 * 2**20),
         cost_estimate=SHORT,
     )(noisy, *in_hbm(lo, hi, code, code_row, q, k, v, kf, vf))
 
@@ -1098,15 +1108,16 @@
     cut = 2 * width
     half = rows // 2
     far_tok = [lax.ppermute(tok[:half], "stream", [(0, 1)])]
-    far_tok.append(lax.ppermute(after(tok[half:], far_tok[0]), "stream", [(0, 1)]))
     (a1, b1), jkey = far_gather(joint, (cut, joint.shape[1] - cut), SHORT, far_tok[0])
-    (u1, d1), ukey = far_gather(after(pair_weights, a1), (hidden, hidden), LONG, far_tok[1])
+    (u1, d1), ukey = far_gather(after(pair_weights, a1), (hidden, hidden), LONG)
     a2, akey = near_gather(a1, jkey, STREAM_BIT)
     b2, bkey = near_gather(b1, jkey, NEAR_BIT)
+    far_tok.append(lax.ppermute(after(tok[half:], a2, b2), "stream", [(0, 1)]))
     a3, akey = last_gather(a2, akey, NEAR_BIT, u1, d1)
     b3, bkey = last_gather(b2, bkey, STREAM_BIT, u1, d1)
     u1, d1 = after(u1, a3[1], b3[1]), after(d1, a3[1], b3[1])
     u_got, d_got = flip(u1, NEAR_BIT), flip(d1, STREAM_BIT)
+    b3[-1] = after(b3[-1], far_tok[1])
     joint = place([a3, b3], [akey, bkey], me).reshape(width, -1)
 
     doc_ids, positions = doc_layout(lengths[0], rows)
@@ -1123,10 +1134,6 @@
     u2, d2 = jnp.concatenate([u1, u_got], axis=0), jnp.concatenate([d1, d_got], axis=0)
     u_got, d_got = flip(u2, STREAM_BIT), flip(d2, NEAR_BIT)
     u_core, d_core = flip(u2, CORE_BIT), flip(d2, CORE_BIT)
-    o, lse = attend(noisy, *masks, after(q, u2, d2), k, v, kf, vf)
-    u_got, d_got = after(u_got, o), after(d_got, o)
-    u3 = [u2, u_got, u_core, flip(u_got, CORE_BIT)]
-    d3 = [d2, d_got, d_core, flip(d_got, CORE_BIT)]
 
     def keys(*bits):
         out = [ukey]
@@ -1135,7 +1142,18 @@
         return [out[0] + out[1], out[2] + out[3], out[4] + out[5], out[6] + out[7]]
 
     ukey, dkey = keys(NEAR_BIT, STREAM_BIT, CORE_BIT), keys(STREAM_BIT, NEAR_BIT, CORE_BIT)
-    up_full, down_full = place_pair(u3, ukey, d3, dkey, me)
+    begun = place_pair([u2, u_core], ukey[::2], [d2, d_core], dkey[::2], n_dev, me)
+    o, lse = attend(noisy, *masks, after(q, u2, d2), k, v, kf, vf)
+    u_got, d_got = after(u_got, o), after(d_got, o)
+    up_full, down_full = place_pair(
+        [u_got, flip(u_got, CORE_BIT)],
+        ukey[1::2],
+        [d_got, flip(d_got, CORE_BIT)],
+        dkey[1::2],
+        n_dev,
+        me,
+        begun,
+    )
     layer_out, gy, ga, dup, ddown, lines, up_lines = mlp(
         place_in, tok, o, cot, joint, up_full.reshape(width, -1), down_full.reshape(-1, width)
     )

time: 238 us -> 232 us (0.975)
  waiting for transfers between devices: 88.2 us -> 80.7 us
    ppermute x1, waiting for transfers between devices: 7.77 us -> 1.63 us  [local(): far_tok.append(lax.ppermute(after(tok[half:], a2, b2), 'stream', [(0, 1)]))]
    pallas_call x1 -> x2, Pallas kernels: 4.72 us -> 5.82 us  [place_pair(): pl.pallas_call(body, out_shape=[pltpu.VMEM(shape, BF16) for shape in shap...]
  transfers between devices with their start and end apart: 44 -> 44, of which waited for: 21 -> 21; matrix products, arithmetic and copies ran while one was open for 3% -> 3% of each run, Pallas kernels for 20% -> 22%
where the time goes in v3:
time: 232 us; the launch traced here: 231 us
  Pallas kernels  84.2 us (36%)
  waiting for transfers between devices  80.7 us (35%)
  starting transfers between devices  53.2 us (23%)
  local copies, waits for them, and re-layouts  5.43 us (2%)
  other arithmetic  3.96 us (2%)
  between operations  3.78 us (2%)
    ppermute x41, waiting for transfers between devices, flip(): lax.ppermute(block, ALL, [(i, i ^ mask) for i in range(device_count())])  70.4 us
    ppermute x41, starting transfers between devices, flip(): lax.ppermute(block, ALL, [(i, i ^ mask) for i in range(device_count())])  44.5 us
    pallas_call x1, Pallas kernels, mlp(): pl.pallas_call(partial(mlp_body, len(ups)), grid_spec=pltpu.PrefetchScala...  24.1 us
    pallas_call x1, Pallas kernels, attend_back(): pl.pallas_call(partial(attend_back_body, early), grid=(pairs,), out_shape...  21.1 us
    pallas_call x1, Pallas kernels, attend(): pl.pallas_call(attend_body, grid=(width // PAIR,), out_shape=[like((rows,...  12 us
    pallas_call x1, Pallas kernels, front(): pl.pallas_call(front_body, grid=(1,), out_shape=[pltpu.HBM((width, rows),...  6.45 us
    pallas_call x2, Pallas kernels, place_pair(): pl.pallas_call(body, out_shape=[pltpu.VMEM(shape, BF16) for shape in shap...  5.82 us
    ppermute x1, waiting for transfers between devices, local(): lax.ppermute(after(send, front_sum.send, back_sum.send), 'stream', [(1, 0)])  5.05 us
  transfers between devices with their start and end apart: 44, of which 21 were waited for; matrix products, arithmetic and copies ran while one was open for 3% of the time, Pallas kernels for 22%

profile of v3, /device:TPU:0, one launch (start us, length us, event | category | flops | bytes accessed | tf_op | source)
XLA Modules:
  0.0 231.2 jit_solution(17246615211211633880)
XLA Ops:
  1.9 5.1 %collective-permute-start.3 = (bf16[1,24,3200]{2,1,0:T(8,128)(2,1)S(1)}, bf16[1,24,3200]{2,1,0:T(8,128)(2,1)S(1)}, u32[]{:S(2)}, u32[]{:S(2)}) collective-permute-start(bf16[1,24,3200]{2,1,0:T(8,128)(2,1)S(1)} %bitcast.68), channel_id=1, source_target_pairs={{0,24},{1,25},{2,26},{3,27},{4,28},{5,29},{6,30},{7,31},{8,16},{9,... | collective-permute-start | bytes 460808 | tf_op jit(solution)/shard_map/ppermute | solution.py:43
  8.8 3.6 %collective-permute-start = (bf16[256,768]{1,0:T(8,128)(2,1)S(1)}, bf16[256,768]{1,0:T(8,128)(2,1)S(1)}, u32[]{:S(2)}, u32[]{:S(2)}) collective-permute-start(bf16[256,768]{1,0:T(8,128)(2,1)S(1)} %get-tuple-element.212), channel_id=1, source_target_pairs={{0,1},{2,3},{4,5},{6,7},{8,9},{10,11},{12,13},{14,15},{16,17},{18,... | collective-permute-start | bytes 1179656 | tf_op jit(solution)/shard_map/ppermute | solution.py:1110
  16.4 3.6 %collective-permute-done.far_tok = bf16[256,768]{1,0:T(8,128)(2,1)S(1)} collective-permute-done((bf16[256,768]{1,0:T(8,128)(2,1)S(1)}, bf16[256,768]{1,0:T(8,128)(2,1)S(1)}, u32[]{:S(2)}, u32[]{:S(2)}) %collective-permute-start) | collective-permute-done | bytes 393248 | tf_op jit(solution)/shard_map/ppermute | solution.py:1110
  20.0 3.5 %collective-permute-start.10 = (bf16[1,24,6144]{2,1,0:T(8,128)(2,1)S(1)}, bf16[1,24,6144]{2,1,0:T(8,128)(2,1)S(1)}, u32[]{:S(2)}, u32[]{:S(2)}) collective-permute-start(bf16[1,24,6144]{2,1,0:T(8,128)(2,1)S(1)} %bitcast.72), channel_id=1, source_target_pairs={{0,24},{1,25},{2,26},{3,27},{4,28},{5,29},{6,30},{7,31},{8,16},{9,... | collective-permute-start | bytes 884744 | tf_op jit(solution)/shard_map/ppermute | solution.py:43
  28.6 3.1 %collective-permute-done.4 = bf16[4,24,1536]{2,1,0:T(8,128)(2,1)S(1)} collective-permute-done((bf16[4,24,1536]{2,1,0:T(8,128)(2,1)S(1)}, bf16[4,24,1536]{2,1,0:T(8,128)(2,1)S(1)}, u32[]{:S(2)}, u32[]{:S(2)}) %collective-permute-start.4) | collective-permute-done | bytes 294944 | tf_op jit(solution)/shard_map/ppermute | solution.py:43
  33.3 3.5 %collective-permute-done.5 = bf16[4,24,1664]{2,1,0:T(8,128)(2,1)S(1)} collective-permute-done((bf16[4,24,1664]{2,1,0:T(8,128)(2,1)S(1)}, bf16[4,24,1664]{2,1,0:T(8,128)(2,1)S(1)}, u32[]{:S(2)}, u32[]{:S(2)}) %collective-permute-start.5) | collective-permute-done | bytes 319520 | tf_op jit(solution)/shard_map/ppermute | solution.py:43
  36.9 3.9 %collective-permute-start.6 = (bf16[256,768]{1,0:T(8,128)(2,1)S(1)}, bf16[256,768]{1,0:T(8,128)(2,1)S(1)}, u32[]{:S(2)}, u32[]{:S(2)}) collective-permute-start(bf16[256,768]{1,0:T(8,128)(2,1)S(1)} %get-tuple-element.110), channel_id=1, source_target_pairs={{0,1},{2,3},{4,5},{6,7},{8,9},{10,11},{12,13},{14,15},{16,17},{18,... | collective-permute-start | bytes 1179656 | tf_op jit(solution)/shard_map/ppermute | solution.py:1115
  40.9 6.3 %collective-permute-done.9.refs_2_ = bf16[1,24,6144]{2,1,0:T(8,128)(2,1)S(1)} collective-permute-done((bf16[1,24,6144]{2,1,0:T(8,128)(2,1)S(1)}, bf16[1,24,6144]{2,1,0:T(8,128)(2,1)S(1)}, u32[]{:S(2)}, u32[]{:S(2)}) %collective-permute-start.9) | collective-permute-done | bytes 294944 | tf_op jit(solution)/shard_map/ppermute | solution.py:43
  60.0 6.4 %shard_map.208 = (bf16[768,512]{1,0:T(8,128)(2,1)}, bf16[768,512]{1,0:T(8,128)(2,1)}, bf16[512,768]{1,0:T(8,128)(2,1)}, bf16[512,768]{1,0:T(8,128)(2,1)}, bf16[5...) custom-call(s32[1]{0:T(128)} %bitcast.4.noisy_ref, bf16[512,768]{1,0:T(8,128)(2,1)S(1)} %bitcast.56, ...), custom_call_target="tpu_custom_call" | custom-call | flops 1 | bytes 1 | tf_op jit(solution)/shard_map/pallas_call | solution.py:522
  73.7 12.0 %shard_map.209 = (bf16[512,768]{1,0:T(8,128)(2,1)S(1)}, f32[48,1024]{1,0:T(8,128)S(1)}) custom-call(s32[1]{0:T(128)} %bitcast.4.noisy_ref, s32[512,1]{1,0:T(8,128)} %copy-done.15, s32[512,1]{1,0:T(8,128)} %get-tuple-element.209.hi, s32[512,1]{1,0:T(8,128)} %get-tuple-element.210.code, s32[1,512]{1,0:T(1,128)} %get-tuple-element.208.code_row, ...), custom_call_target="tpu_custom_call" | custom-call | flops 1 | bytes 1 | tf_op jit(solution)/shard_map/pallas_call | solution.py:635
  86.3 8.9 %collective-permute-done.22.refs_4_ = bf16[8,24,3072]{2,1,0:T(8,128)(2,1)} collective-permute-done((bf16[8,24,3072]{2,1,0:T(8,128)(2,1)S(1)}, bf16[8,24,3072]{2,1,0:T(8,128)(2,1)}, u32[]{:S(2)}, u32[]{:S(2)}) %collective-permute-start.22) | collective-permute-done | bytes 1179680 | tf_op jit(solution)/shard_map/ppermute | solution.py:43
  95.9 3.3 %shard_map.210 = (bf16[32,24,3072]{2,1,0:T(8,128)(2,1)S(1)}, bf16[32,4,24,768]{3,2,1,0:T(8,128)(2,1)S(1)}) custom-call(s32[1]{0:T(128)} %bitcast.20.me_ref, bf16[8,24,3072]{2,1,0:T(8,128)(2,1)S(1)} %constant_dynamic-update-slice_fusion.4.refs_0_, bf16[8,24,3072]{2,1,0:T(8,128)(2,1)} %collective-permute-done.18.refs_1_, ...), custom_call_target="tpu_custom_call" | custom-call | flops 1 | bytes 1 | tf_op jit(solution)/shard_map/pallas_call | solution.py:106
  102.7 24.1 %shard_map.212 = (bf16[512,768]{1,0:T(8,128)(2,1)}, f32[512,768]{1,0:T(8,128)S(1)}, bf16[512,768]{1,0:T(8,128)(2,1)S(1)}, bf16[2,4,48,3072]{3,2,1,0:T(8,128)(2,1...) custom-call(s32[3]{0:T(128)S(1)} %pad_add_fusion.refs_0_.place_ref, ...), custom_call_target="tpu_custom_call" | custom-call | flops 1 | bytes 1 | tf_op jit(solution)/shard_map/pallas_call | solution.py:917
  128.2 4.0 %collective-permute-done.24 = bf16[2,4,48,3072]{3,2,1,0:T(8,128)(2,1)S(1)} collective-permute-done((bf16[2,4,48,3072]{3,2,1,0:T(8,128)(2,1)S(1)}, bf16[2,4,48,3072]{3,2,1,0:T(8,128)(2,1)S(1)}, u32[]{:S(2)}, u32[]{:S(2)}) %collective-permute-start.24) | collective-permute-done | bytes 2359328 | tf_op jit(solution)/shard_map/ppermute | solution.py:43
  132.2 3.4 %collective-permute-done.25 = bf16[2,4,192,768]{3,2,1,0:T(8,128)(2,1)S(1)} collective-permute-done((bf16[2,4,192,768]{3,2,1,0:T(8,128)(2,1)S(1)}, bf16[2,4,192,768]{3,2,1,0:T(8,128)(2,1)S(1)}, u32[]{:S(2)}, u32[]{:S(2)}) %collective-permute-start.25) | collective-permute-done | bytes 2359328 | tf_op jit(solution)/shard_map/ppermute | solution.py:43
  139.0 21.1 %shard_map.214 = (f32[512,768]{1,0:T(8,128)S(1)}, f32[512,768]{1,0:T(8,128)S(1)}, bf16[2,4,48,1536]{3,2,1,0:T(8,128)(2,1)S(1)}, bf16[2,4,48,1536]{3,2,1,0:T(8,12...) custom-call(s32[1]{0:T(128)} %bitcast.4.noisy_ref, ...), custom_call_target="tpu_custom_call" | custom-call | flops 1 | bytes 1 | tf_op jit(solution)/shard_map/pallas_call | solution.py:765
  160.1 5.5 %collective-permute-done.27.refs_3_ = bf16[2,4,1,96,768]{4,3,2,1,0:T(8,128)(2,1)S(1)} collective-permute-done((bf16[2,4,1,96,768]{4,3,2,1,0:T(8,128)(2,1)S(1)}, bf16[2,4,1,96,768]{4,3,2,1,0:T(8,128)(2,1)S(1)}, u32[]{:S(2)}, u32[]{:S(2)}) %collective-permute-start.27) | collective-permute-done | bytes 1179680 | tf_op jit(solution)/shard_map/ppermute | solution.py:43
  169.8 3.1 %shard_map.216 = (f32[512,768]{1,0:T(8,128)S(1)}, bf16[512,768]{1,0:T(8,128)(2,1)S(1)}, bf16[2,4,48,896]{3,2,1,0:T(8,128)(2,1)S(1)}, bf16[2,4,48,896]{3,2,1,0:T(8,128)(2,1)S(1)}) custom-call(s32[1]{0:T(128)} %bitcast.4.noisy_ref, s32[3]{0:T(128)S(1)} %pad_add_fusion.refs_0_.place_ref, bf16[512,768]{1,0:T(8,128)(2,1)S(1)} %bitcast.57, ...), custom_call_target="tpu_custom_call" | custom-call | flops 1 | bytes 1 | tf_op jit(solution)/shard_map/pallas_call | solution.py:992
  173.0 9.4 %collective-permute-done.31.refs_3_ = bf16[1,4,1,96,768]{4,3,2,1,0:T(8,128)(2,1)S(1)} collective-permute-done((bf16[1,4,1,96,768]{4,3,2,1,0:T(8,128)(2,1)S(1)}, bf16[1,4,1,96,768]{4,3,2,1,0:T(8,128)(2,1)S(1)}, u32[]{:S(2)}, u32[]{:S(2)}) %collective-permute-start.31) | collective-permute-done | bytes 589856 | tf_op jit(solution)/shard_map/ppermute | solution.py:43
  191.6 7.9 %collective-permute-done.33.refs_1_ = bf16[2,4,1,24,1536]{4,3,2,1,0:T(8,128)(2,1)S(1)} collective-permute-done((bf16[2,4,1,24,1536]{4,3,2,1,0:T(8,128)(2,1)S(1)}, bf16[2,4,1,24,1536]{4,3,2,1,0:T(8,128)(2,1)S(1)}, u32[]{:S(2)}, u32[]{:S(2)}) %collective-permute-start.33) | collective-permute-done | bytes 589856 | tf_op jit(solution)/shard_map/ppermute | solution.py:43
  204.2 7.8 %collective-permute-done.39.refs_1_ = bf16[1,24,6144]{2,1,0:T(8,128)(2,1)S(1)} collective-permute-done((bf16[1,24,6144]{2,1,0:T(8,128)(2,1)S(1)}, bf16[1,24,6144]{2,1,0:T(8,128)(2,1)S(1)}, u32[]{:S(2)}, u32[]{:S(2)}) %collective-permute-start.39) | collective-permute-done | bytes 294944 | tf_op jit(solution)/shard_map/ppermute | solution.py:43
  213.0 4.0 %collective-permute-start.41 = (bf16[1,24,3200]{2,1,0:T(8,128)(2,1)S(1)}, bf16[1,24,3200]{2,1,0:T(8,128)(2,1)S(1)}, u32[]{:S(2)}, u32[]{:S(2)}) collective-permute-start(bf16[1,24,3200]{2,1,0:T(8,128)(2,1)S(1)} %get-tuple-element.195), channel_id=1, source_target_pairs={{0,8},{1,9},{2,10},{3,11},{4,12},{5,13},{6,14},{7,15},{8,0},{9,1},... | collective-permute-start | bytes 460808 | tf_op jit(solution)/shard_map/ppermute | solution.py:43
  219.5 5.0 %collective-permute-done.35.got = bf16[512,768]{1,0:T(8,128)(2,1)S(1)} collective-permute-done((bf16[512,768]{1,0:T(8,128)(2,1)S(1)}, bf16[512,768]{1,0:T(8,128)(2,1)S(1)}, u32[]{:S(2)}, u32[]{:S(2)}) %collective-permute-start.35) | collective-permute-done | bytes 786464 | tf_op jit(solution)/shard_map/ppermute | solution.py:1198
  226.3 2.7 %collective-permute-done.42.refs_1_ = bf16[1,24,3200]{2,1,0:T(8,128)(2,1)S(1)} collective-permute-done((bf16[1,24,3200]{2,1,0:T(8,128)(2,1)S(1)}, bf16[1,24,3200]{2,1,0:T(8,128)(2,1)S(1)}, u32[]{:S(2)}, u32[]{:S(2)}) %collective-permute-start.42) | collective-permute-done | bytes 153632 | tf_op jit(solution)/shard_map/ppermute | solution.py:43
  (151 shorter events, 66.1 us)
Async XLA Ops:
  1.9 14.6 %collective-permute-start.3 = (bf16[1,24,3200]{2,1,0:T(8,128)(2,1)S(1)}, bf16[1,24,3200]{2,1,0:T(8,128)(2,1)S(1)}, u32[]{:S(2)}, u32[]{:S(2)}) collective-permute-start(bf16[1,24,3200]{2,1,0:T(8,128)(2,1)S(1)} %bitcast.68), channel_id=1, source_target_pairs={{0,24},{1,25},{2,26},{3,27},{4,28},{5,29},{6,30},{7,31},{8,16},{9,... | collective-permute-start | bytes 460808 | tf_op jit(solution)/shard_map/ppermute | solution.py:43
  20.0 16.9 %collective-permute-start.10 = (bf16[1,24,6144]{2,1,0:T(8,128)(2,1)S(1)}, bf16[1,24,6144]{2,1,0:T(8,128)(2,1)S(1)}, u32[]{:S(2)}, u32[]{:S(2)}) collective-permute-start(bf16[1,24,6144]{2,1,0:T(8,128)(2,1)S(1)} %bitcast.72), channel_id=1, source_target_pairs={{0,24},{1,25},{2,26},{3,27},{4,28},{5,29},{6,30},{7,31},{8,16},{9,... | collective-permute-start | bytes 884744 | tf_op jit(solution)/shard_map/ppermute | solution.py:43
  23.6 17.3 %collective-permute-start.8 = (bf16[1,24,6144]{2,1,0:T(8,128)(2,1)S(1)}, bf16[1,24,6144]{2,1,0:T(8,128)(2,1)S(1)}, u32[]{:S(2)}, u32[]{:S(2)}) collective-permute-start(bf16[1,24,6144]{2,1,0:T(8,128)(2,1)S(1)} %bitcast.73), channel_id=1, source_target_pairs={{0,8},{1,9},{2,10},{3,11},{4,12},{5,13},{6,14},{7,15},{8,0},{9,1},... | collective-permute-start | bytes 884744 | tf_op jit(solution)/shard_map/ppermute | solution.py:43
  23.6 23.6 %collective-permute-start.9 = (bf16[1,24,6144]{2,1,0:T(8,128)(2,1)S(1)}, bf16[1,24,6144]{2,1,0:T(8,128)(2,1)S(1)}, u32[]{:S(2)}, u32[]{:S(2)}) collective-permute-start(bf16[1,24,6144]{2,1,0:T(8,128)(2,1)S(1)} %bitcast.74), channel_id=1, source_target_pairs={{0,16},{1,17},{2,18},{3,19},{4,20},{5,21},{6,22},{7,23},{8,24},{9,... | collective-permute-start | bytes 884744 | tf_op jit(solution)/shard_map/ppermute | solution.py:43
  31.7 20.1 %collective-permute-start.7 = (bf16[8,24,1536]{2,1,0:T(8,128)(2,1)S(1)}, bf16[8,24,1536]{2,1,0:T(8,128)(2,1)S(1)}, u32[]{:S(2)}, u32[]{:S(2)}) collective-permute-start(bf16[8,24,1536]{2,1,0:T(8,128)(2,1)S(1)} %constant_dynamic-update-slice_fusion.refs_0_), channel_id=1, source_target_pairs={{0,4},{1,5},{2,6},{3,7},{4,0},{5,1},{6,2},{7,3},{8,12},{9,13},{10,... | collective-permute-start | bytes 1769480 | tf_op jit(solution)/shard_map/ppermute | solution.py:43
  36.9 17.0 %collective-permute-start.6 = (bf16[256,768]{1,0:T(8,128)(2,1)S(1)}, bf16[256,768]{1,0:T(8,128)(2,1)S(1)}, u32[]{:S(2)}, u32[]{:S(2)}) collective-permute-start(bf16[256,768]{1,0:T(8,128)(2,1)S(1)} %get-tuple-element.110), channel_id=1, source_target_pairs={{0,1},{2,3},{4,5},{6,7},{8,9},{10,11},{12,13},{14,15},{16,17},{18,... | collective-permute-start | bytes 1179656 | tf_op jit(solution)/shard_map/ppermute | solution.py:1115
  53.9 14.4 %collective-permute-start.17 = (bf16[4,24,3072]{2,1,0:T(8,128)(2,1)S(1)}, bf16[4,24,3072]{2,1,0:T(8,128)(2,1)S(1)}, u32[]{:S(2)}, u32[]{:S(2)}) collective-permute-start(bf16[4,24,3072]{2,1,0:T(8,128)(2,1)S(1)} %get-tuple-element.123), channel_id=1, source_target_pairs={{0,1},{1,0},{2,3},{3,2},{4,5},{5,4},{6,7},{7,6},{8,9},{9,8},{10,11... | collective-permute-start | bytes 1769480 | tf_op jit(solution)/shard_map/ppermute | solution.py:43
  56.4 14.5 %collective-permute-start.16 = (bf16[4,24,3072]{2,1,0:T(8,128)(2,1)S(1)}, bf16[4,24,3072]{2,1,0:T(8,128)(2,1)S(1)}, u32[]{:S(2)}, u32[]{:S(2)}) collective-permute-start(bf16[4,24,3072]{2,1,0:T(8,128)(2,1)S(1)} %get-tuple-element.121), channel_id=1, source_target_pairs={{0,4},{1,5},{2,6},{3,7},{4,0},{5,1},{6,2},{7,3},{8,12},{9,13},{10,... | collective-permute-start | bytes 1769480 | tf_op jit(solution)/shard_map/ppermute | solution.py:43
  68.4 26.9 %collective-permute-start.22 = (bf16[8,24,3072]{2,1,0:T(8,128)(2,1)S(1)}, bf16[8,24,3072]{2,1,0:T(8,128)(2,1)}, u32[]{:S(2)}, u32[]{:S(2)}) collective-permute-start(bf16[8,24,3072]{2,1,0:T(8,128)(2,1)S(1)} %constant_dynamic-update-slice_fusion.6.refs_2_), channel_id=1, source_target_pairs={{0,4},{1,5},{2,6},{3,7},{4,0},{5,1},{6,2},{7,3},{8,12},{9,13},{10,... | collective-permute-start | bytes 3538952 | tf_op jit(solution)/shard_map/ppermute | solution.py:43
  71.0 24.3 %collective-permute-start.20 = (bf16[8,24,3072]{2,1,0:T(8,128)(2,1)S(1)}, bf16[8,24,3072]{2,1,0:T(8,128)(2,1)}, u32[]{:S(2)}, u32[]{:S(2)}) collective-permute-start(bf16[8,24,3072]{2,1,0:T(8,128)(2,1)S(1)} %constant_dynamic-update-slice_fusion.4.refs_0_), channel_id=1, source_target_pairs={{0,1},{1,0},{2,3},{3,2},{4,5},{5,4},{6,7},{7,6},{8,9},{9,8},{10,11... | collective-permute-start | bytes 3538952 | tf_op jit(solution)/shard_map/ppermute | solution.py:43
  73.2 22.7 %collective-permute-start.19 = (bf16[8,24,3072]{2,1,0:T(8,128)(2,1)S(1)}, bf16[8,24,3072]{2,1,0:T(8,128)(2,1)}, u32[]{:S(2)}, u32[]{:S(2)}) collective-permute-start(bf16[8,24,3072]{2,1,0:T(8,128)(2,1)S(1)} %constant_dynamic-update-slice_fusion.6.refs_2_), channel_id=1, source_target_pairs={{0,2},{1,3},{2,0},{3,1},{4,6},{5,7},{6,4},{7,5},{8,10},{9,11},{10,... | collective-permute-start | bytes 3538952 | tf_op jit(solution)/shard_map/ppermute | solution.py:43
  73.2 22.7 %collective-permute-start.18 = (bf16[8,24,3072]{2,1,0:T(8,128)(2,1)S(1)}, bf16[8,24,3072]{2,1,0:T(8,128)(2,1)}, u32[]{:S(2)}, u32[]{:S(2)}) collective-permute-start(bf16[8,24,3072]{2,1,0:T(8,128)(2,1)S(1)} %constant_dynamic-update-slice_fusion.4.refs_0_), channel_id=1, source_target_pairs={{0,2},{1,3},{2,0},{3,1},{4,6},{5,7},{6,4},{7,5},{8,10},{9,11},{10,... | collective-permute-start | bytes 3538952 | tf_op jit(solution)/shard_map/ppermute | solution.py:43
  137.5 28.1 %collective-permute-start.27 = (bf16[2,4,1,96,768]{4,3,2,1,0:T(8,128)(2,1)S(1)}, bf16[2,4,1,96,768]{4,3,2,1,0:T(8,128)(2,1)S(1)}, u32[]{:S(2)}, u32[]{:S(2)}) collective-permute-start(bf16[2,4,1,96,768]{4,3,2,1,0:T(8,128)(2,1)S(1)} %get-tuple-element.145), channel_id=1, source_target_pairs={{0,1},{1,0},{2,3},{3,2},{4,5},{5,4},{6,7},{7,6},{8,9},{9,8},{10,11... | collective-permute-start | bytes 3538952 | tf_op jit(solution)/shard_map/ppermute | solution.py:43
  138.0 27.7 %collective-permute-start.26 = (bf16[1,4,2,24,3072]{4,3,2,1,0:T(8,128)(2,1)S(1)}, bf16[1,4,2,24,3072]{4,3,2,1,0:T(8,128)(2,1)S(1)}, u32[]{:S(2)}, u32[]{:S(2)}) collective-permute-start(bf16[1,4,2,24,3072]{4,3,2,1,0:T(8,128)(2,1)S(1)} %get-tuple-element.144), channel_id=1, source_target_pairs={{0,4},{1,5},{2,6},{3,7},{4,0},{5,1},{6,2},{7,3},{8,12},{9,13},{10,... | collective-permute-start | bytes 3538952 | tf_op jit(solution)/shard_map/ppermute | solution.py:43
  166.6 15.9 %collective-permute-start.28 = (bf16[2,4,48,1536]{3,2,1,0:T(8,128)(2,1)S(1)}, bf16[2,4,48,1536]{3,2,1,0:T(8,128)(2,1)S(1)}, u32[]{:S(2)}, u32[]{:S(2)}) collective-permute-start(bf16[2,4,48,1536]{3,2,1,0:T(8,128)(2,1)S(1)} %get-tuple-element.166), channel_id=1, source_target_pairs={{0,2},{1,3},{2,0},{3,1},{4,6},{5,7},{6,4},{7,5},{8,10},{9,11},{10,... | collective-permute-start | bytes 3538952 | tf_op jit(solution)/shard_map/ppermute | solution.py:43
  167.1 15.3 %collective-permute-start.31 = (bf16[1,4,1,96,768]{4,3,2,1,0:T(8,128)(2,1)S(1)}, bf16[1,4,1,96,768]{4,3,2,1,0:T(8,128)(2,1)S(1)}, u32[]{:S(2)}, u32[]{:S(2)}) collective-permute-start(bf16[1,4,1,96,768]{4,3,2,1,0:T(8,128)(2,1)S(1)} %get-tuple-element.159), channel_id=1, source_target_pairs={{0,4},{1,5},{2,6},{3,7},{4,0},{5,1},{6,2},{7,3},{8,12},{9,13},{10,... | collective-permute-start | bytes 1769480 | tf_op jit(solution)/shard_map/ppermute | solution.py:43
  168.1 15.0 %collective-permute-start.30 = (bf16[1,4,1,24,3072]{4,3,2,1,0:T(8,128)(2,1)S(1)}, bf16[1,4,1,24,3072]{4,3,2,1,0:T(8,128)(2,1)S(1)}, u32[]{:S(2)}, u32[]{:S(2)}) collective-permute-start(bf16[1,4,1,24,3072]{4,3,2,1,0:T(8,128)(2,1)S(1)} %get-tuple-element.158), channel_id=1, source_target_pairs={{0,1},{1,0},{2,3},{3,2},{4,5},{5,4},{6,7},{7,6},{8,9},{9,8},{10,11... | collective-permute-start | bytes 1769480 | tf_op jit(solution)/shard_map/ppermute | solution.py:43
  184.5 15.3 %collective-permute-start.34 = (bf16[1,4,2,24,1664]{4,3,2,1,0:T(8,128)(2,1)S(1)}, bf16[1,4,2,24,1664]{4,3,2,1,0:T(8,128)(2,1)S(1)}, u32[]{:S(2)}, u32[]{:S(2)}) collective-permute-start(bf16[1,4,2,24,1664]{4,3,2,1,0:T(8,128)(2,1)S(1)} %get-tuple-element.184), channel_id=1, source_target_pairs={{0,4},{1,5},{2,6},{3,7},{4,0},{5,1},{6,2},{7,3},{8,12},{9,13},{10,... | collective-permute-start | bytes 1916936 | tf_op jit(solution)/shard_map/ppermute | solution.py:43
  185.6 13.9 %collective-permute-start.33 = (bf16[2,4,1,24,1536]{4,3,2,1,0:T(8,128)(2,1)S(1)}, bf16[2,4,1,24,1536]{4,3,2,1,0:T(8,128)(2,1)S(1)}, u32[]{:S(2)}, u32[]{:S(2)}) collective-permute-start(bf16[2,4,1,24,1536]{4,3,2,1,0:T(8,128)(2,1)S(1)} %get-tuple-element.182), channel_id=1, source_target_pairs={{0,1},{1,0},{2,3},{3,2},{4,5},{5,4},{6,7},{7,6},{8,9},{9,8},{10,11... | collective-permute-start | bytes 1769480 | tf_op jit(solution)/shard_map/ppermute | solution.py:43
  187.2 15.7 %collective-permute-start.38 = (bf16[1,24,6144]{2,1,0:T(8,128)(2,1)S(1)}, bf16[1,24,6144]{2,1,0:T(8,128)(2,1)S(1)}, u32[]{:S(2)}, u32[]{:S(2)}) collective-permute-start(bf16[1,24,6144]{2,1,0:T(8,128)(2,1)S(1)} %get-tuple-element.175), channel_id=1, source_target_pairs={{0,8},{1,9},{2,10},{3,11},{4,12},{5,13},{6,14},{7,15},{8,0},{9,1},... | collective-permute-start | bytes 884744 | tf_op jit(solution)/shard_map/ppermute | solution.py:43
  188.5 23.5 %collective-permute-start.39 = (bf16[1,24,6144]{2,1,0:T(8,128)(2,1)S(1)}, bf16[1,24,6144]{2,1,0:T(8,128)(2,1)S(1)}, u32[]{:S(2)}, u32[]{:S(2)}) collective-permute-start(bf16[1,24,6144]{2,1,0:T(8,128)(2,1)S(1)} %get-tuple-element.176), channel_id=1, source_target_pairs={{0,16},{1,17},{2,18},{3,19},{4,20},{5,21},{6,22},{7,23},{8,24},{9,... | collective-permute-start | bytes 884744 | tf_op jit(solution)/shard_map/ppermute | solution.py:43
  191.1 20.8 %collective-permute-start.40 = (bf16[1,24,6144]{2,1,0:T(8,128)(2,1)S(1)}, bf16[1,24,6144]{2,1,0:T(8,128)(2,1)S(1)}, u32[]{:S(2)}, u32[]{:S(2)}) collective-permute-start(bf16[1,24,6144]{2,1,0:T(8,128)(2,1)S(1)} %get-tuple-element.177), channel_id=1, source_target_pairs={{0,24},{1,25},{2,26},{3,27},{4,28},{5,29},{6,30},{7,31},{8,16},{9,... | collective-permute-start | bytes 884744 | tf_op jit(solution)/shard_map/ppermute | solution.py:43
  202.9 21.6 %collective-permute-start.35 = (bf16[512,768]{1,0:T(8,128)(2,1)S(1)}, bf16[512,768]{1,0:T(8,128)(2,1)S(1)}, u32[]{:S(2)}, u32[]{:S(2)}) collective-permute-start(bf16[512,768]{1,0:T(8,128)(2,1)S(1)} %get-tuple-element.187), channel_id=1, source_target_pairs={{1,0},{3,2},{5,4},{7,6},{9,8},{11,10},{13,12},{15,14},{17,16},{19,... | collective-permute-start | bytes 2359304 | tf_op jit(solution)/shard_map/ppermute | solution.py:1198
  213.0 13.2 %collective-permute-start.41 = (bf16[1,24,3200]{2,1,0:T(8,128)(2,1)S(1)}, bf16[1,24,3200]{2,1,0:T(8,128)(2,1)S(1)}, u32[]{:S(2)}, u32[]{:S(2)}) collective-permute-start(bf16[1,24,3200]{2,1,0:T(8,128)(2,1)S(1)} %get-tuple-element.195), channel_id=1, source_target_pairs={{0,8},{1,9},{2,10},{3,11},{4,12},{5,13},{6,14},{7,15},{8,0},{9,1},... | collective-permute-start | bytes 460808 | tf_op jit(solution)/shard_map/ppermute | solution.py:43
  (40 other events, 350.6 us)

commit v4 on v3

--- a/solution.py
+++ b/solution.py
@@ -1021,12 +1021,20 @@
                 :, at + p * PAIR : at + (p + 1) * PAIR
             ]
     out[...] = total[:, 3 * width : 4 * width]
-    small[...] = total[:, 4 * width :]
+    row = lax.broadcasted_iota(jnp.int32, (8, SMALL), 0)
+    lane = lax.broadcasted_iota(jnp.int32, (8, SMALL), 1)
+    small[...] = lax.dot_general(
+        (row == lane).astype(F32),
+        total[:, 4 * width :],
+        (((1,), (1,)), ((), ())),
+        precision=lax.Precision.HIGHEST,
+        preferred_element_type=F32,
+    )
 
 
 def last_sum(keep, got, width):
     rows = keep.shape[1]
-    shapes = ((rows, 3 * width), (rows, width), (rows, SMALL))
+    shapes = ((rows, 3 * width), (rows, width), (8, rows))
     return pl.pallas_call(
         partial(last_sum_body, width // PAIR),
         out_shape=[like(shape, F32) for shape in shapes],
@@ -1203,7 +1211,7 @@
     owned_qkv, owned_out, owned_small = last_sum(attn_far.keep, attn_far.got, width)
 
     def small_owned(i):
-        return owned_small[:, i]
+        return owned_small[i]
 
     return (
         layer_out[None],
@@ -1213,7 +1221,7 @@
         owned_out,
         small_owned(1),
         owned_up,
-        owned_small[:, 3:7].T.reshape(-1),
+        owned_small[3:7].reshape(-1),
         owned_down,
         small_owned(2),
     )

time: 232 us -> 231 us (level)
  no operation moved by 1% of the time
where the time goes in v4:
time: 231 us
  Pallas kernels  84.2 us (36%)
  waiting for transfers between devices  80.6 us (35%)
  starting transfers between devices  53.2 us (23%)
  local copies, waits for them, and re-layouts  5.04 us (2%)
  other arithmetic  3.95 us (2%)
  between operations  3.78 us (2%)
    ppermute x41, waiting for transfers between devices, flip(): lax.ppermute(block, ALL, [(i, i ^ mask) for i in range(device_count())])  70.4 us
    ppermute x41, starting transfers between devices, flip(): lax.ppermute(block, ALL, [(i, i ^ mask) for i in range(device_count())])  44.5 us
    pallas_call x1, Pallas kernels, mlp(): pl.pallas_call(partial(mlp_body, len(ups)), grid_spec=pltpu.PrefetchScala...  24.1 us
    pallas_call x1, Pallas kernels, attend_back(): pl.pallas_call(partial(attend_back_body, early), grid=(pairs,), out_shape...  21.1 us
    pallas_call x1, Pallas kernels, attend(): pl.pallas_call(attend_body, grid=(width // PAIR,), out_shape=[like((rows,...  12 us
    pallas_call x1, Pallas kernels, front(): pl.pallas_call(front_body, grid=(1,), out_shape=[pltpu.HBM((width, rows),...  6.48 us
    pallas_call x2, Pallas kernels, place_pair(): pl.pallas_call(body, out_shape=[pltpu.VMEM(shape, BF16) for shape in shap...  5.82 us
    ppermute x1, waiting for transfers between devices, local(): lax.ppermute(after(send, front_sum.send, back_sum.send), 'stream', [(1, 0)])  5.05 us
  transfers between devices with their start and end apart: 44, of which 21 were waited for; matrix products, arithmetic and copies ran while one was open for 3% of the time, Pallas kernels for 22%

profile of v4, /device:TPU:0, one launch (start us, length us, event | category | flops | bytes accessed | tf_op | source)
XLA Modules:
  0.0 230.9 jit_solution(9660452529200215406)
XLA Ops:
  1.9 5.1 %collective-permute-start.3 = (bf16[1,24,3200]{2,1,0:T(8,128)(2,1)S(1)}, bf16[1,24,3200]{2,1,0:T(8,128)(2,1)S(1)}, u32[]{:S(2)}, u32[]{:S(2)}) collective-permute-start(bf16[1,24,3200]{2,1,0:T(8,128)(2,1)S(1)} %bitcast.72), channel_id=1, source_target_pairs={{0,24},{1,25},{2,26},{3,27},{4,28},{5,29},{6,30},{7,31},{8,16},{9,... | collective-permute-start | bytes 460808 | tf_op jit(solution)/shard_map/ppermute | solution.py:43
  8.8 3.6 %collective-permute-start = (bf16[256,768]{1,0:T(8,128)(2,1)S(1)}, bf16[256,768]{1,0:T(8,128)(2,1)S(1)}, u32[]{:S(2)}, u32[]{:S(2)}) collective-permute-start(bf16[256,768]{1,0:T(8,128)(2,1)S(1)} %get-tuple-element.209), channel_id=1, source_target_pairs={{0,1},{2,3},{4,5},{6,7},{8,9},{10,11},{12,13},{14,15},{16,17},{18,... | collective-permute-start | bytes 1179656 | tf_op jit(solution)/shard_map/ppermute | solution.py:1118
  16.4 3.6 %collective-permute-done.far_tok = bf16[256,768]{1,0:T(8,128)(2,1)S(1)} collective-permute-done((bf16[256,768]{1,0:T(8,128)(2,1)S(1)}, bf16[256,768]{1,0:T(8,128)(2,1)S(1)}, u32[]{:S(2)}, u32[]{:S(2)}) %collective-permute-start) | collective-permute-done | bytes 393248 | tf_op jit(solution)/shard_map/ppermute | solution.py:1118
  20.0 3.5 %collective-permute-start.10 = (bf16[1,24,6144]{2,1,0:T(8,128)(2,1)S(1)}, bf16[1,24,6144]{2,1,0:T(8,128)(2,1)S(1)}, u32[]{:S(2)}, u32[]{:S(2)}) collective-permute-start(bf16[1,24,6144]{2,1,0:T(8,128)(2,1)S(1)} %bitcast.76), channel_id=1, source_target_pairs={{0,24},{1,25},{2,26},{3,27},{4,28},{5,29},{6,30},{7,31},{8,16},{9,... | collective-permute-start | bytes 884744 | tf_op jit(solution)/shard_map/ppermute | solution.py:43
  28.6 3.1 %collective-permute-done.4 = bf16[4,24,1536]{2,1,0:T(8,128)(2,1)S(1)} collective-permute-done((bf16[4,24,1536]{2,1,0:T(8,128)(2,1)S(1)}, bf16[4,24,1536]{2,1,0:T(8,128)(2,1)S(1)}, u32[]{:S(2)}, u32[]{:S(2)}) %collective-permute-start.4) | collective-permute-done | bytes 294944 | tf_op jit(solution)/shard_map/ppermute | solution.py:43
  33.3 3.5 %collective-permute-done.5 = bf16[4,24,1664]{2,1,0:T(8,128)(2,1)S(1)} collective-permute-done((bf16[4,24,1664]{2,1,0:T(8,128)(2,1)S(1)}, bf16[4,24,1664]{2,1,0:T(8,128)(2,1)S(1)}, u32[]{:S(2)}, u32[]{:S(2)}) %collective-permute-start.5) | collective-permute-done | bytes 319520 | tf_op jit(solution)/shard_map/ppermute | solution.py:43
  36.9 3.9 %collective-permute-start.6 = (bf16[256,768]{1,0:T(8,128)(2,1)S(1)}, bf16[256,768]{1,0:T(8,128)(2,1)S(1)}, u32[]{:S(2)}, u32[]{:S(2)}) collective-permute-start(bf16[256,768]{1,0:T(8,128)(2,1)S(1)} %get-tuple-element.110), channel_id=1, source_target_pairs={{0,1},{2,3},{4,5},{6,7},{8,9},{10,11},{12,13},{14,15},{16,17},{18,... | collective-permute-start | bytes 1179656 | tf_op jit(solution)/shard_map/ppermute | solution.py:1123
  40.9 6.3 %collective-permute-done.9.refs_2_ = bf16[1,24,6144]{2,1,0:T(8,128)(2,1)S(1)} collective-permute-done((bf16[1,24,6144]{2,1,0:T(8,128)(2,1)S(1)}, bf16[1,24,6144]{2,1,0:T(8,128)(2,1)S(1)}, u32[]{:S(2)}, u32[]{:S(2)}) %collective-permute-start.9) | collective-permute-done | bytes 294944 | tf_op jit(solution)/shard_map/ppermute | solution.py:43
  60.0 6.5 %shard_map.208 = (bf16[768,512]{1,0:T(8,128)(2,1)}, bf16[768,512]{1,0:T(8,128)(2,1)}, bf16[512,768]{1,0:T(8,128)(2,1)}, bf16[512,768]{1,0:T(8,128)(2,1)}, bf16[5...) custom-call(s32[1]{0:T(128)} %bitcast.4.noisy_ref, bf16[512,768]{1,0:T(8,128)(2,1)S(1)} %bitcast.60, ...), custom_call_target="tpu_custom_call" | custom-call | flops 1 | bytes 1 | tf_op jit(solution)/shard_map/pallas_call | solution.py:522
  73.7 12.0 %shard_map.209 = (bf16[512,768]{1,0:T(8,128)(2,1)S(1)}, f32[48,1024]{1,0:T(8,128)S(1)}) custom-call(s32[1]{0:T(128)} %bitcast.4.noisy_ref, s32[512,1]{1,0:T(8,128)} %copy-done.15, s32[512,1]{1,0:T(8,128)} %get-tuple-element.206.hi, s32[512,1]{1,0:T(8,128)} %get-tuple-element.207.code, s32[1,512]{1,0:T(1,128)} %get-tuple-element.205.code_row, ...), custom_call_target="tpu_custom_call" | custom-call | flops 1 | bytes 1 | tf_op jit(solution)/shard_map/pallas_call | solution.py:635
  86.3 9.0 %collective-permute-done.22.refs_4_ = bf16[8,24,3072]{2,1,0:T(8,128)(2,1)} collective-permute-done((bf16[8,24,3072]{2,1,0:T(8,128)(2,1)S(1)}, bf16[8,24,3072]{2,1,0:T(8,128)(2,1)}, u32[]{:S(2)}, u32[]{:S(2)}) %collective-permute-start.22) | collective-permute-done | bytes 1179680 | tf_op jit(solution)/shard_map/ppermute | solution.py:43
  95.9 3.3 %shard_map.210 = (bf16[32,24,3072]{2,1,0:T(8,128)(2,1)S(1)}, bf16[32,4,24,768]{3,2,1,0:T(8,128)(2,1)S(1)}) custom-call(s32[1]{0:T(128)} %bitcast.20.me_ref, bf16[8,24,3072]{2,1,0:T(8,128)(2,1)S(1)} %constant_dynamic-update-slice_fusion.4.refs_0_, bf16[8,24,3072]{2,1,0:T(8,128)(2,1)} %collective-permute-done.18.refs_1_, ...), custom_call_target="tpu_custom_call" | custom-call | flops 1 | bytes 1 | tf_op jit(solution)/shard_map/pallas_call | solution.py:106
  102.7 24.1 %shard_map.212 = (bf16[512,768]{1,0:T(8,128)(2,1)}, f32[512,768]{1,0:T(8,128)S(1)}, bf16[512,768]{1,0:T(8,128)(2,1)S(1)}, bf16[2,4,48,3072]{3,2,1,0:T(8,128)(2,1...) custom-call(s32[3]{0:T(128)S(1)} %pad_add_fusion.refs_0_.place_ref, ...), custom_call_target="tpu_custom_call" | custom-call | flops 1 | bytes 1 | tf_op jit(solution)/shard_map/pallas_call | solution.py:917
  128.2 4.0 %collective-permute-done.24 = bf16[2,4,48,3072]{3,2,1,0:T(8,128)(2,1)S(1)} collective-permute-done((bf16[2,4,48,3072]{3,2,1,0:T(8,128)(2,1)S(1)}, bf16[2,4,48,3072]{3,2,1,0:T(8,128)(2,1)S(1)}, u32[]{:S(2)}, u32[]{:S(2)}) %collective-permute-start.24) | collective-permute-done | bytes 2359328 | tf_op jit(solution)/shard_map/ppermute | solution.py:43
  132.2 3.4 %collective-permute-done.25 = bf16[2,4,192,768]{3,2,1,0:T(8,128)(2,1)S(1)} collective-permute-done((bf16[2,4,192,768]{3,2,1,0:T(8,128)(2,1)S(1)}, bf16[2,4,192,768]{3,2,1,0:T(8,128)(2,1)S(1)}, u32[]{:S(2)}, u32[]{:S(2)}) %collective-permute-start.25) | collective-permute-done | bytes 2359328 | tf_op jit(solution)/shard_map/ppermute | solution.py:43
  139.0 21.1 %shard_map.214 = (f32[512,768]{1,0:T(8,128)S(1)}, f32[512,768]{1,0:T(8,128)S(1)}, bf16[2,4,48,1536]{3,2,1,0:T(8,128)(2,1)S(1)}, bf16[2,4,48,1536]{3,2,1,0:T(8,12...) custom-call(s32[1]{0:T(128)} %bitcast.4.noisy_ref, ...), custom_call_target="tpu_custom_call" | custom-call | flops 1 | bytes 1 | tf_op jit(solution)/shard_map/pallas_call | solution.py:765
  160.0 5.5 %collective-permute-done.27.refs_3_ = bf16[2,4,1,96,768]{4,3,2,1,0:T(8,128)(2,1)S(1)} collective-permute-done((bf16[2,4,1,96,768]{4,3,2,1,0:T(8,128)(2,1)S(1)}, bf16[2,4,1,96,768]{4,3,2,1,0:T(8,128)(2,1)S(1)}, u32[]{:S(2)}, u32[]{:S(2)}) %collective-permute-start.27) | collective-permute-done | bytes 1179680 | tf_op jit(solution)/shard_map/ppermute | solution.py:43
  169.8 3.1 %shard_map.216 = (f32[512,768]{1,0:T(8,128)S(1)}, bf16[512,768]{1,0:T(8,128)(2,1)S(1)}, bf16[2,4,48,896]{3,2,1,0:T(8,128)(2,1)S(1)}, bf16[2,4,48,896]{3,2,1,0:T(8,128)(2,1)S(1)}) custom-call(s32[1]{0:T(128)} %bitcast.4.noisy_ref, s32[3]{0:T(128)S(1)} %pad_add_fusion.refs_0_.place_ref, bf16[512,768]{1,0:T(8,128)(2,1)S(1)} %bitcast.61, ...), custom_call_target="tpu_custom_call" | custom-call | flops 1 | bytes 1 | tf_op jit(solution)/shard_map/pallas_call | solution.py:992
  173.0 9.4 %collective-permute-done.31.refs_3_ = bf16[1,4,1,96,768]{4,3,2,1,0:T(8,128)(2,1)S(1)} collective-permute-done((bf16[1,4,1,96,768]{4,3,2,1,0:T(8,128)(2,1)S(1)}, bf16[1,4,1,96,768]{4,3,2,1,0:T(8,128)(2,1)S(1)}, u32[]{:S(2)}, u32[]{:S(2)}) %collective-permute-start.31) | collective-permute-done | bytes 589856 | tf_op jit(solution)/shard_map/ppermute | solution.py:43
  191.6 7.9 %collective-permute-done.33.refs_1_ = bf16[2,4,1,24,1536]{4,3,2,1,0:T(8,128)(2,1)S(1)} collective-permute-done((bf16[2,4,1,24,1536]{4,3,2,1,0:T(8,128)(2,1)S(1)}, bf16[2,4,1,24,1536]{4,3,2,1,0:T(8,128)(2,1)S(1)}, u32[]{:S(2)}, u32[]{:S(2)}) %collective-permute-start.33) | collective-permute-done | bytes 589856 | tf_op jit(solution)/shard_map/ppermute | solution.py:43
  204.2 7.8 %collective-permute-done.39.refs_1_ = bf16[1,24,6144]{2,1,0:T(8,128)(2,1)S(1)} collective-permute-done((bf16[1,24,6144]{2,1,0:T(8,128)(2,1)S(1)}, bf16[1,24,6144]{2,1,0:T(8,128)(2,1)S(1)}, u32[]{:S(2)}, u32[]{:S(2)}) %collective-permute-start.39) | collective-permute-done | bytes 294944 | tf_op jit(solution)/shard_map/ppermute | solution.py:43
  213.0 4.0 %collective-permute-start.41 = (bf16[1,24,3200]{2,1,0:T(8,128)(2,1)S(1)}, bf16[1,24,3200]{2,1,0:T(8,128)(2,1)S(1)}, u32[]{:S(2)}, u32[]{:S(2)}) collective-permute-start(bf16[1,24,3200]{2,1,0:T(8,128)(2,1)S(1)} %get-tuple-element.195), channel_id=1, source_target_pairs={{0,8},{1,9},{2,10},{3,11},{4,12},{5,13},{6,14},{7,15},{8,0},{9,1},... | collective-permute-start | bytes 460808 | tf_op jit(solution)/shard_map/ppermute | solution.py:43
  219.5 5.0 %collective-permute-done.35.got = bf16[512,768]{1,0:T(8,128)(2,1)S(1)} collective-permute-done((bf16[512,768]{1,0:T(8,128)(2,1)S(1)}, bf16[512,768]{1,0:T(8,128)(2,1)S(1)}, u32[]{:S(2)}, u32[]{:S(2)}) %collective-permute-start.35) | collective-permute-done | bytes 786464 | tf_op jit(solution)/shard_map/ppermute | solution.py:1206
  226.2 2.7 %collective-permute-done.42.refs_1_ = bf16[1,24,3200]{2,1,0:T(8,128)(2,1)S(1)} collective-permute-done((bf16[1,24,3200]{2,1,0:T(8,128)(2,1)S(1)}, bf16[1,24,3200]{2,1,0:T(8,128)(2,1)S(1)}, u32[]{:S(2)}, u32[]{:S(2)}) %collective-permute-start.42) | collective-permute-done | bytes 153632 | tf_op jit(solution)/shard_map/ppermute | solution.py:43
  (150 shorter events, 65.7 us)
Async XLA Ops:
  1.9 14.6 %collective-permute-start.3 = (bf16[1,24,3200]{2,1,0:T(8,128)(2,1)S(1)}, bf16[1,24,3200]{2,1,0:T(8,128)(2,1)S(1)}, u32[]{:S(2)}, u32[]{:S(2)}) collective-permute-start(bf16[1,24,3200]{2,1,0:T(8,128)(2,1)S(1)} %bitcast.72), channel_id=1, source_target_pairs={{0,24},{1,25},{2,26},{3,27},{4,28},{5,29},{6,30},{7,31},{8,16},{9,... | collective-permute-start | bytes 460808 | tf_op jit(solution)/shard_map/ppermute | solution.py:43
  20.0 16.9 %collective-permute-start.10 = (bf16[1,24,6144]{2,1,0:T(8,128)(2,1)S(1)}, bf16[1,24,6144]{2,1,0:T(8,128)(2,1)S(1)}, u32[]{:S(2)}, u32[]{:S(2)}) collective-permute-start(bf16[1,24,6144]{2,1,0:T(8,128)(2,1)S(1)} %bitcast.76), channel_id=1, source_target_pairs={{0,24},{1,25},{2,26},{3,27},{4,28},{5,29},{6,30},{7,31},{8,16},{9,... | collective-permute-start | bytes 884744 | tf_op jit(solution)/shard_map/ppermute | solution.py:43
  23.6 17.3 %collective-permute-start.8 = (bf16[1,24,6144]{2,1,0:T(8,128)(2,1)S(1)}, bf16[1,24,6144]{2,1,0:T(8,128)(2,1)S(1)}, u32[]{:S(2)}, u32[]{:S(2)}) collective-permute-start(bf16[1,24,6144]{2,1,0:T(8,128)(2,1)S(1)} %bitcast.77), channel_id=1, source_target_pairs={{0,8},{1,9},{2,10},{3,11},{4,12},{5,13},{6,14},{7,15},{8,0},{9,1},... | collective-permute-start | bytes 884744 | tf_op jit(solution)/shard_map/ppermute | solution.py:43
  23.6 23.6 %collective-permute-start.9 = (bf16[1,24,6144]{2,1,0:T(8,128)(2,1)S(1)}, bf16[1,24,6144]{2,1,0:T(8,128)(2,1)S(1)}, u32[]{:S(2)}, u32[]{:S(2)}) collective-permute-start(bf16[1,24,6144]{2,1,0:T(8,128)(2,1)S(1)} %bitcast.78), channel_id=1, source_target_pairs={{0,16},{1,17},{2,18},{3,19},{4,20},{5,21},{6,22},{7,23},{8,24},{9,... | collective-permute-start | bytes 884744 | tf_op jit(solution)/shard_map/ppermute | solution.py:43
  31.7 20.1 %collective-permute-start.7 = (bf16[8,24,1536]{2,1,0:T(8,128)(2,1)S(1)}, bf16[8,24,1536]{2,1,0:T(8,128)(2,1)S(1)}, u32[]{:S(2)}, u32[]{:S(2)}) collective-permute-start(bf16[8,24,1536]{2,1,0:T(8,128)(2,1)S(1)} %constant_dynamic-update-slice_fusion.refs_0_), channel_id=1, source_target_pairs={{0,4},{1,5},{2,6},{3,7},{4,0},{5,1},{6,2},{7,3},{8,12},{9,13},{10,... | collective-permute-start | bytes 1769480 | tf_op jit(solution)/shard_map/ppermute | solution.py:43
  36.9 17.0 %collective-permute-start.6 = (bf16[256,768]{1,0:T(8,128)(2,1)S(1)}, bf16[256,768]{1,0:T(8,128)(2,1)S(1)}, u32[]{:S(2)}, u32[]{:S(2)}) collective-permute-start(bf16[256,768]{1,0:T(8,128)(2,1)S(1)} %get-tuple-element.110), channel_id=1, source_target_pairs={{0,1},{2,3},{4,5},{6,7},{8,9},{10,11},{12,13},{14,15},{16,17},{18,... | collective-permute-start | bytes 1179656 | tf_op jit(solution)/shard_map/ppermute | solution.py:1123
  53.9 14.4 %collective-permute-start.17 = (bf16[4,24,3072]{2,1,0:T(8,128)(2,1)S(1)}, bf16[4,24,3072]{2,1,0:T(8,128)(2,1)S(1)}, u32[]{:S(2)}, u32[]{:S(2)}) collective-permute-start(bf16[4,24,3072]{2,1,0:T(8,128)(2,1)S(1)} %get-tuple-element.123), channel_id=1, source_target_pairs={{0,1},{1,0},{2,3},{3,2},{4,5},{5,4},{6,7},{7,6},{8,9},{9,8},{10,11... | collective-permute-start | bytes 1769480 | tf_op jit(solution)/shard_map/ppermute | solution.py:43
  56.4 14.5 %collective-permute-start.16 = (bf16[4,24,3072]{2,1,0:T(8,128)(2,1)S(1)}, bf16[4,24,3072]{2,1,0:T(8,128)(2,1)S(1)}, u32[]{:S(2)}, u32[]{:S(2)}) collective-permute-start(bf16[4,24,3072]{2,1,0:T(8,128)(2,1)S(1)} %get-tuple-element.121), channel_id=1, source_target_pairs={{0,4},{1,5},{2,6},{3,7},{4,0},{5,1},{6,2},{7,3},{8,12},{9,13},{10,... | collective-permute-start | bytes 1769480 | tf_op jit(solution)/shard_map/ppermute | solution.py:43
  68.4 26.9 %collective-permute-start.22 = (bf16[8,24,3072]{2,1,0:T(8,128)(2,1)S(1)}, bf16[8,24,3072]{2,1,0:T(8,128)(2,1)}, u32[]{:S(2)}, u32[]{:S(2)}) collective-permute-start(bf16[8,24,3072]{2,1,0:T(8,128)(2,1)S(1)} %constant_dynamic-update-slice_fusion.6.refs_2_), channel_id=1, source_target_pairs={{0,4},{1,5},{2,6},{3,7},{4,0},{5,1},{6,2},{7,3},{8,12},{9,13},{10,... | collective-permute-start | bytes 3538952 | tf_op jit(solution)/shard_map/ppermute | solution.py:43
  71.0 24.3 %collective-permute-start.20 = (bf16[8,24,3072]{2,1,0:T(8,128)(2,1)S(1)}, bf16[8,24,3072]{2,1,0:T(8,128)(2,1)}, u32[]{:S(2)}, u32[]{:S(2)}) collective-permute-start(bf16[8,24,3072]{2,1,0:T(8,128)(2,1)S(1)} %constant_dynamic-update-slice_fusion.4.refs_0_), channel_id=1, source_target_pairs={{0,1},{1,0},{2,3},{3,2},{4,5},{5,4},{6,7},{7,6},{8,9},{9,8},{10,11... | collective-permute-start | bytes 3538952 | tf_op jit(solution)/shard_map/ppermute | solution.py:43
  73.2 22.7 %collective-permute-start.19 = (bf16[8,24,3072]{2,1,0:T(8,128)(2,1)S(1)}, bf16[8,24,3072]{2,1,0:T(8,128)(2,1)}, u32[]{:S(2)}, u32[]{:S(2)}) collective-permute-start(bf16[8,24,3072]{2,1,0:T(8,128)(2,1)S(1)} %constant_dynamic-update-slice_fusion.6.refs_2_), channel_id=1, source_target_pairs={{0,2},{1,3},{2,0},{3,1},{4,6},{5,7},{6,4},{7,5},{8,10},{9,11},{10,... | collective-permute-start | bytes 3538952 | tf_op jit(solution)/shard_map/ppermute | solution.py:43
  73.2 22.7 %collective-permute-start.18 = (bf16[8,24,3072]{2,1,0:T(8,128)(2,1)S(1)}, bf16[8,24,3072]{2,1,0:T(8,128)(2,1)}, u32[]{:S(2)}, u32[]{:S(2)}) collective-permute-start(bf16[8,24,3072]{2,1,0:T(8,128)(2,1)S(1)} %constant_dynamic-update-slice_fusion.4.refs_0_), channel_id=1, source_target_pairs={{0,2},{1,3},{2,0},{3,1},{4,6},{5,7},{6,4},{7,5},{8,10},{9,11},{10,... | collective-permute-start | bytes 3538952 | tf_op jit(solution)/shard_map/ppermute | solution.py:43
  137.5 28.1 %collective-permute-start.27 = (bf16[2,4,1,96,768]{4,3,2,1,0:T(8,128)(2,1)S(1)}, bf16[2,4,1,96,768]{4,3,2,1,0:T(8,128)(2,1)S(1)}, u32[]{:S(2)}, u32[]{:S(2)}) collective-permute-start(bf16[2,4,1,96,768]{4,3,2,1,0:T(8,128)(2,1)S(1)} %get-tuple-element.145), channel_id=1, source_target_pairs={{0,1},{1,0},{2,3},{3,2},{4,5},{5,4},{6,7},{7,6},{8,9},{9,8},{10,11... | collective-permute-start | bytes 3538952 | tf_op jit(solution)/shard_map/ppermute | solution.py:43
  138.0 27.7 %collective-permute-start.26 = (bf16[1,4,2,24,3072]{4,3,2,1,0:T(8,128)(2,1)S(1)}, bf16[1,4,2,24,3072]{4,3,2,1,0:T(8,128)(2,1)S(1)}, u32[]{:S(2)}, u32[]{:S(2)}) collective-permute-start(bf16[1,4,2,24,3072]{4,3,2,1,0:T(8,128)(2,1)S(1)} %get-tuple-element.144), channel_id=1, source_target_pairs={{0,4},{1,5},{2,6},{3,7},{4,0},{5,1},{6,2},{7,3},{8,12},{9,13},{10,... | collective-permute-start | bytes 3538952 | tf_op jit(solution)/shard_map/ppermute | solution.py:43
  166.5 15.9 %collective-permute-start.28 = (bf16[2,4,48,1536]{3,2,1,0:T(8,128)(2,1)S(1)}, bf16[2,4,48,1536]{3,2,1,0:T(8,128)(2,1)S(1)}, u32[]{:S(2)}, u32[]{:S(2)}) collective-permute-start(bf16[2,4,48,1536]{3,2,1,0:T(8,128)(2,1)S(1)} %get-tuple-element.166), channel_id=1, source_target_pairs={{0,2},{1,3},{2,0},{3,1},{4,6},{5,7},{6,4},{7,5},{8,10},{9,11},{10,... | collective-permute-start | bytes 3538952 | tf_op jit(solution)/shard_map/ppermute | solution.py:43
  167.1 15.3 %collective-permute-start.31 = (bf16[1,4,1,96,768]{4,3,2,1,0:T(8,128)(2,1)S(1)}, bf16[1,4,1,96,768]{4,3,2,1,0:T(8,128)(2,1)S(1)}, u32[]{:S(2)}, u32[]{:S(2)}) collective-permute-start(bf16[1,4,1,96,768]{4,3,2,1,0:T(8,128)(2,1)S(1)} %get-tuple-element.159), channel_id=1, source_target_pairs={{0,4},{1,5},{2,6},{3,7},{4,0},{5,1},{6,2},{7,3},{8,12},{9,13},{10,... | collective-permute-start | bytes 1769480 | tf_op jit(solution)/shard_map/ppermute | solution.py:43
  168.1 15.0 %collective-permute-start.30 = (bf16[1,4,1,24,3072]{4,3,2,1,0:T(8,128)(2,1)S(1)}, bf16[1,4,1,24,3072]{4,3,2,1,0:T(8,128)(2,1)S(1)}, u32[]{:S(2)}, u32[]{:S(2)}) collective-permute-start(bf16[1,4,1,24,3072]{4,3,2,1,0:T(8,128)(2,1)S(1)} %get-tuple-element.158), channel_id=1, source_target_pairs={{0,1},{1,0},{2,3},{3,2},{4,5},{5,4},{6,7},{7,6},{8,9},{9,8},{10,11... | collective-permute-start | bytes 1769480 | tf_op jit(solution)/shard_map/ppermute | solution.py:43
  184.5 15.3 %collective-permute-start.34 = (bf16[1,4,2,24,1664]{4,3,2,1,0:T(8,128)(2,1)S(1)}, bf16[1,4,2,24,1664]{4,3,2,1,0:T(8,128)(2,1)S(1)}, u32[]{:S(2)}, u32[]{:S(2)}) collective-permute-start(bf16[1,4,2,24,1664]{4,3,2,1,0:T(8,128)(2,1)S(1)} %get-tuple-element.184), channel_id=1, source_target_pairs={{0,4},{1,5},{2,6},{3,7},{4,0},{5,1},{6,2},{7,3},{8,12},{9,13},{10,... | collective-permute-start | bytes 1916936 | tf_op jit(solution)/shard_map/ppermute | solution.py:43
  185.6 13.9 %collective-permute-start.33 = (bf16[2,4,1,24,1536]{4,3,2,1,0:T(8,128)(2,1)S(1)}, bf16[2,4,1,24,1536]{4,3,2,1,0:T(8,128)(2,1)S(1)}, u32[]{:S(2)}, u32[]{:S(2)}) collective-permute-start(bf16[2,4,1,24,1536]{4,3,2,1,0:T(8,128)(2,1)S(1)} %get-tuple-element.182), channel_id=1, source_target_pairs={{0,1},{1,0},{2,3},{3,2},{4,5},{5,4},{6,7},{7,6},{8,9},{9,8},{10,11... | collective-permute-start | bytes 1769480 | tf_op jit(solution)/shard_map/ppermute | solution.py:43
  187.2 15.7 %collective-permute-start.38 = (bf16[1,24,6144]{2,1,0:T(8,128)(2,1)S(1)}, bf16[1,24,6144]{2,1,0:T(8,128)(2,1)S(1)}, u32[]{:S(2)}, u32[]{:S(2)}) collective-permute-start(bf16[1,24,6144]{2,1,0:T(8,128)(2,1)S(1)} %get-tuple-element.175), channel_id=1, source_target_pairs={{0,8},{1,9},{2,10},{3,11},{4,12},{5,13},{6,14},{7,15},{8,0},{9,1},... | collective-permute-start | bytes 884744 | tf_op jit(solution)/shard_map/ppermute | solution.py:43
  188.5 23.5 %collective-permute-start.39 = (bf16[1,24,6144]{2,1,0:T(8,128)(2,1)S(1)}, bf16[1,24,6144]{2,1,0:T(8,128)(2,1)S(1)}, u32[]{:S(2)}, u32[]{:S(2)}) collective-permute-start(bf16[1,24,6144]{2,1,0:T(8,128)(2,1)S(1)} %get-tuple-element.176), channel_id=1, source_target_pairs={{0,16},{1,17},{2,18},{3,19},{4,20},{5,21},{6,22},{7,23},{8,24},{9,... | collective-permute-start | bytes 884744 | tf_op jit(solution)/shard_map/ppermute | solution.py:43
  191.1 20.8 %collective-permute-start.40 = (bf16[1,24,6144]{2,1,0:T(8,128)(2,1)S(1)}, bf16[1,24,6144]{2,1,0:T(8,128)(2,1)S(1)}, u32[]{:S(2)}, u32[]{:S(2)}) collective-permute-start(bf16[1,24,6144]{2,1,0:T(8,128)(2,1)S(1)} %get-tuple-element.177), channel_id=1, source_target_pairs={{0,24},{1,25},{2,26},{3,27},{4,28},{5,29},{6,30},{7,31},{8,16},{9,... | collective-permute-start | bytes 884744 | tf_op jit(solution)/shard_map/ppermute | solution.py:43
  202.9 21.6 %collective-permute-start.35 = (bf16[512,768]{1,0:T(8,128)(2,1)S(1)}, bf16[512,768]{1,0:T(8,128)(2,1)S(1)}, u32[]{:S(2)}, u32[]{:S(2)}) collective-permute-start(bf16[512,768]{1,0:T(8,128)(2,1)S(1)} %get-tuple-element.187), channel_id=1, source_target_pairs={{1,0},{3,2},{5,4},{7,6},{9,8},{11,10},{13,12},{15,14},{17,16},{19,... | collective-permute-start | bytes 2359304 | tf_op jit(solution)/shard_map/ppermute | solution.py:1206
  213.0 13.2 %collective-permute-start.41 = (bf16[1,24,3200]{2,1,0:T(8,128)(2,1)S(1)}, bf16[1,24,3200]{2,1,0:T(8,128)(2,1)S(1)}, u32[]{:S(2)}, u32[]{:S(2)}) collective-permute-start(bf16[1,24,3200]{2,1,0:T(8,128)(2,1)S(1)} %get-tuple-element.195), channel_id=1, source_target_pairs={{0,8},{1,9},{2,10},{3,11},{4,12},{5,13},{6,14},{7,15},{8,0},{9,1},... | collective-permute-start | bytes 460808 | tf_op jit(solution)/shard_map/ppermute | solution.py:43
  (40 other events, 350.6 us)
